TPU v7x, 32 devices: a whole 2x2x4 slice. The times are simulated.
32 devices in a mesh: row: 4 (over y, core), col: 8 (over z, x).
Axes of the slice: x: 2, y: 2, z: 4, core: 2. Of those that a mesh axis runs over, the one named last changes fastest.
Arguments:
- output_grad: bfloat16 [1024, 8192], P('col', 'row'), may hold values from -16 to 16
- gate_preact: bfloat16 [1024, 28672], P('row', 'col'), may hold values from -6 to 6
- up_preact: bfloat16 [1024, 28672], P('row', 'col'), may hold values from -6 to 6
- gate_weight: bfloat16 [8192, 28672], P('row', 'col'), may hold values from -0.0625 to 0.0625
- up_weight: bfloat16 [8192, 28672], P('row', 'col'), may hold values from -0.0625 to 0.0625
- down_weight: bfloat16 [28672, 8192], P('col', 'row'), may hold values from -0.03125 to 0.03125
Outputs:
- input_grad: bfloat16 [1024, 8192], P('col', 'row')
- gate_factor: float32 [3584, 28672], P('row', 'col')
All inputs are finite; a program needn't handle non-finite values.
Results may differ from a plain program's by a relative error of at most 0.0049.
Values may be sent and summed in bfloat16 or wider, within the bound.
A program may use at most 192 MiB of HBM per device.

v0:
```python
import jax
import jax.numpy as jnp
from jax import lax
from jax.sharding import PartitionSpec as P

TOKENS = 1024
SLAB_DEV = 896


def from_root(block, axis, holder):
    block = jnp.where(lax.axis_index(axis) == holder, block, jnp.zeros_like(block))
    return lax.psum(block, axis)


def swiglu_grads(hidden_grad, gate_preact, up_preact):
    gate_float = gate_preact.astype(jnp.float32)
    up_float = up_preact.astype(jnp.float32)
    logistic = jax.nn.sigmoid(gate_float)
    derivative = logistic * (1.0 + gate_float * (1.0 - logistic))
    grad_gate = (hidden_grad * up_float * derivative).astype(jnp.bfloat16)
    grad_up = (hidden_grad * gate_float * logistic).astype(jnp.bfloat16)
    return (grad_gate, grad_up)


def contract_last(left, right):
    return lax.dot_general(
        left, right, (((1,), (1,)), ((), ())), preferred_element_type=jnp.float32
    )


def shards(output_grad, gate_preact, up_preact, gate_weight, up_weight, down_weight):
    cotangent_all = lax.all_gather(output_grad, "col", axis=0, tiled=True)
    hidden_part = contract_last(cotangent_all, down_weight)
    hidden_grad = lax.psum(hidden_part, "row")
    gate_all, up_all = (
        lax.all_gather(gate_preact, "row", axis=0, tiled=True),
        lax.all_gather(up_preact, "row", axis=0, tiled=True),
    )
    grad_gate, grad_up = swiglu_grads(hidden_grad, gate_all, up_all)
    units_dev = grad_gate.shape[1]
    first_unit = lax.axis_index("row") * SLAB_DEV
    owner_column = first_unit // units_dev
    offset = first_unit % units_dev
    own_slab = lax.dynamic_slice_in_dim(grad_gate, offset, SLAB_DEV, 1)
    slab_grads = from_root(own_slab, "col", owner_column)
    gate_factor = (
        lax.dot_general(
            slab_grads, grad_gate, (((0,), (0,)), ((), ())), preferred_element_type=jnp.float32
        )
        / TOKENS
    )
    input_float = lax.psum_scatter(
        contract_last(grad_gate, gate_weight) + contract_last(grad_up, up_weight),
        "col",
        scatter_dimension=0,
        tiled=True,
    )
    return (input_float.astype(jnp.bfloat16), gate_factor)


def solution(mesh):
    return jax.shard_map(
        shards,
        mesh=mesh,
        in_specs=(
            P("col", "row"),
            P("row", "col"),
            P("row", "col"),
            P("row", "col"),
            P("row", "col"),
            P("col", "row"),
        ),
        out_specs=(P("col", "row"), P("row", "col")),
        check_vma=False,
    )
```

profile of v0, /device:TPU:0, one launch (start us, length us, event | category | flops | bytes accessed | tf_op | source)
XLA Modules:
  0.0 742.4 jit_solution(10430943090364665841)
XLA Ops:
  7.2 0.0 all-gather.4.cloned.1.call-start
  7.2 0.7 all-gather.4.cloned.1.call-update
  7.9 0.0 all-gather.8.cloned.1.call-start
  7.9 0.7 all-gather.8.cloned.1.call-update
  8.6 0.0 all-gather.6.cloned.1.call-start
  8.7 0.7 all-gather.6.cloned.1.call-update
  9.4 0.0 all-reduce.3.cloned.1.call-start
  9.4 76.8 %all-gather.4.cloned.1.call-done = bf16[1024,2048]{1,0:T(8,128)(2,1)} async-done(((bf16[128,2048]{1,0:T(8,128)(2,1)}), bf16[1024,2048]{1,0:T(8,128)(2,1)}) %all-gather.4.cloned.1.call-update) | async-done | bytes 4194320 | tf_op jit(solution)/shard_map/all_gather | solution.py:32
  86.3 22.8 %fusion.15 = f32[1024,3584]{1,0:T(8,128)} fusion(bf16[1024,2048]{1,0:T(8,128)(2,1)} %all-gather.4.cloned.1.call-done, bf16[3584,2048]{1,0:T(8,128)(2,1)} %param.11), kind=kOutput, calls=%fused_computation.17 | convolution fusion | flops 15032385536 | bytes 33554432 | tf_op jit(solution)/shard_map/dot_general | solution.py:26
  109.1 0.0 all-reduce.3.cloned.1.call-update
  109.1 0.0 all-reduce.5.cloned.1.call-start
  109.2 29.3 %all-gather.8.cloned.1.call-done = bf16[1024,3584]{1,0:T(8,128)(2,1)} async-done(((bf16[256,3584]{1,0:T(8,128)(2,1)}), bf16[1024,3584]{1,0:T(8,128)(2,1)}) %all-gather.8.cloned.1.call-update) | async-done | bytes 7340048 | tf_op jit(solution)/shard_map/all_gather | solution.py:36
  138.4 53.9 %all-gather.6.cloned.1.call-done = bf16[1024,3584]{1,0:T(8,128)(2,1)} async-done(((bf16[256,3584]{1,0:T(8,128)(2,1)}), bf16[1024,3584]{1,0:T(8,128)(2,1)}) %all-gather.6.cloned.1.call-update) | async-done | bytes 7340048 | tf_op jit(solution)/shard_map/all_gather | solution.py:37
  192.4 256.9 %all-reduce.3.cloned.1.call-done = f32[1024,3584]{1,0:T(8,128)} async-done(((f32[1024,3584]{1,0:T(8,128)}), f32[1024,3584]{1,0:T(8,128)}) %all-reduce.3.cloned.1.call-update) | async-done | bytes 14680080 | tf_op jit(solution)/shard_map/psum | solution.py:34
  449.3 11.6 %fusion.6 = bf16[1024,3584]{1,0:T(8,128)(2,1)S(1)} fusion(bf16[1024,3584]{1,0:T(8,128)(2,1)} %all-gather.8.cloned.1.call-done, f32[1024,3584]{1,0:T(8,128)} %all-reduce.3.cloned.1.call-done, bf16[1024,3584]{1,0:T(8,128)(2,1)} %all-gather.6.cloned.1.call-done), kind=kLoop, calls=%fused_computation.9 | loop fusion | flops 44040192 | bytes 36700160 | tf_op jit(solution)/shard_map/convert_element_type | solution.py:20
  460.9 0.0 copy-start
  461.0 22.0 %fusion.16 = f32[1024,2048]{1,0:T(8,128)} fusion(bf16[1024,3584]{1,0:T(8,128)(2,1)S(1)} %fusion.6, bf16[2048,3584]{1,0:T(8,128)(2,1)} %param.9), kind=kOutput, calls=%fused_computation.18 | convolution fusion | flops 15032385536 | bytes 30408704 | tf_op jit(solution)/shard_map/dot_general | solution.py:26
  482.9 0.0 copy-done
  482.9 2.3 dynamic-slice_select_fusion
  485.2 0.0 all-reduce.5.cloned.1.call-update
  485.3 0.2 reduce-scatter.2.cloned.1.call-start
  485.5 31.6 %fusion.11 = f32[1024,2048]{1,0:T(8,128)} fusion(f32[1024,2048]{1,0:T(8,128)} %fusion.16, bf16[2048,3584]{1,0:T(8,128)(2,1)} %param.10, f32[1024,3584]{1,0:T(8,128)} %all-reduce.3.cloned.1.call-done, bf16[1024,3584]{1,0:T(8,128)(2,1)} %all-gather.8.cloned.1.call-done), kind=kOutput, calls=%fused_computation.14 | convolution fusion | flops 15060172800 | bytes 53477376 | tf_op jit(solution)/shard_map/dot_general | solution.py:26
  517.1 0.0 reduce-scatter.2.cloned.1.call-update
  517.1 64.3 %all-reduce.5.cloned.1.call-done = bf16[1024,896]{1,0:T(8,128)(2,1)} async-done(((bf16[1024,896]{1,0:T(8,128)(2,1)}), bf16[1024,896]{1,0:T(8,128)(2,1)}) %all-reduce.5.cloned.1.call-update) | async-done | bytes 1835024 | tf_op jit(solution)/shard_map/psum | solution.py:12
  581.4 12.5 %convolution_multiply_fusion = f32[896,3584]{1,0:T(8,128)} fusion(bf16[1024,896]{1,0:T(8,128)(2,1)} %all-reduce.5.cloned.1.call-done, bf16[1024,3584]{1,0:T(8,128)(2,1)} %copy-done), kind=kOutput, calls=%fused_computation.12 | convolution fusion | flops 6579879936 | bytes 22020096 | tf_op jit(solution)/shard_map/dot_general | solution.py:47
  593.8 139.7 %reduce-scatter.2.cloned.1.call-done = f32[128,2048]{1,0:T(8,128)} async-done(((f32[1024,2048]{1,0:T(8,128)}), f32[128,2048]{1,0:T(8,128)}) %reduce-scatter.2.cloned.1.call-update) | async-done | bytes 1048592 | tf_op jit(solution)/shard_map/reduce_scatter | solution.py:52
  733.5 2.1 convert_element_type.19
Async XLA Ops:
  7.2 79.1 %all-gather.4.cloned.1.call-start = ((), (), s32[]{:S(2)}) async-start(), calls=%async_computation.1 | async-start | bytes 4718592 | tf_op jit(solution)/shard_map/all_gather | solution.py:32
  7.9 130.6 %all-gather.8.cloned.1.call-start = ((), (), s32[]{:S(2)}) async-start(), calls=%async_computation.4 | async-start | bytes 9175040 | tf_op jit(solution)/shard_map/all_gather | solution.py:36
  8.6 183.7 %all-gather.6.cloned.1.call-start = ((), (), s32[]{:S(2)}) async-start(), calls=%async_computation.3 | async-start | bytes 9175040 | tf_op jit(solution)/shard_map/all_gather | solution.py:37
  9.4 439.9 %all-reduce.3.cloned.1.call-start = ((), (), s32[]{:S(2)}) async-start(), calls=%async_computation.2 | async-start | bytes 29360128 | tf_op jit(solution)/shard_map/psum | solution.py:34
  109.1 472.3 %all-reduce.5.cloned.1.call-start = ((), (), s32[]{:S(2)}) async-start(), calls=%async_computation.6 | async-start | bytes 3670016 | tf_op jit(solution)/shard_map/psum | solution.py:12
  460.9 22.0 %copy-start = (bf16[1024,3584]{1,0:T(8,128)(2,1)}, bf16[1024,3584]{1,0:T(8,128)(2,1)S(1)}, u32[]{:S(2)}) copy-start(bf16[1024,3584]{1,0:T(8,128)(2,1)S(1)} %fusion.6) | copy-start | bytes 22020100
  485.3 248.2 %reduce-scatter.2.cloned.1.call-start = ((), (), s32[]{:S(2)}) async-start(), calls=%async_computation.5 | async-start | bytes 9437184 | tf_op jit(solution)/shard_map/reduce_scatter | solution.py:52
Sparse Core Ops, SparseCore 0:
  10.1 76.0 all-gather.3
  87.8 50.5 all-gather.7
  140.0 52.3 all-gather.5
  194.7 254.5 all-reduce.2
  485.4 95.9 all-reduce.4
  584.9 148.6 reduce-scatter.1
where the time goes:
time: 743 us; the launch traced here: 742 us
  waiting for transfers between devices  623 us (84%)
  matrix products  88.8 us (12%)
  other arithmetic  16 us (2%)
  between operations  14.2 us (2%)
    psum x1, waiting for transfers between devices, shards(): hidden_grad = lax.psum(hidden_part, 'row')  257 us
    reduce_scatter x1, waiting for transfers between devices, shards(): lax.psum_scatter(contract_last(grad_gate, gate_weight) + contract_last(gr...  140 us
    all_gather x1, waiting for transfers between devices, shards(): cotangent_all = lax.all_gather(output_grad, 'col', axis=0, tiled=True)  76.8 us
    dot_general x3, matrix products, contract_last(): lax.dot_general(left, right, (((1,), (1,)), ((), ())), preferred_element_...  76.3 us
    psum x1, waiting for transfers between devices, from_root(): return lax.psum(block, axis)  64.3 us
    all_gather x1, waiting for transfers between devices, shards(): lax.all_gather(up_preact, 'row', axis=0, tiled=True)  53.9 us
    all_gather x1, waiting for transfers between devices, shards(): lax.all_gather(gate_preact, 'row', axis=0, tiled=True)  29.3 us
  transfers between devices with their start and end apart: 6, of which 6 were waited for; matrix products, arithmetic and copies ran while one was open for 9% of the time, Pallas kernels for 0%

commit v1 on v0

v1 whole, which is shorter than its diff:
```python
import jax
import jax.numpy as jnp
from jax import lax
from jax.sharding import PartitionSpec as P

CHUNKS = 2


def contract_last(left, right):
    return lax.dot_general(
        left, right, (((1,), (1,)), ((), ())), preferred_element_type=jnp.float32
    )


def swap(block, axis, size, bit):
    return lax.ppermute(block, axis, [(i, i ^ bit) for i in range(size)])


def halves(blocks, bit_value):
    pairs = blocks.reshape((blocks.shape[0] // 2, 2) + blocks.shape[1:])
    other = lax.dynamic_index_in_dim(pairs, 1 - bit_value, 1, keepdims=False)
    own = lax.dynamic_index_in_dim(pairs, bit_value, 1, keepdims=False)
    return other, own


def flat(blocks):
    return blocks.reshape((-1, blocks.shape[-1]))


def halving(product, operands, axis, size):
    index = lax.axis_index(axis)
    m = operands[0].shape[1]
    received = []
    bit = 1
    while bit < size:
        bit_value = (index // bit) % 2
        split = [halves(x, bit_value) for x in operands]
        split_received = [halves(x, bit_value) for x in received]
        sent = product(*[flat(other) for other, _ in split])
        for other, _ in split_received:
            sent = sent + flat(other).astype(jnp.float32)
        sent = swap(sent.astype(jnp.bfloat16), axis, size, bit)
        operands = [own for _, own in split]
        received = [own for _, own in split_received]
        received.append(sent.reshape((-1, m, sent.shape[-1])))
        bit *= 2
    total = product(*[flat(x) for x in operands])
    for x in received:
        total = total + flat(x).astype(jnp.float32)
    return total


def doubling(block, axis, size):
    index = lax.axis_index(axis)
    blocks = block[None]
    bit = size // 2
    while bit:
        other = swap(blocks, axis, size, bit)
        low = (index // bit) % 2 == 0
        first = jnp.where(low, blocks, other)
        second = jnp.where(low, other, blocks)
        blocks = jnp.stack([first, second], axis=1).reshape((-1,) + block.shape)
        bit //= 2
    return blocks


def swiglu_grads(hidden_grad, gate_preact, up_preact):
    gate_float = gate_preact.astype(jnp.float32)
    up_float = up_preact.astype(jnp.float32)
    logistic = jax.nn.sigmoid(gate_float)
    derivative = logistic * (1.0 + gate_float * (1.0 - logistic))
    grad_gate = (hidden_grad * up_float * derivative).astype(jnp.bfloat16)
    grad_up = (hidden_grad * gate_float * logistic).astype(jnp.bfloat16)
    return (grad_gate, grad_up)


def from_root(block, axis, holder):
    block = jnp.where(lax.axis_index(axis) == holder, block, jnp.zeros_like(block))
    return lax.psum(block, axis)


def make_shards(rows, cols, tokens, slab_dev):
    def shards(output_grad, gate_preact, up_preact, gate_weight, up_weight, down_weight):
        units_dev = gate_weight.shape[1]
        part = output_grad.shape[0] // CHUNKS
        cols_per_row = cols // rows
        first_unit = lax.axis_index("row") * slab_dev
        owner_column = first_unit // units_dev
        offset = first_unit % units_dev

        def local_tokens(preact, h):
            split = preact.reshape((cols_per_row, CHUNKS, part, preact.shape[1]))
            return split[:, h].reshape((cols_per_row * part, preact.shape[1]))

        cotangents = [
            lax.all_gather(output_grad[h * part : (h + 1) * part], "col", axis=0, tiled=True)
            for h in range(CHUNKS)
        ]
        slabs, gates, outs = [], [], []
        for h in range(CHUNKS):
            cotangent = cotangents[h].reshape((rows, -1, output_grad.shape[1]))
            hidden_grad = halving(
                lambda x: contract_last(x, down_weight), [cotangent], "row", rows
            )
            grad_gate, grad_up = swiglu_grads(
                hidden_grad, local_tokens(gate_preact, h), local_tokens(up_preact, h)
            )
            gate_all = flat(doubling(grad_gate, "row", rows))
            own_slab = lax.dynamic_slice_in_dim(gate_all, offset, slab_dev, 1)
            slabs.append(from_root(own_slab, "col", owner_column))
            gates.append(gate_all)
            up_all = flat(doubling(grad_up, "row", rows))
            outs.append(
                halving(
                    lambda g, u: contract_last(g, gate_weight) + contract_last(u, up_weight),
                    [gate_all.reshape((cols, part, -1)), up_all.reshape((cols, part, -1))],
                    "col",
                    cols,
                )
            )
        factor = 0.0
        for slab, gate in zip(slabs, gates):
            factor = factor + lax.dot_general(
                slab, gate, (((0,), (0,)), ((), ())), preferred_element_type=jnp.float32
            )
        input_grad = jnp.concatenate([x.astype(jnp.bfloat16) for x in outs], axis=0)
        return (input_grad, factor / tokens)

    return shards


def solution(mesh):
    rows, cols = mesh.shape["row"], mesh.shape["col"]

    def run(output_grad, gate_preact, up_preact, gate_weight, up_weight, down_weight):
        tokens = output_grad.shape[0]
        shards = make_shards(rows, cols, tokens, SLAB_DEV)
        return jax.shard_map(
            shards,
            mesh=mesh,
            in_specs=(
                P("col", "row"),
                P("row", "col"),
                P("row", "col"),
                P("row", "col"),
                P("row", "col"),
                P("col", "row"),
            ),
            out_specs=(P("col", "row"), P("row", "col")),
            check_vma=False,
        )(output_grad, gate_preact, up_preact, gate_weight, up_weight, down_weight)

    return run


SLAB_DEV = 896
```

time: 743 us -> 578 us (0.78)
  waiting for transfers between devices: 623 us -> 248 us
  matrix products: 88.8 us -> 248 us
  local copies, waits for them, and re-layouts: 0.01 us -> 24.9 us
  starting transfers between devices: 0.42 us -> 14.8 us
    psum x1 -> x0, waiting for transfers between devices: 257 us -> none  [shards(): hidden_grad = lax.psum(hidden_part, 'row')]
    dot_general x3 -> x22, matrix products: 76.3 us -> 235 us  [contract_last(): lax.dot_general(left, right, (((1,), (1,)), ((), ())), preferred_element_...]
    reduce_scatter x1 -> x0, waiting for transfers between devices: 140 us -> none  [shards(): lax.psum_scatter(contract_last(grad_gate, gate_weight) + contract_last(gr...]
    ppermute x0 -> x18, waiting for transfers between devices: none -> 101 us  [swap(): return lax.ppermute(block, axis, [(i, i ^ bit) for i in range(size)])]
    all_gather x3 -> x2, waiting for transfers between devices: 160 us -> 99.8 us  [shards(): lax.all_gather(output_grad[h * part:(h + 1) * part], 'col', axis=0, tiled...]
    psum x1, waiting for transfers between devices: 64.3 us -> 46 us  [from_root(): return lax.psum(block, axis)]
    dynamic_slice x0 -> x11, local copies, waits for them, and re-layouts: none -> 17.3 us  [halves(): other = lax.dynamic_index_in_dim(pairs, 1 - bit_value, 1, keepdims=False)]
    ppermute x0 -> x18, starting transfers between devices: none -> 14.7 us  [swap(): return lax.ppermute(block, axis, [(i, i ^ bit) for i in range(size)])]
  transfers between devices with their start and end apart: 6 -> 21, of which waited for: 6 -> 11; matrix products, arithmetic and copies ran while one was open for 9% -> 47% of each run, Pallas kernels for 0% -> 0%
where the time goes in v1:
time: 578 us; the launch traced here: 572 us
  waiting for transfers between devices  248 us (43%)
  matrix products  248 us (43%)
  local copies, waits for them, and re-layouts  24.9 us (4%)
  other arithmetic  21.8 us (4%)
  starting transfers between devices  14.8 us (3%)
  between operations  14.6 us (3%)
    dot_general x22, matrix products, contract_last(): lax.dot_general(left, right, (((1,), (1,)), ((), ())), preferred_element_...  235 us
    ppermute x18, waiting for transfers between devices, swap(): return lax.ppermute(block, axis, [(i, i ^ bit) for i in range(size)])  101 us
    all_gather x2, waiting for transfers between devices, shards(): lax.all_gather(output_grad[h * part:(h + 1) * part], 'col', axis=0, tiled...  99.8 us
    psum x1, waiting for transfers between devices, from_root(): return lax.psum(block, axis)  46 us
    dynamic_slice x11, local copies, waits for them, and re-layouts, halves(): other = lax.dynamic_index_in_dim(pairs, 1 - bit_value, 1, keepdims=False)  17.3 us
    ppermute x18, starting transfers between devices, swap(): return lax.ppermute(block, axis, [(i, i ^ bit) for i in range(size)])  14.7 us
    dot_general x2, matrix products, shards(): lax.dot_general(slab, gate, (((0,), (0,)), ((), ())), preferred_element_t...  12.8 us
  transfers between devices with their start and end apart: 21, of which 11 were waited for; matrix products, arithmetic and copies ran while one was open for 47% of the time, Pallas kernels for 0%

profile of v1, /device:TPU:0, one launch (start us, length us, event | category | flops | bytes accessed | tf_op | source)
XLA Modules:
  0.0 571.8 jit_solution(6053253638162738080)
XLA Ops:
  7.2 1.9 fusion.86
  10.1 3.3 fusion.84
  13.4 49.3 %all-gather.5.cloned.1.call-done = bf16[512,2048]{1,0:T(8,128)(2,1)} async-done(((bf16[64,2048]{1,0:T(8,128)(2,1)}), bf16[512,2048]{1,0:T(8,128)(2,1)}) %all-gather.5.cloned.1.call-update) | async-done | bytes 2097168 | tf_op jit(solution)/shard_map/all_gather | solution.py:96
  62.7 50.5 %all-gather.3.cloned.1.call-done = bf16[512,2048]{1,0:T(8,128)(2,1)} async-done(((bf16[64,2048]{1,0:T(8,128)(2,1)}), bf16[512,2048]{1,0:T(8,128)(2,1)}) %all-gather.3.cloned.1.call-update) | async-done | bytes 2097168 | tf_op jit(solution)/shard_map/all_gather | solution.py:96
  113.2 2.8 constant_dynamic-slice_fusion.7
  116.0 10.7 %convolution_convert_fusion = bf16[256,3584]{1,0:T(8,128)(2,1)} fusion(bf16[256,2048]{1,0:T(8,128)(2,1)} %bitcast.291, bf16[3584,2048]{1,0:T(8,128)(2,1)} %param.11), kind=kOutput, calls=%fused_computation.1 | convolution fusion | flops 3759013888 | bytes 17563648 | tf_op jit(solution)/shard_map/dot_general | solution.py:10
  126.8 16.3 %convolution_convert_fusion.1 = bf16[256,3584]{1,0:T(8,128)(2,1)} fusion(bf16[256,2048]{1,0:T(8,128)(2,1)S(1)} %bitcast.290, bf16[3584,2048]{1,0:T(8,128)(2,1)} %param.11), kind=kOutput, calls=%fused_computation.2 | convolution fusion | flops 3759013888 | bytes 17563648 | tf_op jit(solution)/shard_map/dot_general | solution.py:10
  143.6 10.3 %fusion.36 = f32[128,3584]{1,0:T(8,128)S(1)} fusion(bf16[3584,2048]{1,0:T(8,128)(2,1)} %param.11, bf16[2,2,128,2048]{3,2,1,0:T(8,128)(2,1)} %bitcast.282, s32[]{:T(128)S(6)} %select_n.263, s32[]{:T(128)S(6)} %select_n.265), kind=kOutput, calls=%fused_computation.94 | convolution fusion | flops 1879048192 | bytes 17039368 | tf_op jit(solution)/shard_map/dot_general | solution.py:10
  153.9 11.4 %fusion.20 = bf16[128,3584]{1,0:T(8,128)(2,1)} fusion(bf16[1,2,128,3584]{3,2,1,0:T(8,128)(2,1)} %bitcast.46, s32[]{:T(128)S(6)} %select_n.267, bf16[3584,2048]{1,0:T(8,128)(2,1)} %param.11, bf16[2,2,128,2048]{3,2,1,0:T(8,128)(2,1)} %bitcast.283, s32[]{:T(128)S(6)} %select_n.268, s32[]{:T(128)S(6)} %select_n.265), kind=kOutput, calls=%fused_computation.47 | convolution fusion | flops 1880424448 | bytes 17039372 | tf_op jit(solution)/shard_map/dot_general | solution.py:10
  165.3 1.5 collective-permute-start.10
  166.8 10.3 %fusion.42 = f32[128,3584]{1,0:T(8,128)S(1)} fusion(bf16[3584,2048]{1,0:T(8,128)(2,1)} %param.11, bf16[2,2,128,2048]{3,2,1,0:T(8,128)(2,1)} %bitcast.279, s32[]{:T(128)S(6)} %select_n.263, s32[]{:T(128)S(6)} %select_n.265), kind=kOutput, calls=%fused_computation.98 | convolution fusion | flops 1879048192 | bytes 17039368 | tf_op jit(solution)/shard_map/dot_general | solution.py:10
  177.1 11.9 %fusion.22 = bf16[128,3584]{1,0:T(8,128)(2,1)} fusion(bf16[1,2,128,3584]{3,2,1,0:T(8,128)(2,1)} %bitcast.3, s32[]{:T(128)S(6)} %select_n.267, bf16[3584,2048]{1,0:T(8,128)(2,1)} %param.11, bf16[2,2,128,2048]{3,2,1,0:T(8,128)(2,1)} %bitcast.280, s32[]{:T(128)S(6)} %select_n.268, s32[]{:T(128)S(6)} %select_n.265), kind=kOutput, calls=%fused_computation.52 | convolution fusion | flops 1880424448 | bytes 17039372 | tf_op jit(solution)/shard_map/dot_general | solution.py:10
  189.5 2.6 fusion.19
  192.2 1.5 collective-permute-start.11
  194.3 18.2 %collective-permute-done.1 = bf16[128,3584]{1,0:T(8,128)(2,1)S(1)} collective-permute-done((bf16[128,3584]{1,0:T(8,128)(2,1)}, bf16[128,3584]{1,0:T(8,128)(2,1)S(1)}, u32[]{:S(2)}, u32[]{:S(2)}) %collective-permute-start.1) | collective-permute-done | bytes 917536 | tf_op jit(solution)/shard_map/ppermute | solution.py:16
  212.4 2.4 fusion.10
  215.4 1.5 collective-permute-start.4
  216.9 15.2 %collective-permute-done.11 = bf16[1,128,3584]{2,1,0:T(8,128)(2,1)S(1)} collective-permute-done((bf16[1,128,3584]{2,1,0:T(8,128)(2,1)S(1)}, bf16[1,128,3584]{2,1,0:T(8,128)(2,1)S(1)}, u32[]{:S(2)}, u32[]{:S(2)}) %collective-permute-start.11) | collective-permute-done | bytes 917536 | tf_op jit(solution)/shard_map/ppermute | solution.py:16
  232.5 19.3 %collective-permute-done.13 = bf16[1,128,3584]{2,1,0:T(8,128)(2,1)S(1)} collective-permute-done((bf16[1,128,3584]{2,1,0:T(8,128)(2,1)S(1)}, bf16[1,128,3584]{2,1,0:T(8,128)(2,1)S(1)}, u32[]{:S(2)}, u32[]{:S(2)}) %collective-permute-start.13) | collective-permute-done | bytes 917536 | tf_op jit(solution)/shard_map/ppermute | solution.py:16
  251.9 1.4 maximum_bitcast_fusion.3
  253.3 18.1 %collective-permute-done.2 = bf16[1,128,3584]{2,1,0:T(8,128)(2,1)S(1)} collective-permute-done((bf16[1,128,3584]{2,1,0:T(8,128)(2,1)S(1)}, bf16[1,128,3584]{2,1,0:T(8,128)(2,1)S(1)}, u32[]{:S(2)}, u32[]{:S(2)}) %collective-permute-start.2) | collective-permute-done | bytes 917536 | tf_op jit(solution)/shard_map/ppermute | solution.py:16
  271.8 18.0 %collective-permute-done.4 = bf16[1,128,3584]{2,1,0:T(8,128)(2,1)S(1)} collective-permute-done((bf16[1,128,3584]{2,1,0:T(8,128)(2,1)S(1)}, bf16[1,128,3584]{2,1,0:T(8,128)(2,1)S(1)}, u32[]{:S(2)}, u32[]{:S(2)}) %collective-permute-start.4) | collective-permute-done | bytes 917536 | tf_op jit(solution)/shard_map/ppermute | solution.py:16
  290.1 1.6 maximum_bitcast_fusion.1
  293.4 1.9 constant_dynamic-slice_fusion.4
  296.1 1.5 constant_dynamic-slice_fusion.12
  297.6 1.0 constant_dynamic-slice_fusion.2
  298.6 10.5 %fusion.52 = f32[64,2048]{1,0:T(8,128)} fusion(bf16[2048,3584]{1,0:T(8,128)(2,1)} %param.9, bf16[2,2,64,3584]{3,2,1,0:T(8,128)(2,1)S(1)} %bitcast.265, s32[]{:T(128)S(6)} %select_n.278, s32[]{:T(128)S(6)} %select_n.282), kind=kOutput, calls=%fused_computation.108 | convolution fusion | flops 939524096 | bytes 15663112 | tf_op jit(solution)/shard_map/dot_general | solution.py:10
  309.1 10.5 %fusion.58 = f32[64,2048]{1,0:T(8,128)} fusion(bf16[2048,3584]{1,0:T(8,128)(2,1)} %param.9, bf16[2,2,64,3584]{3,2,1,0:T(8,128)(2,1)S(1)} %bitcast.267, s32[]{:T(128)S(6)} %select_n.278, s32[]{:T(128)S(6)} %select_n.282), kind=kOutput, calls=%fused_computation.114 | convolution fusion | flops 939524096 | bytes 15663112 | tf_op jit(solution)/shard_map/dot_general | solution.py:10
  319.6 1.1 constant_dynamic-slice_fusion.10
  320.8 10.5 %fusion.49 = f32[64,2048]{1,0:T(8,128)} fusion(bf16[2048,3584]{1,0:T(8,128)(2,1)} %param.9, bf16[2,2,64,3584]{3,2,1,0:T(8,128)(2,1)S(1)} %bitcast.266, s32[]{:T(128)S(6)} %select_n.290, s32[]{:T(128)S(6)} %select_n.282), kind=kOutput, calls=%fused_computation.105 | convolution fusion | flops 939524096 | bytes 15663112 | tf_op jit(solution)/shard_map/dot_general | solution.py:10
  331.3 9.7 %fusion.55 = f32[64,2048]{1,0:T(8,128)S(1)} fusion(bf16[2048,3584]{1,0:T(8,128)(2,1)} %param.9, bf16[2,2,64,3584]{3,2,1,0:T(8,128)(2,1)S(1)} %bitcast.269, s32[]{:T(128)S(6)} %select_n.290, s32[]{:T(128)S(6)} %select_n.282), kind=kOutput, calls=%fused_computation.111 | convolution fusion | flops 939524096 | bytes 15663112 | tf_op jit(solution)/shard_map/dot_general | solution.py:10
  341.0 2.0 select_bitcast_fusion.1
  343.5 2.1 constant_dynamic-slice_fusion.3
  345.7 8.7 %fusion.89 = f32[256,2048]{1,0:T(8,128)} fusion(bf16[256,3584]{1,0:T(8,128)(2,1)S(1)} %bitcast.287, bf16[2048,3584]{1,0:T(8,128)(2,1)} %param.9), kind=kOutput, calls=%fused_computation.157 | convolution fusion | flops 3758096384 | bytes 18612224 | tf_op jit(solution)/shard_map/dot_general | solution.py:10
  354.4 11.3 %fusion.1 = bf16[256,2048]{1,0:T(8,128)(2,1)} fusion(f32[256,2048]{1,0:T(8,128)} %fusion.89, bf16[256,3584]{1,0:T(8,128)(2,1)} %bitcast.289, bf16[2048,3584]{1,0:T(8,128)(2,1)} %param.10), kind=kOutput, calls=%fused_computation.16 | convolution fusion | flops 3759144960 | bytes 19660800 | tf_op jit(solution)/shard_map/dot_general | solution.py:10
  366.3 2.2 constant_dynamic-slice_fusion.1
  368.4 10.7 %convolution_add_fusion.5 = f32[64,2048]{1,0:T(8,128)} fusion(f32[64,2048]{1,0:T(8,128)S(1)} %copy-done.16, bf16[2048,3584]{1,0:T(8,128)(2,1)} %param.10, bf16[2,2,64,3584]{3,2,1,0:T(8,128)(2,1)} %bitcast.259, s32[]{:T(128)S(6)} %select_n.278, s32[]{:T(128)S(6)} %select_n.282), kind=kOutput, calls=%fused_computation.20 | convolution fusion | flops 939655168 | bytes 16187400 | tf_op jit(solution)/shard_map/dot_general | solution.py:10
  379.1 11.0 %fusion.90 = f32[128,2048]{1,0:T(8,128)} fusion(bf16[128,3584]{1,0:T(8,128)(2,1)S(1)} %bitcast.273, bf16[2048,3584]{1,0:T(8,128)(2,1)} %param.9), kind=kOutput, calls=%fused_computation.158 | convolution fusion | flops 1879048192 | bytes 16646144 | tf_op jit(solution)/shard_map/dot_general | solution.py:10
  390.2 1.9 select_bitcast_fusion.5
  392.6 1.5 constant_dynamic-slice_fusion.11
  395.5 10.6 %convolution_add_fusion.7 = f32[64,2048]{1,0:T(8,128)} fusion(f32[64,2048]{1,0:T(8,128)S(1)} %copy-done.15, bf16[2048,3584]{1,0:T(8,128)(2,1)} %param.10, bf16[2,2,64,3584]{3,2,1,0:T(8,128)(2,1)S(1)} %bitcast.262, s32[]{:T(128)S(6)} %select_n.278, s32[]{:T(128)S(6)} %select_n.282), kind=kOutput, calls=%fused_computation.22 | convolution fusion | flops 939655168 | bytes 16187400 | tf_op jit(solution)/shard_map/dot_general | solution.py:10
  406.2 9.0 %fusion.87 = f32[256,2048]{1,0:T(8,128)} fusion(bf16[256,3584]{1,0:T(8,128)(2,1)S(1)} %bitcast.286, bf16[2048,3584]{1,0:T(8,128)(2,1)} %param.9), kind=kOutput, calls=%fused_computation.155 | convolution fusion | flops 3758096384 | bytes 18612224 | tf_op jit(solution)/shard_map/dot_general | solution.py:10
  415.2 11.3 %fusion = bf16[256,2048]{1,0:T(8,128)(2,1)} fusion(f32[256,2048]{1,0:T(8,128)} %fusion.87, bf16[256,3584]{1,0:T(8,128)(2,1)} %bitcast.288, bf16[2048,3584]{1,0:T(8,128)(2,1)} %param.10), kind=kOutput, calls=%fused_computation.15 | convolution fusion | flops 3759144960 | bytes 19660800 | tf_op jit(solution)/shard_map/dot_general | solution.py:10
  426.6 1.5 collective-permute-start.6
  428.0 2.7 dynamic-slice_select_fusion.1
  430.7 1.4 dynamic-slice_select_fusion
  432.1 10.5 %fusion.88 = f32[128,2048]{1,0:T(8,128)S(1)} fusion(bf16[128,3584]{1,0:T(8,128)(2,1)S(1)} %bitcast.270, bf16[2048,3584]{1,0:T(8,128)(2,1)} %param.9), kind=kOutput, calls=%fused_computation.156 | convolution fusion | flops 1879048192 | bytes 16646144 | tf_op jit(solution)/shard_map/dot_general | solution.py:10
  442.7 1.1 constant_dynamic-slice_fusion
  443.8 10.0 %fusion.24 = bf16[128,2048]{1,0:T(8,128)(2,1)S(1)} fusion(bf16[2,1,64,2048]{3,2,1,0:T(8,128)(2,1)S(1)} %constant_dynamic-slice_fusion, f32[128,2048]{1,0:T(8,128)S(1)} %copy-done.6, bf16[128,3584]{1,0:T(8,128)(2,1)S(1)} %bitcast.271, bf16[2048,3584]{1,0:T(8,128)(2,1)} %param.10), kind=kOutput, calls=%fused_computation.64 | convolution fusion | flops 1880096768 | bytes 17694720 | tf_op jit(solution)/shard_map/dot_general | solution.py:10
  453.8 1.6 collective-permute-start.16
  455.4 3.5 collective-permute-done.6
  458.9 1.1 constant_dynamic-slice_fusion.8
  460.0 10.0 %fusion.25 = bf16[128,2048]{1,0:T(8,128)(2,1)S(1)} fusion(bf16[2,1,64,2048]{3,2,1,0:T(8,128)(2,1)S(1)} %constant_dynamic-slice_fusion.8, f32[128,2048]{1,0:T(8,128)S(1)} %fusion.88, bf16[128,3584]{1,0:T(8,128)(2,1)S(1)} %bitcast.272, bf16[2048,3584]{1,0:T(8,128)(2,1)} %param.10), kind=kOutput, calls=%fused_computation.66 | convolution fusion | flops 1880096768 | bytes 17694720 | tf_op jit(solution)/shard_map/dot_general | solution.py:10
  470.1 1.5 collective-permute-start.7
  471.6 1.9 collective-permute-done.16
  473.5 10.1 %fusion.26 = bf16[64,2048]{1,0:T(8,128)(2,1)S(1)} fusion(bf16[1,2,64,2048]{3,2,1,0:T(8,128)(2,1)S(1)} %bitcast.292, s32[]{:T(128)S(6)} %select_n.289, bf16[2,2,64,2048]{3,2,1,0:T(8,128)(2,1)} %bitcast.73, s32[]{:T(128)S(6)} %select_n.290, s32[]{:T(128)S(6)} %select_n.282, f32[64,2048]{1,0:T(8,128)S(1)} %copy-done.12, bf16[2048,3584]{1,0:T(8,128)(2,1)} %param.10, ...), kind=kOutput, calls=%fused_computation.79 | convolution fusion | flops 940310528 | bytes 16452096 | tf_op jit(solution)/shard_map/dot_general | solution.py:10
  483.6 2.6 collective-permute-start.17
  486.2 7.0 %collective-permute-done.7 = bf16[128,2048]{1,0:T(8,128)(2,1)S(1)} collective-permute-done((bf16[128,2048]{1,0:T(8,128)(2,1)S(1)}, bf16[128,2048]{1,0:T(8,128)(2,1)S(1)}, u32[]{:S(2)}, u32[]{:S(2)}) %collective-permute-start.7) | collective-permute-done | bytes 524320 | tf_op jit(solution)/shard_map/ppermute | solution.py:16
  493.2 9.8 %fusion.29 = bf16[64,2048]{1,0:T(8,128)(2,1)S(1)} fusion(bf16[1,2,64,2048]{3,2,1,0:T(8,128)(2,1)S(1)} %bitcast.294, s32[]{:T(128)S(6)} %select_n.289, bf16[2,2,64,2048]{3,2,1,0:T(8,128)(2,1)} %bitcast.32, s32[]{:T(128)S(6)} %select_n.290, s32[]{:T(128)S(6)} %select_n.282, f32[64,2048]{1,0:T(8,128)S(1)} %fusion.55, bf16[2048,3584]{1,0:T(8,128)(2,1)} %param.10, ...), kind=kOutput, calls=%fused_computation.86 | convolution fusion | flops 940310528 | bytes 16452096 | tf_op jit(solution)/shard_map/dot_general | solution.py:10
  503.0 46.0 %all-reduce.3.cloned.1.call-done = (bf16[512,896]{1,0:T(8,128)(2,1)}, bf16[512,896]{1,0:T(8,128)(2,1)}) async-done(((bf16[512,896]{1,0:T(8,128)(2,1)}, bf16[512,896]{1,0:T(8,128)(2,1)}), (bf16[512,896]{1,0:T(8,128)(2,1)}, bf16[512,896]{1,0:T(8,128)(2,1)})) %all-reduce.3.cloned.1.call-update) | async-done | bytes 1835024 | tf_op jit(solution)/shard_map/psum | solution.py:79
  549.1 6.0 %fusion.91 = f32[896,3584]{1,0:T(8,128)S(1)} fusion(bf16[512,896]{1,0:T(8,128)(2,1)} %get-tuple-element.2, bf16[512,3584]{1,0:T(8,128)(2,1)} %bitcast.255), kind=kOutput, calls=%fused_computation.159 | convolution fusion | flops 3288334336 | bytes 17432576 | tf_op jit(solution)/shard_map/dot_general | solution.py:123
  555.1 1.2 fusion.28
  556.3 1.1 fusion.31
  558.3 6.8 %add_multiply_fusion = f32[896,3584]{1,0:T(8,128)} fusion(f32[896,3584]{1,0:T(8,128)S(1)} %fusion.91, bf16[512,896]{1,0:T(8,128)(2,1)S(1)} %copy-done.19, bf16[512,3584]{1,0:T(8,128)(2,1)S(1)} %bitcast.252), kind=kOutput, calls=%fused_computation | convolution fusion | flops 3294756864 | bytes 30277632 | tf_op jit(solution)/shard_map/dot_general | solution.py:123
  (85 shorter events, 11.0 us)
Async XLA Ops:
  7.2 55.6 %all-gather.5.cloned.1.call-start = ((), (), s32[]{:S(2)}) async-start(), calls=%async_computation.1 | async-start | bytes 2359296 | tf_op jit(solution)/shard_map/all_gather | solution.py:96
  9.1 104.1 %all-gather.3.cloned.1.call-start = ((), (), s32[]{:S(2)}) async-start(), calls=%async_computation | async-start | bytes 2359296 | tf_op jit(solution)/shard_map/all_gather | solution.py:96
  9.9 539.2 %all-reduce.3.cloned.1.call-start = ((), (), s32[]{:S(2)}) async-start(), calls=%async_computation.2 | async-start | bytes 3670016 | tf_op jit(solution)/shard_map/psum | solution.py:79
  126.8 27.2 %collective-permute-start.9 = (bf16[256,3584]{1,0:T(8,128)(2,1)}, bf16[256,3584]{1,0:T(8,128)(2,1)}, u32[]{:S(2)}, u32[]{:S(2)}) collective-permute-start(bf16[256,3584]{1,0:T(8,128)(2,1)} %convolution_convert_fusion), channel_id=1, source_target_pairs={{0,8},{8,0},{16,24},{24,16},{1,9},{9,1},{17,25},{25,17},{2,10},{10... | collective-permute-start | bytes 5505032 | tf_op jit(solution)/shard_map/ppermute | solution.py:16
  143.0 34.0 %collective-permute-start = (bf16[256,3584]{1,0:T(8,128)(2,1)}, bf16[256,3584]{1,0:T(8,128)(2,1)}, u32[]{:S(2)}, u32[]{:S(2)}) collective-permute-start(bf16[256,3584]{1,0:T(8,128)(2,1)} %convolution_convert_fusion.1), channel_id=1, source_target_pairs={{0,8},{8,0},{16,24},{24,16},{1,9},{9,1},{17,25},{25,17},{2,10},{10... | collective-permute-start | bytes 5505032 | tf_op jit(solution)/shard_map/ppermute | solution.py:16
  165.3 24.2 %collective-permute-start.10 = (bf16[128,3584]{1,0:T(8,128)(2,1)}, bf16[128,3584]{1,0:T(8,128)(2,1)}, u32[]{:S(2)}, u32[]{:S(2)}) collective-permute-start(bf16[128,3584]{1,0:T(8,128)(2,1)} %fusion.20), channel_id=1, source_target_pairs={{0,16},{8,24},{16,0},{24,8},{1,17},{9,25},{17,1},{25,9},{2,18},{10... | collective-permute-start | bytes 2752520 | tf_op jit(solution)/shard_map/ppermute | solution.py:16
  177.1 12.4 %copy-start.11 = (bf16[2,1,64,3584]{3,2,1,0:T(8,128)(2,1)S(1)}, bf16[2,1,64,3584]{3,2,1,0:T(8,128)(2,1)}, u32[]{:S(2)}) copy-start(bf16[2,1,64,3584]{3,2,1,0:T(8,128)(2,1)} %get-tuple-element.40) | copy-start | bytes 2752516
  189.0 23.5 %collective-permute-start.1 = (bf16[128,3584]{1,0:T(8,128)(2,1)}, bf16[128,3584]{1,0:T(8,128)(2,1)S(1)}, u32[]{:S(2)}, u32[]{:S(2)}) collective-permute-start(bf16[128,3584]{1,0:T(8,128)(2,1)} %fusion.22), channel_id=1, source_target_pairs={{0,16},{8,24},{16,0},{24,8},{1,17},{9,25},{17,1},{25,9},{2,18},{10... | collective-permute-start | bytes 2752520 | tf_op jit(solution)/shard_map/ppermute | solution.py:16
  192.2 39.9 %collective-permute-start.11 = (bf16[1,128,3584]{2,1,0:T(8,128)(2,1)S(1)}, bf16[1,128,3584]{2,1,0:T(8,128)(2,1)S(1)}, u32[]{:S(2)}, u32[]{:S(2)}) collective-permute-start(bf16[1,128,3584]{2,1,0:T(8,128)(2,1)S(1)} %bitcast.277), channel_id=1, source_target_pairs={{0,16},{8,24},{16,0},{24,8},{1,17},{9,25},{17,1},{25,9},{2,18},{10... | collective-permute-start | bytes 2752520 | tf_op jit(solution)/shard_map/ppermute | solution.py:16
  193.7 58.0 %collective-permute-start.13 = (bf16[1,128,3584]{2,1,0:T(8,128)(2,1)S(1)}, bf16[1,128,3584]{2,1,0:T(8,128)(2,1)S(1)}, u32[]{:S(2)}, u32[]{:S(2)}) collective-permute-start(bf16[1,128,3584]{2,1,0:T(8,128)(2,1)S(1)} %bitcast.275), channel_id=1, source_target_pairs={{0,16},{8,24},{16,0},{24,8},{1,17},{9,25},{17,1},{25,9},{2,18},{10... | collective-permute-start | bytes 2752520 | tf_op jit(solution)/shard_map/ppermute | solution.py:16
  214.8 56.6 %collective-permute-start.2 = (bf16[1,128,3584]{2,1,0:T(8,128)(2,1)S(1)}, bf16[1,128,3584]{2,1,0:T(8,128)(2,1)S(1)}, u32[]{:S(2)}, u32[]{:S(2)}) collective-permute-start(bf16[1,128,3584]{2,1,0:T(8,128)(2,1)S(1)} %bitcast.276), channel_id=1, source_target_pairs={{0,16},{8,24},{16,0},{24,8},{1,17},{9,25},{17,1},{25,9},{2,18},{10... | collective-permute-start | bytes 2752520 | tf_op jit(solution)/shard_map/ppermute | solution.py:16
  215.4 74.4 %collective-permute-start.4 = (bf16[1,128,3584]{2,1,0:T(8,128)(2,1)S(1)}, bf16[1,128,3584]{2,1,0:T(8,128)(2,1)S(1)}, u32[]{:S(2)}, u32[]{:S(2)}) collective-permute-start(bf16[1,128,3584]{2,1,0:T(8,128)(2,1)S(1)} %bitcast.274), channel_id=1, source_target_pairs={{0,16},{8,24},{16,0},{24,8},{1,17},{9,25},{17,1},{25,9},{2,18},{10... | collective-permute-start | bytes 2752520 | tf_op jit(solution)/shard_map/ppermute | solution.py:16
  232.4 59.2 %collective-permute-start.12 = (bf16[2,128,3584]{2,1,0:T(8,128)(2,1)S(1)}, bf16[2,128,3584]{2,1,0:T(8,128)(2,1)S(1)}, u32[]{:S(2)}, u32[]{:S(2)}) collective-permute-start(bf16[2,128,3584]{2,1,0:T(8,128)(2,1)S(1)} %maximum_bitcast_fusion.2), channel_id=1, source_target_pairs={{0,8},{8,0},{16,24},{24,16},{1,9},{9,1},{17,25},{25,17},{2,10},{10... | collective-permute-start | bytes 5505032 | tf_op jit(solution)/shard_map/ppermute | solution.py:16
  253.3 87.6 %collective-permute-start.14 = (bf16[2,128,3584]{2,1,0:T(8,128)(2,1)}, bf16[2,128,3584]{2,1,0:T(8,128)(2,1)}, u32[]{:S(2)}, u32[]{:S(2)}) collective-permute-start(bf16[2,128,3584]{2,1,0:T(8,128)(2,1)} %maximum_bitcast_fusion.3), channel_id=1, source_target_pairs={{0,8},{8,0},{16,24},{24,16},{1,9},{9,1},{17,25},{25,17},{2,10},{10... | collective-permute-start | bytes 5505032 | tf_op jit(solution)/shard_map/ppermute | solution.py:16
  271.7 20.8 %collective-permute-start.3 = (bf16[2,128,3584]{2,1,0:T(8,128)(2,1)S(1)}, bf16[2,128,3584]{2,1,0:T(8,128)(2,1)S(1)}, u32[]{:S(2)}, u32[]{:S(2)}) collective-permute-start(bf16[2,128,3584]{2,1,0:T(8,128)(2,1)S(1)} %maximum_bitcast_fusion), channel_id=1, source_target_pairs={{0,8},{8,0},{16,24},{24,16},{1,9},{9,1},{17,25},{25,17},{2,10},{10... | collective-permute-start | bytes 5505032 | tf_op jit(solution)/shard_map/ppermute | solution.py:16
  290.1 1.6 copy-start.3
  291.6 98.5 %collective-permute-start.5 = (bf16[2,128,3584]{2,1,0:T(8,128)(2,1)}, bf16[2,128,3584]{2,1,0:T(8,128)(2,1)}, u32[]{:S(2)}, u32[]{:S(2)}) collective-permute-start(bf16[2,128,3584]{2,1,0:T(8,128)(2,1)} %maximum_bitcast_fusion.1), channel_id=1, source_target_pairs={{0,8},{8,0},{16,24},{24,16},{1,9},{9,1},{17,25},{25,17},{2,10},{10... | collective-permute-start | bytes 5505032 | tf_op jit(solution)/shard_map/ppermute | solution.py:16
  292.5 138.2 %copy-start = (bf16[2,2,128,3584]{3,2,1,0:T(8,128)(2,1)}, bf16[2,2,128,3584]{3,2,1,0:T(8,128)(2,1)S(1)}, u32[]{:S(2)}) copy-start(bf16[2,2,128,3584]{3,2,1,0:T(8,128)(2,1)S(1)} %copy.18) | copy-start | bytes 11010052
  293.3 2.7 copy-start.2
  343.5 2.2 copy-start.18
  365.7 2.7 copy-start.16
  365.7 77.0 %collective-permute-start.15 = (bf16[256,2048]{1,0:T(8,128)(2,1)}, bf16[256,2048]{1,0:T(8,128)(2,1)}, u32[]{:S(2)}, u32[]{:S(2)}) collective-permute-start(bf16[256,2048]{1,0:T(8,128)(2,1)} %fusion.1), channel_id=1, source_target_pairs={{0,1},{1,0},{2,3},{3,2},{4,5},{5,4},{6,7},{7,6},{8,9},{9,8},{10,11... | collective-permute-start | bytes 3145736 | tf_op jit(solution)/shard_map/ppermute | solution.py:16
  368.4 10.7 %copy-start.10 = (bf16[2,1,64,3584]{3,2,1,0:T(8,128)(2,1)S(1)}, bf16[2,1,64,3584]{3,2,1,0:T(8,128)(2,1)}, u32[]{:S(2)}) copy-start(bf16[2,1,64,3584]{3,2,1,0:T(8,128)(2,1)} %constant_dynamic-slice_fusion.2) | copy-start | bytes 2752516
  379.1 11.0 %copy-start.4 = (bf16[1,1,128,3584]{3,2,1,0:T(8,128)(2,1)S(1)}, bf16[1,1,128,3584]{3,2,1,0:T(8,128)(2,1)}, u32[]{:S(2)}) copy-start(bf16[1,1,128,3584]{3,2,1,0:T(8,128)(2,1)} %copy-done.3) | copy-start | bytes 2752516
  394.1 12.0 %copy-start.5 = (bf16[4,1,64,3584]{3,2,1,0:T(8,128)(2,1)}, bf16[4,1,64,3584]{3,2,1,0:T(8,128)(2,1)S(1)}, u32[]{:S(2)}) copy-start(bf16[4,1,64,3584]{3,2,1,0:T(8,128)(2,1)S(1)} %get-tuple-element.9) | copy-start | bytes 5505028
  394.1 1.4 copy-start.15
  395.5 10.6 %copy-start.17 = (bf16[4,1,64,3584]{3,2,1,0:T(8,128)(2,1)S(1)}, bf16[4,1,64,3584]{3,2,1,0:T(8,128)(2,1)}, u32[]{:S(2)}) copy-start(bf16[4,1,64,3584]{3,2,1,0:T(8,128)(2,1)} %get-tuple-element.10) | copy-start | bytes 5505028
  426.6 32.3 %collective-permute-start.6 = (bf16[256,2048]{1,0:T(8,128)(2,1)}, bf16[256,2048]{1,0:T(8,128)(2,1)}, u32[]{:S(2)}, u32[]{:S(2)}) collective-permute-start(bf16[256,2048]{1,0:T(8,128)(2,1)} %fusion), channel_id=1, source_target_pairs={{0,1},{1,0},{2,3},{3,2},{4,5},{5,4},{6,7},{7,6},{8,9},{9,8},{10,11... | collective-permute-start | bytes 3145736 | tf_op jit(solution)/shard_map/ppermute | solution.py:16
  430.7 1.4 copy-start.7
  432.1 11.6 %copy-start.6 = (f32[128,2048]{1,0:T(8,128)S(1)}, f32[128,2048]{1,0:T(8,128)}, u32[]{:S(2)}) copy-start(f32[128,2048]{1,0:T(8,128)} %fusion.90) | copy-start | bytes 3145732
  432.1 11.6 %copy-start.8 = (bf16[2,1,64,3584]{3,2,1,0:T(8,128)(2,1)S(1)}, bf16[2,1,64,3584]{3,2,1,0:T(8,128)(2,1)}, u32[]{:S(2)}) copy-start(bf16[2,1,64,3584]{3,2,1,0:T(8,128)(2,1)} %constant_dynamic-slice_fusion.1) | copy-start | bytes 2752516
  443.8 16.2 %copy-start.9 = (bf16[2,1,64,3584]{3,2,1,0:T(8,128)(2,1)S(1)}, bf16[2,1,64,3584]{3,2,1,0:T(8,128)(2,1)}, u32[]{:S(2)}) copy-start(bf16[2,1,64,3584]{3,2,1,0:T(8,128)(2,1)} %constant_dynamic-slice_fusion.9) | copy-start | bytes 2752516
  453.8 19.7 %collective-permute-start.16 = (bf16[128,2048]{1,0:T(8,128)(2,1)S(1)}, bf16[128,2048]{1,0:T(8,128)(2,1)S(1)}, u32[]{:S(2)}, u32[]{:S(2)}) collective-permute-start(bf16[128,2048]{1,0:T(8,128)(2,1)S(1)} %fusion.24), channel_id=1, source_target_pairs={{0,2},{1,3},{2,0},{3,1},{4,6},{5,7},{6,4},{7,5},{8,10},{9,11},{10,... | collective-permute-start | bytes 1572872 | tf_op jit(solution)/shard_map/ppermute | solution.py:16
  460.0 13.5 %copy-start.12 = (f32[64,2048]{1,0:T(8,128)S(1)}, f32[64,2048]{1,0:T(8,128)}, u32[]{:S(2)}) copy-start(f32[64,2048]{1,0:T(8,128)} %fusion.49) | copy-start | bytes 1572868
  470.1 23.1 %collective-permute-start.7 = (bf16[128,2048]{1,0:T(8,128)(2,1)S(1)}, bf16[128,2048]{1,0:T(8,128)(2,1)S(1)}, u32[]{:S(2)}, u32[]{:S(2)}) collective-permute-start(bf16[128,2048]{1,0:T(8,128)(2,1)S(1)} %fusion.25), channel_id=1, source_target_pairs={{0,2},{1,3},{2,0},{3,1},{4,6},{5,7},{6,4},{7,5},{8,10},{9,11},{10,... | collective-permute-start | bytes 1572872 | tf_op jit(solution)/shard_map/ppermute | solution.py:16
  483.6 71.4 %collective-permute-start.17 = (bf16[64,2048]{1,0:T(8,128)(2,1)S(1)}, bf16[64,2048]{1,0:T(8,128)(2,1)S(1)}, u32[]{:S(2)}, u32[]{:S(2)}) collective-permute-start(bf16[64,2048]{1,0:T(8,128)(2,1)S(1)} %fusion.26), channel_id=1, source_target_pairs={{0,4},{1,5},{2,6},{3,7},{4,0},{5,1},{6,2},{7,3},{8,12},{9,13},{10,... | collective-permute-start | bytes 786440 | tf_op jit(solution)/shard_map/ppermute | solution.py:16
  503.0 53.3 %collective-permute-start.8 = (bf16[64,2048]{1,0:T(8,128)(2,1)S(1)}, bf16[64,2048]{1,0:T(8,128)(2,1)S(1)}, u32[]{:S(2)}, u32[]{:S(2)}) collective-permute-start(bf16[64,2048]{1,0:T(8,128)(2,1)S(1)} %fusion.29), channel_id=1, source_target_pairs={{0,4},{1,5},{2,6},{3,7},{4,0},{5,1},{6,2},{7,3},{8,12},{9,13},{10,... | collective-permute-start | bytes 786440 | tf_op jit(solution)/shard_map/ppermute | solution.py:16
  549.0 6.0 %copy-start.13 = (f32[64,2048]{1,0:T(8,128)S(1)}, f32[64,2048]{1,0:T(8,128)}, u32[]{:S(2)}) copy-start(f32[64,2048]{1,0:T(8,128)} %convolution_add_fusion.5) | copy-start | bytes 1572868
  549.0 7.3 %copy-start.14 = (f32[64,2048]{1,0:T(8,128)S(1)}, f32[64,2048]{1,0:T(8,128)}, u32[]{:S(2)}) copy-start(f32[64,2048]{1,0:T(8,128)} %convolution_add_fusion.7) | copy-start | bytes 1572868
  549.0 9.2 %copy-start.19 = (bf16[512,896]{1,0:T(8,128)(2,1)S(1)}, bf16[512,896]{1,0:T(8,128)(2,1)}, u32[]{:S(2)}) copy-start(bf16[512,896]{1,0:T(8,128)(2,1)} %get-tuple-element.3) | copy-start | bytes 2752516
  555.0 3.2 copy-start.1
Sparse Core Ops, SparseCore 0:
  10.7 51.9 all-gather.4
  65.4 47.7 all-gather.2
  432.2 116.7 all-reduce.2

commit v2 on v0

v2 whole, which is shorter than its diff:
```python
import jax
import jax.numpy as jnp
from jax import lax
from jax.sharding import PartitionSpec as P

CHUNKS = 2
SLAB_DEV = 896


def contract_last(left, right):
    return lax.dot_general(
        left, right, (((1,), (1,)), ((), ())), preferred_element_type=jnp.float32
    )


def swap(block, axis, size, bit):
    return lax.ppermute(block, axis, [(i, i ^ bit) for i in range(size)])


def bits_down(size):
    bit = size // 2
    while bit:
        yield bit
        bit //= 2


def gather_relative(block, axis, size):
    pieces = {0: block}
    for bit in bits_down(size):
        for k in sorted(pieces):
            pieces[k | bit] = swap(pieces[k], axis, size, bit)
    return [pieces[k] for k in range(size)]


def halving_order(size):
    if size == 1:
        return [0]
    rest = halving_order(size // 2)
    return [2 * k + 1 for k in rest] + [2 * k for k in rest]


def halving(total, axis, size):
    m = total.shape[0] // size
    received = []
    bit, left = 1, size
    while left > 1:
        half = left // 2 * m
        sent = total[:half]
        for x in received:
            sent = sent + x[:half].astype(jnp.float32)
        received = [x[half:] for x in received]
        received.append(swap(sent.astype(jnp.bfloat16), axis, size, bit))
        total = total[half:]
        bit, left = bit * 2, left // 2
    for x in received:
        total = total + x.astype(jnp.float32)
    return total


def pick(stacked, index, m):
    return lax.dynamic_slice_in_dim(stacked, index * m, m, 0)


def swiglu_grads(hidden_grad, gate_preact, up_preact):
    gate_float = gate_preact.astype(jnp.float32)
    up_float = up_preact.astype(jnp.float32)
    logistic = jax.nn.sigmoid(gate_float)
    derivative = logistic * (1.0 + gate_float * (1.0 - logistic))
    grad_gate = (hidden_grad * up_float * derivative).astype(jnp.bfloat16)
    grad_up = (hidden_grad * gate_float * logistic).astype(jnp.bfloat16)
    return (grad_gate, grad_up)


def make_shards(rows, cols):
    def shards(output_grad, gate_preact, up_preact, gate_weight, up_weight, down_weight):
        units_dev = gate_weight.shape[1]
        part = output_grad.shape[0] // CHUNKS
        tokens = output_grad.shape[0] * cols
        per_row = cols // rows
        row, col = lax.axis_index("row"), lax.axis_index("col")
        offset = (row * SLAB_DEV) % units_dev
        holders = [r * SLAB_DEV // units_dev for r in range(rows)]
        from_holder = col ^ ((row * SLAB_DEV) // units_dev)

        def broadcast(slab):
            for bit in bits_down(cols):
                pairs = [
                    (r * cols + (holders[r] ^ k), r * cols + (holders[r] ^ k ^ bit))
                    for r in range(rows)
                    for k in range(0, cols, 2 * bit)
                ]
                arrived = lax.ppermute(slab, ("row", "col"), pairs)
                slab = jnp.where(from_holder % (2 * bit) == bit, arrived, slab)
            return slab

        def local_tokens(preact, h):
            split = preact.reshape((per_row, CHUNKS, part, preact.shape[1]))
            return split[:, h].reshape((per_row * part, preact.shape[1]))

        def cotangent(h):
            pieces = gather_relative(output_grad[h * part : (h + 1) * part], "col", cols)
            stacked = jnp.concatenate(pieces, axis=0)
            wanted = [
                col ^ ((row ^ j) * per_row + sub)
                for j in halving_order(rows)
                for sub in range(per_row)
            ]
            return jnp.concatenate([pick(stacked, k, part) for k in wanted], axis=0)

        def scatter(total):
            blocks = []
            for k in halving_order(cols):
                target = col ^ k
                position = (row ^ (target // per_row)) * per_row + target % per_row
                blocks.append(pick(total, position, part))
            return halving(jnp.concatenate(blocks, axis=0), "col", cols)

        hidden = [
            halving(contract_last(cotangent(h), down_weight), "row", rows) for h in range(CHUNKS)
        ]
        grads = [
            swiglu_grads(hidden[h], local_tokens(gate_preact, h), local_tokens(up_preact, h))
            for h in range(CHUNKS)
        ]
        gates, slabs, outs = [], [], []
        for h in range(CHUNKS):
            gates.append(jnp.concatenate(gather_relative(grads[h][0], "row", rows), axis=0))
            slabs.append(broadcast(lax.dynamic_slice_in_dim(gates[h], offset, SLAB_DEV, 1)))
        for h in range(CHUNKS):
            up_all = jnp.concatenate(gather_relative(grads[h][1], "row", rows), axis=0)
            outs.append(
                scatter(contract_last(gates[h], gate_weight) + contract_last(up_all, up_weight))
            )
        factor = lax.dot_general(
            jnp.concatenate(slabs, axis=0),
            jnp.concatenate(gates, axis=0),
            (((0,), (0,)), ((), ())),
            preferred_element_type=jnp.float32,
        )
        input_grad = jnp.concatenate([x.astype(jnp.bfloat16) for x in outs], axis=0)
        return (input_grad, factor / tokens)

    return shards


def solution(mesh):
    return jax.shard_map(
        make_shards(mesh.shape["row"], mesh.shape["col"]),
        mesh=mesh,
        in_specs=(
            P("col", "row"),
            P("row", "col"),
            P("row", "col"),
            P("row", "col"),
            P("row", "col"),
            P("col", "row"),
        ),
        out_specs=(P("col", "row"), P("row", "col")),
        check_vma=False,
    )
```

time: 743 us -> 415 us (0.56)
  waiting for transfers between devices: 623 us -> 236 us
  starting transfers between devices: 0.42 us -> 40.9 us
  local copies, waits for them, and re-layouts: 0.01 us -> 31.2 us
  between operations: 14.2 us -> 1.16 us
    psum x2 -> x0, waiting for transfers between devices: 321 us -> none  [the longest x1 257 us: shards(): hidden_grad = lax.psum(hidden_part, 'row')]
    ppermute x0 -> x42, waiting for transfers between devices: none -> 236 us  [the longest x36 181 us: swap(): return lax.ppermute(block, axis, [(i, i ^ bit) for i in range(size)])]
    all_gather x3 -> x0, waiting for transfers between devices: 160 us -> none  [the longest x1 76.8 us: shards(): cotangent_all = lax.all_gather(output_grad, 'col', axis=0, tiled=True)]
    reduce_scatter x1 -> x0, waiting for transfers between devices: 140 us -> none  [shards(): lax.psum_scatter(contract_last(grad_gate, gate_weight) + contract_last(gr...]
    ppermute x0 -> x42, starting transfers between devices: none -> 40.9 us  [the longest x36 30.5 us: swap(): return lax.ppermute(block, axis, [(i, i ^ bit) for i in range(size)])]
    unnamed x2 -> x48, local copies, waits for them, and re-layouts: 0.01 us -> 19.9 us
    dot_general x3 -> x6, matrix products: 76.3 us -> 76.7 us  [contract_last(): lax.dot_general(left, right, (((1,), (1,)), ((), ())), preferred_element_...]
  transfers between devices with their start and end apart: 6 -> 42, of which waited for: 6 -> 23; matrix products, arithmetic and copies ran while one was open for 9% -> 25% of each run, Pallas kernels for 0% -> 0%
where the time goes in v2:
time: 415 us; the launch traced here: 414 us
  waiting for transfers between devices  236 us (57%)
  matrix products  86.9 us (21%)
  starting transfers between devices  40.9 us (10%)
  local copies, waits for them, and re-layouts  31.2 us (8%)
  other arithmetic  17.6 us (4%)
    ppermute x36, waiting for transfers between devices, swap(): return lax.ppermute(block, axis, [(i, i ^ bit) for i in range(size)])  181 us
    dot_general x6, matrix products, contract_last(): lax.dot_general(left, right, (((1,), (1,)), ((), ())), preferred_element_...  76.7 us
    ppermute x6, waiting for transfers between devices, broadcast(): arrived = lax.ppermute(slab, ('row', 'col'), pairs)  54.8 us
    ppermute x36, starting transfers between devices, swap(): return lax.ppermute(block, axis, [(i, i ^ bit) for i in range(size)])  30.5 us
    unnamed x48, local copies, waits for them, and re-layouts  19.9 us
    ppermute x6, starting transfers between devices, broadcast(): arrived = lax.ppermute(slab, ('row', 'col'), pairs)  10.4 us
    dot_general x1, matrix products, shards(): lax.dot_general(jnp.concatenate(slabs, axis=0), jnp.concatenate(gates, ax...  10.3 us
  transfers between devices with their start and end apart: 42, of which 23 were waited for; matrix products, arithmetic and copies ran while one was open for 25% of the time, Pallas kernels for 0%

profile of v2, /device:TPU:0, one launch (start us, length us, event | category | flops | bytes accessed | tf_op | source)
XLA Modules:
  0.0 413.8 jit_solution(12003274347547916847)
XLA Ops:
  0.6 2.0 fusion.48
  2.6 2.9 collective-permute-start.18
  5.5 1.6 collective-permute-start.19
  7.1 2.6 collective-permute-start.21
  10.7 1.9 collective-permute-done.18
  12.6 3.5 collective-permute-start.3
  16.0 5.0 %collective-permute-done.19 = bf16[64,2048]{1,0:T(8,128)(2,1)S(1)} collective-permute-done((bf16[64,2048]{1,0:T(8,128)(2,1)}, bf16[64,2048]{1,0:T(8,128)(2,1)S(1)}, u32[]{:S(2)}, u32[]{:S(2)}) %collective-permute-start.19) | collective-permute-done | bytes 262176 | tf_op jit(solution)/shard_map/ppermute | solution.py:17
  21.1 1.3 collective-permute-done.21
  25.2 6.6 %collective-permute-done.1 = bf16[64,2048]{1,0:T(8,128)(2,1)S(1)} collective-permute-done((bf16[64,2048]{1,0:T(8,128)(2,1)}, bf16[64,2048]{1,0:T(8,128)(2,1)S(1)}, u32[]{:S(2)}, u32[]{:S(2)}) %collective-permute-start.1) | collective-permute-done | bytes 262176 | tf_op jit(solution)/shard_map/ppermute | solution.py:17
  31.9 2.6 collective-permute-start.5
  35.2 2.3 collective-permute-done.23
  37.5 4.1 collective-permute-done.5
  44.9 1.8 collective-permute-done.4
  46.7 4.4 %collective-permute-done.24 = bf16[64,2048]{1,0:T(8,128)(2,1)S(1)} collective-permute-done((bf16[64,2048]{1,0:T(8,128)(2,1)S(1)}, bf16[64,2048]{1,0:T(8,128)(2,1)S(1)}, u32[]{:S(2)}, u32[]{:S(2)}) %collective-permute-start.24) | collective-permute-done | bytes 262176 | tf_op jit(solution)/shard_map/ppermute | solution.py:17
  51.9 2.1 collective-permute-done.6
  54.0 1.7 dynamic-slice_dynamic-update-slice_fusion.7
  56.8 11.3 %fusion.50 = f32[512,3584]{1,0:T(8,128)S(1)} fusion(bf16[512,2048]{1,0:T(8,128)(2,1)S(1)} %dynamic-slice_dynamic-update-slice_fusion, bf16[3584,2048]{1,0:T(8,128)(2,1)} %param.11), kind=kOutput, calls=%fused_computation.138 | convolution fusion | flops 7516192768 | bytes 24117248 | tf_op jit(solution)/shard_map/dot_general | solution.py:11
  68.1 1.5 slice.214
  74.7 11.9 %fusion.49 = f32[512,3584]{1,0:T(8,128)S(1)} fusion(bf16[512,2048]{1,0:T(8,128)(2,1)} %dynamic-slice_dynamic-update-slice_fusion.8, bf16[3584,2048]{1,0:T(8,128)(2,1)} %param.11), kind=kOutput, calls=%fused_computation.137 | convolution fusion | flops 7516192768 | bytes 24117248 | tf_op jit(solution)/shard_map/dot_general | solution.py:11
  87.4 2.1 copy-done.4
  89.5 1.8 copy-done.5
  91.6 1.4 fusion.34
  93.0 1.6 collective-permute-start.26
  95.3 20.8 %collective-permute-done.26 = bf16[128,3584]{1,0:T(8,128)(2,1)S(1)} collective-permute-done((bf16[128,3584]{1,0:T(8,128)(2,1)S(1)}, bf16[128,3584]{1,0:T(8,128)(2,1)S(1)}, u32[]{:S(2)}, u32[]{:S(2)}) %collective-permute-start.26) | collective-permute-done | bytes 917536 | tf_op jit(solution)/shard_map/ppermute | solution.py:17
  116.2 3.4 fusion.31
  119.6 1.5 collective-permute-start.31
  121.1 14.7 %collective-permute-done.8 = bf16[128,3584]{1,0:T(8,128)(2,1)S(1)} collective-permute-done((bf16[128,3584]{1,0:T(8,128)(2,1)S(1)}, bf16[128,3584]{1,0:T(8,128)(2,1)S(1)}, u32[]{:S(2)}, u32[]{:S(2)}) %collective-permute-start.8) | collective-permute-done | bytes 917536 | tf_op jit(solution)/shard_map/ppermute | solution.py:17
  135.9 3.7 fusion.22
  140.1 1.5 collective-permute-start.10
  142.2 13.5 %collective-permute-done.31 = bf16[128,3584]{1,0:T(8,128)(2,1)} collective-permute-done((bf16[128,3584]{1,0:T(8,128)(2,1)}, bf16[128,3584]{1,0:T(8,128)(2,1)}, u32[]{:S(2)}, u32[]{:S(2)}) %collective-permute-start.31) | collective-permute-done | bytes 917536 | tf_op jit(solution)/shard_map/ppermute | solution.py:17
  155.6 1.5 collective-permute-start.13
  157.2 18.0 %collective-permute-done.10 = bf16[128,3584]{1,0:T(8,128)(2,1)S(1)} collective-permute-done((bf16[128,3584]{1,0:T(8,128)(2,1)S(1)}, bf16[128,3584]{1,0:T(8,128)(2,1)S(1)}, u32[]{:S(2)}, u32[]{:S(2)}) %collective-permute-start.10) | collective-permute-done | bytes 917536 | tf_op jit(solution)/shard_map/ppermute | solution.py:17
  175.8 19.0 %collective-permute-done.28 = bf16[128,3584]{1,0:T(8,128)(2,1)S(1)} collective-permute-done((bf16[128,3584]{1,0:T(8,128)(2,1)S(1)}, bf16[128,3584]{1,0:T(8,128)(2,1)S(1)}, u32[]{:S(2)}, u32[]{:S(2)}) %collective-permute-start.28) | collective-permute-done | bytes 917536 | tf_op jit(solution)/shard_map/ppermute | solution.py:17
  194.8 19.4 %collective-permute-done.13 = bf16[128,3584]{1,0:T(8,128)(2,1)} collective-permute-done((bf16[128,3584]{1,0:T(8,128)(2,1)}, bf16[128,3584]{1,0:T(8,128)(2,1)}, u32[]{:S(2)}, u32[]{:S(2)}) %collective-permute-start.13) | collective-permute-done | bytes 917536 | tf_op jit(solution)/shard_map/ppermute | solution.py:17
  214.7 13.0 %fusion.8 = f32[512,2048]{1,0:T(8,128)} fusion(bf16[2048,3584]{1,0:T(8,128)(2,1)} %param.10, bf16[128,3584]{1,0:T(8,128)(2,1)S(1)} %collective-permute-done.32, bf16[128,3584]{1,0:T(8,128)(2,1)} %collective-permute-done.31, bf16[128,3584]{1,0:T(8,128)(2,1)S(1)} %collective-permute-done.30, bf16[128,3584]{1,0:T(8,128)(2,1)} %get-tuple-element.5), kind=kOutput, calls=%fused_computation.13 | convolution fusion | flops 7530872832 | bytes 22544384 | tf_op jit(solution)/shard_map/dot_general | solution.py:11
  227.8 13.4 %convolution_add_fusion = f32[512,2048]{1,0:T(8,128)} fusion(f32[512,2048]{1,0:T(8,128)} %fusion.8, bf16[2048,3584]{1,0:T(8,128)(2,1)} %param.9, bf16[128,3584]{1,0:T(8,128)(2,1)} %collective-permute-done.29, bf16[128,3584]{1,0:T(8,128)(2,1)S(1)} %collective-permute-done.28, bf16[128,3584]{1,0:T(8,128)(2,1)S(1)} %collective-permute-done.27, ...), kind=kOutput, calls=%fused_computation.21 | convolution fusion | flops 7531921408 | bytes 26738688 | tf_op jit(solution)/shard_map/dot_general | solution.py:11
  241.1 1.7 dynamic-slice_convert_fusion.3
  243.7 13.7 %fusion = f32[512,2048]{1,0:T(8,128)} fusion(bf16[2048,3584]{1,0:T(8,128)(2,1)} %param.10, bf16[128,3584]{1,0:T(8,128)(2,1)} %collective-permute-done.14, bf16[128,3584]{1,0:T(8,128)(2,1)} %collective-permute-done.13, bf16[128,3584]{1,0:T(8,128)(2,1)} %collective-permute-done.12, bf16[128,3584]{1,0:T(8,128)(2,1)} %get-tuple-element.3), kind=kOutput, calls=%fused_computation.4 | convolution fusion | flops 7530872832 | bytes 22544384 | tf_op jit(solution)/shard_map/dot_general | solution.py:11
  257.4 13.5 %convolution_add_fusion.1 = f32[512,2048]{1,0:T(8,128)} fusion(f32[512,2048]{1,0:T(8,128)} %fusion, bf16[2048,3584]{1,0:T(8,128)(2,1)} %param.9, bf16[128,3584]{1,0:T(8,128)(2,1)} %collective-permute-done.11, bf16[128,3584]{1,0:T(8,128)(2,1)S(1)} %collective-permute-done.10, bf16[128,3584]{1,0:T(8,128)(2,1)S(1)} %collective-permute-done.9, ...), kind=kOutput, calls=%fused_computation.22 | convolution fusion | flops 7531921408 | bytes 26738688 | tf_op jit(solution)/shard_map/dot_general | solution.py:11
  270.8 1.7 dynamic-slice_convert_fusion.7
  272.6 1.4 collective-permute-start.15
  274.0 2.2 constant_dynamic-update-slice_fusion.20
  277.1 1.3 pad_maximum_fusion.1
  279.0 3.7 collective-permute-start.39
  282.7 1.5 pad_maximum_fusion
  284.7 1.3 collective-permute-start.36
  286.2 1.4 constant_dynamic-update-slice_fusion.16
  288.7 14.7 %collective-permute-done.39 = bf16[512,896]{1,0:T(8,128)(2,1)S(1)} collective-permute-done((bf16[512,896]{1,0:T(8,128)(2,1)S(1)}, bf16[512,896]{1,0:T(8,128)(2,1)S(1)}, u32[]{:S(2)}, u32[]{:S(2)}) %collective-permute-start.39) | collective-permute-done | bytes 917536 | tf_op jit(solution)/shard_map/ppermute | solution.py:92
  303.9 1.3 collective-permute-start.40
  305.3 1.2 fusion.42
  306.7 2.1 collective-permute-start.16
  308.8 14.3 %collective-permute-done.36 = bf16[512,896]{1,0:T(8,128)(2,1)S(1)} collective-permute-done((bf16[512,896]{1,0:T(8,128)(2,1)S(1)}, bf16[512,896]{1,0:T(8,128)(2,1)S(1)}, u32[]{:S(2)}, u32[]{:S(2)}) %collective-permute-start.36) | collective-permute-done | bytes 917536 | tf_op jit(solution)/shard_map/ppermute | solution.py:92
  323.6 1.3 collective-permute-start.37
  324.9 29.0 %collective-permute-done.34 = bf16[128,2048]{1,0:T(8,128)(2,1)S(1)} collective-permute-done((bf16[128,2048]{1,0:T(8,128)(2,1)S(1)}, bf16[128,2048]{1,0:T(8,128)(2,1)S(1)}, u32[]{:S(2)}, u32[]{:S(2)}) %collective-permute-start.34) | collective-permute-done | bytes 524320 | tf_op jit(solution)/shard_map/ppermute | solution.py:17
  353.9 1.0 add_convert_fusion.1
  355.1 10.1 %collective-permute-done.16 = bf16[128,2048]{1,0:T(8,128)(2,1)S(1)} collective-permute-done((bf16[128,2048]{1,0:T(8,128)(2,1)S(1)}, bf16[128,2048]{1,0:T(8,128)(2,1)S(1)}, u32[]{:S(2)}, u32[]{:S(2)}) %collective-permute-start.16) | collective-permute-done | bytes 524320 | tf_op jit(solution)/shard_map/ppermute | solution.py:17
  365.5 1.3 collective-permute-start.41
  366.8 18.0 %collective-permute-done.37 = bf16[512,896]{1,0:T(8,128)(2,1)S(1)} collective-permute-done((bf16[512,896]{1,0:T(8,128)(2,1)S(1)}, bf16[512,896]{1,0:T(8,128)(2,1)S(1)}, u32[]{:S(2)}, u32[]{:S(2)}) %collective-permute-start.37) | collective-permute-done | bytes 917536 | tf_op jit(solution)/shard_map/ppermute | solution.py:92
  384.9 1.3 collective-permute-start.38
  386.3 4.2 %collective-permute-done.35 = bf16[64,2048]{1,0:T(8,128)(2,1)S(1)} collective-permute-done((bf16[64,2048]{1,0:T(8,128)(2,1)S(1)}, bf16[64,2048]{1,0:T(8,128)(2,1)S(1)}, u32[]{:S(2)}, u32[]{:S(2)}) %collective-permute-start.35) | collective-permute-done | bytes 262176 | tf_op jit(solution)/shard_map/ppermute | solution.py:17
  390.5 1.1 add_convert_fusion
  391.5 3.0 collective-permute-done.17
  395.6 7.8 %collective-permute-done.38 = bf16[512,896]{1,0:T(8,128)(2,1)S(1)} collective-permute-done((bf16[512,896]{1,0:T(8,128)(2,1)S(1)}, bf16[512,896]{1,0:T(8,128)(2,1)S(1)}, u32[]{:S(2)}, u32[]{:S(2)}) %collective-permute-start.38) | collective-permute-done | bytes 917536 | tf_op jit(solution)/shard_map/ppermute | solution.py:92
  403.6 10.3 %convolution_multiply_fusion = f32[896,3584]{1,0:T(8,128)} fusion(bf16[1024,3584]{1,0:T(8,128)(2,1)S(1)} %constant_dynamic-update-slice_fusion.16, bf16[512,896]{1,0:T(8,128)(2,1)S(1)} %broadcast_select_fusion.4, bf16[512,896]{1,0:T(8,128)(2,1)S(1)} %broadcast_select_fusion.5), kind=kOutput, calls=%fused_computation | convolution fusion | flops 6583549952 | bytes 22020096 | tf_op jit(solution)/shard_map/dot_general | solution.py:134
  (111 shorter events, 26.3 us)
Async XLA Ops:
  2.6 10.0 %collective-permute-start.18 = (bf16[64,2048]{1,0:T(8,128)(2,1)}, bf16[64,2048]{1,0:T(8,128)(2,1)S(1)}, u32[]{:S(2)}, u32[]{:S(2)}) collective-permute-start(bf16[64,2048]{1,0:T(8,128)(2,1)} %get-tuple-element.25), channel_id=1, source_target_pairs={{0,1},{1,0},{2,3},{3,2},{4,5},{5,4},{6,7},{7,6},{8,9},{9,8},{10,11... | collective-permute-start | bytes 786440 | tf_op jit(solution)/shard_map/ppermute | solution.py:17
  5.5 15.5 %collective-permute-start.19 = (bf16[64,2048]{1,0:T(8,128)(2,1)}, bf16[64,2048]{1,0:T(8,128)(2,1)S(1)}, u32[]{:S(2)}, u32[]{:S(2)}) collective-permute-start(bf16[64,2048]{1,0:T(8,128)(2,1)} %get-tuple-element.25), channel_id=1, source_target_pairs={{0,2},{1,3},{2,0},{3,1},{4,6},{5,7},{6,4},{7,5},{8,10},{9,11},{10,... | collective-permute-start | bytes 786440 | tf_op jit(solution)/shard_map/ppermute | solution.py:17
  7.1 15.3 %collective-permute-start.21 = (bf16[64,2048]{1,0:T(8,128)(2,1)}, bf16[64,2048]{1,0:T(8,128)(2,1)S(1)}, u32[]{:S(2)}, u32[]{:S(2)}) collective-permute-start(bf16[64,2048]{1,0:T(8,128)(2,1)} %get-tuple-element.25), channel_id=1, source_target_pairs={{0,4},{1,5},{2,6},{3,7},{4,0},{5,1},{6,2},{7,3},{8,12},{9,13},{10,... | collective-permute-start | bytes 786440 | tf_op jit(solution)/shard_map/ppermute | solution.py:17
  9.7 14.8 %collective-permute-start = (bf16[64,2048]{1,0:T(8,128)(2,1)}, bf16[64,2048]{1,0:T(8,128)(2,1)S(1)}, u32[]{:S(2)}, u32[]{:S(2)}) collective-permute-start(bf16[64,2048]{1,0:T(8,128)(2,1)} %get-tuple-element.22), channel_id=1, source_target_pairs={{0,1},{1,0},{2,3},{3,2},{4,5},{5,4},{6,7},{7,6},{8,9},{9,8},{10,11... | collective-permute-start | bytes 786440 | tf_op jit(solution)/shard_map/ppermute | solution.py:17
  10.2 21.6 %collective-permute-start.1 = (bf16[64,2048]{1,0:T(8,128)(2,1)}, bf16[64,2048]{1,0:T(8,128)(2,1)S(1)}, u32[]{:S(2)}, u32[]{:S(2)}) collective-permute-start(bf16[64,2048]{1,0:T(8,128)(2,1)} %get-tuple-element.22), channel_id=1, source_target_pairs={{0,2},{1,3},{2,0},{3,1},{4,6},{5,7},{6,4},{7,5},{8,10},{9,11},{10,... | collective-permute-start | bytes 786440 | tf_op jit(solution)/shard_map/ppermute | solution.py:17
  12.6 19.3 %collective-permute-start.3 = (bf16[64,2048]{1,0:T(8,128)(2,1)}, bf16[64,2048]{1,0:T(8,128)(2,1)S(1)}, u32[]{:S(2)}, u32[]{:S(2)}) collective-permute-start(bf16[64,2048]{1,0:T(8,128)(2,1)} %get-tuple-element.22), channel_id=1, source_target_pairs={{0,4},{1,5},{2,6},{3,7},{4,0},{5,1},{6,2},{7,3},{8,12},{9,13},{10,... | collective-permute-start | bytes 786440 | tf_op jit(solution)/shard_map/ppermute | solution.py:17
  21.1 13.5 %collective-permute-start.20 = (bf16[64,2048]{1,0:T(8,128)(2,1)S(1)}, bf16[64,2048]{1,0:T(8,128)(2,1)S(1)}, u32[]{:S(2)}, u32[]{:S(2)}) collective-permute-start(bf16[64,2048]{1,0:T(8,128)(2,1)S(1)} %collective-permute-done.19), channel_id=1, source_target_pairs={{0,1},{1,0},{2,3},{3,2},{4,5},{5,4},{6,7},{7,6},{8,9},{9,8},{10,11... | collective-permute-start | bytes 786440 | tf_op jit(solution)/shard_map/ppermute | solution.py:17
  22.4 21.0 %collective-permute-start.22 = (bf16[64,2048]{1,0:T(8,128)(2,1)S(1)}, bf16[64,2048]{1,0:T(8,128)(2,1)S(1)}, u32[]{:S(2)}, u32[]{:S(2)}) collective-permute-start(bf16[64,2048]{1,0:T(8,128)(2,1)S(1)} %collective-permute-done.21), channel_id=1, source_target_pairs={{0,1},{1,0},{2,3},{3,2},{4,5},{5,4},{6,7},{7,6},{8,9},{9,8},{10,11... | collective-permute-start | bytes 786440 | tf_op jit(solution)/shard_map/ppermute | solution.py:17
  24.5 12.9 %collective-permute-start.23 = (bf16[64,2048]{1,0:T(8,128)(2,1)S(1)}, bf16[64,2048]{1,0:T(8,128)(2,1)S(1)}, u32[]{:S(2)}, u32[]{:S(2)}) collective-permute-start(bf16[64,2048]{1,0:T(8,128)(2,1)S(1)} %collective-permute-done.21), channel_id=1, source_target_pairs={{0,2},{1,3},{2,0},{3,1},{4,6},{5,7},{6,4},{7,5},{8,10},{9,11},{10,... | collective-permute-start | bytes 786440 | tf_op jit(solution)/shard_map/ppermute | solution.py:17
  31.8 13.1 %collective-permute-start.2 = (bf16[64,2048]{1,0:T(8,128)(2,1)S(1)}, bf16[64,2048]{1,0:T(8,128)(2,1)S(1)}, u32[]{:S(2)}, u32[]{:S(2)}) collective-permute-start(bf16[64,2048]{1,0:T(8,128)(2,1)S(1)} %collective-permute-done.1), channel_id=1, source_target_pairs={{0,1},{1,0},{2,3},{3,2},{4,5},{5,4},{6,7},{7,6},{8,9},{9,8},{10,11... | collective-permute-start | bytes 786440 | tf_op jit(solution)/shard_map/ppermute | solution.py:17
  31.9 9.7 %collective-permute-start.5 = (bf16[64,2048]{1,0:T(8,128)(2,1)S(1)}, bf16[64,2048]{1,0:T(8,128)(2,1)S(1)}, u32[]{:S(2)}, u32[]{:S(2)}) collective-permute-start(bf16[64,2048]{1,0:T(8,128)(2,1)S(1)} %collective-permute-done.3), channel_id=1, source_target_pairs={{0,2},{1,3},{2,0},{3,1},{4,6},{5,7},{6,4},{7,5},{8,10},{9,11},{10,... | collective-permute-start | bytes 786440 | tf_op jit(solution)/shard_map/ppermute | solution.py:17
  34.6 12.1 %collective-permute-start.4 = (bf16[64,2048]{1,0:T(8,128)(2,1)S(1)}, bf16[64,2048]{1,0:T(8,128)(2,1)S(1)}, u32[]{:S(2)}, u32[]{:S(2)}) collective-permute-start(bf16[64,2048]{1,0:T(8,128)(2,1)S(1)} %collective-permute-done.3), channel_id=1, source_target_pairs={{0,1},{1,0},{2,3},{3,2},{4,5},{5,4},{6,7},{7,6},{8,9},{9,8},{10,11... | collective-permute-start | bytes 786440 | tf_op jit(solution)/shard_map/ppermute | solution.py:17
  37.4 13.7 %collective-permute-start.24 = (bf16[64,2048]{1,0:T(8,128)(2,1)S(1)}, bf16[64,2048]{1,0:T(8,128)(2,1)S(1)}, u32[]{:S(2)}, u32[]{:S(2)}) collective-permute-start(bf16[64,2048]{1,0:T(8,128)(2,1)S(1)} %collective-permute-done.23), channel_id=1, source_target_pairs={{0,1},{1,0},{2,3},{3,2},{4,5},{5,4},{6,7},{7,6},{8,9},{9,8},{10,11... | collective-permute-start | bytes 786440 | tf_op jit(solution)/shard_map/ppermute | solution.py:17
  41.6 12.3 %collective-permute-start.6 = (bf16[64,2048]{1,0:T(8,128)(2,1)S(1)}, bf16[64,2048]{1,0:T(8,128)(2,1)S(1)}, u32[]{:S(2)}, u32[]{:S(2)}) collective-permute-start(bf16[64,2048]{1,0:T(8,128)(2,1)S(1)} %collective-permute-done.5), channel_id=1, source_target_pairs={{0,1},{1,0},{2,3},{3,2},{4,5},{5,4},{6,7},{7,6},{8,9},{9,8},{10,11... | collective-permute-start | bytes 786440 | tf_op jit(solution)/shard_map/ppermute | solution.py:17
  51.8 4.8 %copy-start.1 = (bf16[512,2048]{1,0:T(8,128)(2,1)S(1)}, bf16[512,2048]{1,0:T(8,128)(2,1)}, u32[]{:S(2)}) copy-start(bf16[512,2048]{1,0:T(8,128)(2,1)} %constant_dynamic-update-slice_fusion.8) | copy-start | bytes 6291460
  69.6 22.0 %collective-permute-start.25 = (bf16[256,3584]{1,0:T(8,128)(2,1)}, bf16[256,3584]{1,0:T(8,128)(2,1)}, u32[]{:S(2)}, u32[]{:S(2)}) collective-permute-start(bf16[256,3584]{1,0:T(8,128)(2,1)} %slice.214), channel_id=1, source_target_pairs={{0,8},{8,0},{16,24},{24,16},{1,9},{9,1},{17,25},{25,17},{2,10},{10... | collective-permute-start | bytes 5505032 | tf_op jit(solution)/shard_map/ppermute | solution.py:17
  86.6 8.0 %copy-start = (f32[512,3584]{1,0:T(8,128)}, f32[512,3584]{1,0:T(8,128)S(1)}, u32[]{:S(2)}) copy-start(f32[512,3584]{1,0:T(8,128)S(1)} %fusion.49) | copy-start | bytes 22020100
  86.6 2.9 copy-start.4
  86.6 4.7 %copy-start.5 = (bf16[256,3584]{1,0:T(8,128)(2,1)S(1)}, bf16[256,3584]{1,0:T(8,128)(2,1)}, u32[]{:S(2)}) copy-start(bf16[256,3584]{1,0:T(8,128)(2,1)} %param.7) | copy-start | bytes 5505028
  86.8 7.8 %collective-permute-start.7 = (bf16[256,3584]{1,0:T(8,128)(2,1)S(1)}, bf16[256,3584]{1,0:T(8,128)(2,1)S(1)}, u32[]{:S(2)}, u32[]{:S(2)}) collective-permute-start(bf16[256,3584]{1,0:T(8,128)(2,1)S(1)} %slice.215), channel_id=1, source_target_pairs={{0,8},{8,0},{16,24},{24,16},{1,9},{9,1},{17,25},{25,17},{2,10},{10... | collective-permute-start | bytes 5505032 | tf_op jit(solution)/shard_map/ppermute | solution.py:17
  93.0 23.2 %collective-permute-start.26 = (bf16[128,3584]{1,0:T(8,128)(2,1)S(1)}, bf16[128,3584]{1,0:T(8,128)(2,1)S(1)}, u32[]{:S(2)}, u32[]{:S(2)}) collective-permute-start(bf16[128,3584]{1,0:T(8,128)(2,1)S(1)} %fusion.34), channel_id=1, source_target_pairs={{0,16},{8,24},{16,0},{24,8},{1,17},{9,25},{17,1},{25,9},{2,18},{10... | collective-permute-start | bytes 2752520 | tf_op jit(solution)/shard_map/ppermute | solution.py:17
  94.8 41.1 %collective-permute-start.8 = (bf16[128,3584]{1,0:T(8,128)(2,1)S(1)}, bf16[128,3584]{1,0:T(8,128)(2,1)S(1)}, u32[]{:S(2)}, u32[]{:S(2)}) collective-permute-start(bf16[128,3584]{1,0:T(8,128)(2,1)S(1)} %fusion.36), channel_id=1, source_target_pairs={{0,16},{8,24},{16,0},{24,8},{1,17},{9,25},{17,1},{25,9},{2,18},{10... | collective-permute-start | bytes 2752520 | tf_op jit(solution)/shard_map/ppermute | solution.py:17
  119.6 36.0 %collective-permute-start.31 = (bf16[128,3584]{1,0:T(8,128)(2,1)}, bf16[128,3584]{1,0:T(8,128)(2,1)}, u32[]{:S(2)}, u32[]{:S(2)}) collective-permute-start(bf16[128,3584]{1,0:T(8,128)(2,1)} %get-tuple-element.5), channel_id=1, source_target_pairs={{0,16},{8,24},{16,0},{24,8},{1,17},{9,25},{17,1},{25,9},{2,18},{10... | collective-permute-start | bytes 2752520 | tf_op jit(solution)/shard_map/ppermute | solution.py:17
  139.6 17.6 %collective-permute-start.9 = (bf16[128,3584]{1,0:T(8,128)(2,1)S(1)}, bf16[128,3584]{1,0:T(8,128)(2,1)S(1)}, u32[]{:S(2)}, u32[]{:S(2)}) collective-permute-start(bf16[128,3584]{1,0:T(8,128)(2,1)S(1)} %get-tuple-element.2), channel_id=1, source_target_pairs={{0,8},{8,0},{16,24},{24,16},{1,9},{9,1},{17,25},{25,17},{2,10},{10... | collective-permute-start | bytes 2752520 | tf_op jit(solution)/shard_map/ppermute | solution.py:17
  139.6 35.7 %collective-permute-start.30 = (bf16[128,3584]{1,0:T(8,128)(2,1)}, bf16[128,3584]{1,0:T(8,128)(2,1)S(1)}, u32[]{:S(2)}, u32[]{:S(2)}) collective-permute-start(bf16[128,3584]{1,0:T(8,128)(2,1)} %get-tuple-element.5), channel_id=1, source_target_pairs={{0,8},{8,0},{16,24},{24,16},{1,9},{9,1},{17,25},{25,17},{2,10},{10... | collective-permute-start | bytes 2752520 | tf_op jit(solution)/shard_map/ppermute | solution.py:17
  140.1 35.1 %collective-permute-start.10 = (bf16[128,3584]{1,0:T(8,128)(2,1)S(1)}, bf16[128,3584]{1,0:T(8,128)(2,1)S(1)}, u32[]{:S(2)}, u32[]{:S(2)}) collective-permute-start(bf16[128,3584]{1,0:T(8,128)(2,1)S(1)} %get-tuple-element.2), channel_id=1, source_target_pairs={{0,16},{8,24},{16,0},{24,8},{1,17},{9,25},{17,1},{25,9},{2,18},{10... | collective-permute-start | bytes 2752520 | tf_op jit(solution)/shard_map/ppermute | solution.py:17
  141.6 53.3 %collective-permute-start.28 = (bf16[128,3584]{1,0:T(8,128)(2,1)S(1)}, bf16[128,3584]{1,0:T(8,128)(2,1)S(1)}, u32[]{:S(2)}, u32[]{:S(2)}) collective-permute-start(bf16[128,3584]{1,0:T(8,128)(2,1)S(1)} %get-tuple-element.4), channel_id=1, source_target_pairs={{0,16},{8,24},{16,0},{24,8},{1,17},{9,25},{17,1},{25,9},{2,18},{10... | collective-permute-start | bytes 2752520 | tf_op jit(solution)/shard_map/ppermute | solution.py:17
  155.6 58.6 %collective-permute-start.13 = (bf16[128,3584]{1,0:T(8,128)(2,1)}, bf16[128,3584]{1,0:T(8,128)(2,1)}, u32[]{:S(2)}, u32[]{:S(2)}) collective-permute-start(bf16[128,3584]{1,0:T(8,128)(2,1)} %get-tuple-element.3), channel_id=1, source_target_pairs={{0,16},{8,24},{16,0},{24,8},{1,17},{9,25},{17,1},{25,9},{2,18},{10... | collective-permute-start | bytes 2752520 | tf_op jit(solution)/shard_map/ppermute | solution.py:17
  157.1 57.1 %collective-permute-start.32 = (bf16[128,3584]{1,0:T(8,128)(2,1)}, bf16[128,3584]{1,0:T(8,128)(2,1)S(1)}, u32[]{:S(2)}, u32[]{:S(2)}) collective-permute-start(bf16[128,3584]{1,0:T(8,128)(2,1)} %collective-permute-done.31), channel_id=1, source_target_pairs={{0,8},{8,0},{16,24},{24,16},{1,9},{9,1},{17,25},{25,17},{2,10},{10... | collective-permute-start | bytes 2752520 | tf_op jit(solution)/shard_map/ppermute | solution.py:17
  175.2 52.6 %collective-permute-start.27 = (bf16[128,3584]{1,0:T(8,128)(2,1)S(1)}, bf16[128,3584]{1,0:T(8,128)(2,1)S(1)}, u32[]{:S(2)}, u32[]{:S(2)}) collective-permute-start(bf16[128,3584]{1,0:T(8,128)(2,1)S(1)} %get-tuple-element.4), channel_id=1, source_target_pairs={{0,8},{8,0},{16,24},{24,16},{1,9},{9,1},{17,25},{25,17},{2,10},{10... | collective-permute-start | bytes 2752520 | tf_op jit(solution)/shard_map/ppermute | solution.py:17
  175.2 19.6 %copy-start.6 = (bf16[1024,3584]{1,0:T(8,128)(2,1)}, bf16[1024,3584]{1,0:T(8,128)(2,1)S(1)}, u32[]{:S(2)}) copy-start(bf16[1024,3584]{1,0:T(8,128)(2,1)S(1)} %constant_dynamic-update-slice_fusion.21) | copy-start | bytes 22020100
  175.3 68.4 %collective-permute-start.12 = (bf16[128,3584]{1,0:T(8,128)(2,1)}, bf16[128,3584]{1,0:T(8,128)(2,1)}, u32[]{:S(2)}, u32[]{:S(2)}) collective-permute-start(bf16[128,3584]{1,0:T(8,128)(2,1)} %get-tuple-element.3), channel_id=1, source_target_pairs={{0,8},{8,0},{16,24},{24,16},{1,9},{9,1},{17,25},{25,17},{2,10},{10... | collective-permute-start | bytes 2752520 | tf_op jit(solution)/shard_map/ppermute | solution.py:17
  194.8 62.5 %collective-permute-start.11 = (bf16[128,3584]{1,0:T(8,128)(2,1)S(1)}, bf16[128,3584]{1,0:T(8,128)(2,1)}, u32[]{:S(2)}, u32[]{:S(2)}) collective-permute-start(bf16[128,3584]{1,0:T(8,128)(2,1)S(1)} %collective-permute-done.10), channel_id=1, source_target_pairs={{0,8},{8,0},{16,24},{24,16},{1,9},{9,1},{17,25},{25,17},{2,10},{10... | collective-permute-start | bytes 2752520 | tf_op jit(solution)/shard_map/ppermute | solution.py:17
  214.2 13.5 %collective-permute-start.29 = (bf16[128,3584]{1,0:T(8,128)(2,1)S(1)}, bf16[128,3584]{1,0:T(8,128)(2,1)}, u32[]{:S(2)}, u32[]{:S(2)}) collective-permute-start(bf16[128,3584]{1,0:T(8,128)(2,1)S(1)} %collective-permute-done.28), channel_id=1, source_target_pairs={{0,8},{8,0},{16,24},{24,16},{1,9},{9,1},{17,25},{25,17},{2,10},{10... | collective-permute-start | bytes 2752520 | tf_op jit(solution)/shard_map/ppermute | solution.py:17
  214.2 29.4 %collective-permute-start.14 = (bf16[128,3584]{1,0:T(8,128)(2,1)}, bf16[128,3584]{1,0:T(8,128)(2,1)}, u32[]{:S(2)}, u32[]{:S(2)}) collective-permute-start(bf16[128,3584]{1,0:T(8,128)(2,1)} %collective-permute-done.13), channel_id=1, source_target_pairs={{0,8},{8,0},{16,24},{24,16},{1,9},{9,1},{17,25},{25,17},{2,10},{10... | collective-permute-start | bytes 2752520 | tf_op jit(solution)/shard_map/ppermute | solution.py:17
  242.9 62.4 %collective-permute-start.33 = (bf16[256,2048]{1,0:T(8,128)(2,1)S(1)}, bf16[256,2048]{1,0:T(8,128)(2,1)}, u32[]{:S(2)}, u32[]{:S(2)}) collective-permute-start(bf16[256,2048]{1,0:T(8,128)(2,1)S(1)} %pad_maximum_fusion.3), channel_id=1, source_target_pairs={{0,1},{1,0},{2,3},{3,2},{4,5},{5,4},{6,7},{7,6},{8,9},{9,8},{10,11... | collective-permute-start | bytes 3145736 | tf_op jit(solution)/shard_map/ppermute | solution.py:17
  272.6 33.9 %collective-permute-start.15 = (bf16[256,2048]{1,0:T(8,128)(2,1)S(1)}, bf16[256,2048]{1,0:T(8,128)(2,1)S(1)}, u32[]{:S(2)}, u32[]{:S(2)}) collective-permute-start(bf16[256,2048]{1,0:T(8,128)(2,1)S(1)} %pad_maximum_fusion.2), channel_id=1, source_target_pairs={{0,1},{1,0},{2,3},{3,2},{4,5},{5,4},{6,7},{7,6},{8,9},{9,8},{10,11... | collective-permute-start | bytes 3145736 | tf_op jit(solution)/shard_map/ppermute | solution.py:17
  278.4 7.6 %copy-start.7 = (bf16[1024,3584]{1,0:T(8,128)(2,1)S(1)}, bf16[1024,3584]{1,0:T(8,128)(2,1)}, u32[]{:S(2)}) copy-start(bf16[1024,3584]{1,0:T(8,128)(2,1)} %constant_dynamic-update-slice_fusion.19) | copy-start | bytes 22020100
  279.0 24.4 %collective-permute-start.39 = (bf16[512,896]{1,0:T(8,128)(2,1)S(1)}, bf16[512,896]{1,0:T(8,128)(2,1)S(1)}, u32[]{:S(2)}, u32[]{:S(2)}) collective-permute-start(bf16[512,896]{1,0:T(8,128)(2,1)S(1)} %constant_dynamic-slice_fusion), channel_id=1, source_target_pairs={{0,4},{8,12},{16,20},{24,28}} | collective-permute-start | bytes 2752520 | tf_op jit(solution)/shard_map/ppermute | solution.py:92
  282.6 6.0 %copy-start.3 = (f32[512,2048]{1,0:T(8,128)S(1)}, f32[512,2048]{1,0:T(8,128)}, u32[]{:S(2)}) copy-start(f32[512,2048]{1,0:T(8,128)} %convolution_add_fusion.1) | copy-start | bytes 12582916
  284.7 38.4 %collective-permute-start.36 = (bf16[512,896]{1,0:T(8,128)(2,1)S(1)}, bf16[512,896]{1,0:T(8,128)(2,1)S(1)}, u32[]{:S(2)}, u32[]{:S(2)}) collective-permute-start(bf16[512,896]{1,0:T(8,128)(2,1)S(1)} %constant_dynamic-slice_fusion.1), channel_id=1, source_target_pairs={{0,4},{8,12},{16,20},{24,28}} | collective-permute-start | bytes 2752520 | tf_op jit(solution)/shard_map/ppermute | solution.py:92
  286.0 2.5 copy-start.2
  303.9 61.4 %collective-permute-start.40 = (bf16[512,896]{1,0:T(8,128)(2,1)S(1)}, bf16[512,896]{1,0:T(8,128)(2,1)S(1)}, u32[]{:S(2)}, u32[]{:S(2)}) collective-permute-start(bf16[512,896]{1,0:T(8,128)(2,1)S(1)} %broadcast_select_fusion), channel_id=1, source_target_pairs={{0,2},{4,6},{8,10},{12,14},{16,18},{20,22},{24,26},{28,30}} | collective-permute-start | bytes 2752520 | tf_op jit(solution)/shard_map/ppermute | solution.py:92
  306.4 47.5 %collective-permute-start.34 = (bf16[128,2048]{1,0:T(8,128)(2,1)S(1)}, bf16[128,2048]{1,0:T(8,128)(2,1)S(1)}, u32[]{:S(2)}, u32[]{:S(2)}) collective-permute-start(bf16[128,2048]{1,0:T(8,128)(2,1)S(1)} %fusion.42), channel_id=1, source_target_pairs={{0,2},{1,3},{2,0},{3,1},{4,6},{5,7},{6,4},{7,5},{8,10},{9,11},{10,... | collective-permute-start | bytes 1572872 | tf_op jit(solution)/shard_map/ppermute | solution.py:17
  306.7 58.5 %collective-permute-start.16 = (bf16[128,2048]{1,0:T(8,128)(2,1)S(1)}, bf16[128,2048]{1,0:T(8,128)(2,1)S(1)}, u32[]{:S(2)}, u32[]{:S(2)}) collective-permute-start(bf16[128,2048]{1,0:T(8,128)(2,1)S(1)} %fusion.41), channel_id=1, source_target_pairs={{0,2},{1,3},{2,0},{3,1},{4,6},{5,7},{6,4},{7,5},{8,10},{9,11},{10,... | collective-permute-start | bytes 1572872 | tf_op jit(solution)/shard_map/ppermute | solution.py:17
  323.6 61.3 %collective-permute-start.37 = (bf16[512,896]{1,0:T(8,128)(2,1)S(1)}, bf16[512,896]{1,0:T(8,128)(2,1)S(1)}, u32[]{:S(2)}, u32[]{:S(2)}) collective-permute-start(bf16[512,896]{1,0:T(8,128)(2,1)S(1)} %broadcast_select_fusion.1), channel_id=1, source_target_pairs={{0,2},{4,6},{8,10},{12,14},{16,18},{20,22},{24,26},{28,30}} | collective-permute-start | bytes 2752520 | tf_op jit(solution)/shard_map/ppermute | solution.py:92
  355.0 35.5 %collective-permute-start.35 = (bf16[64,2048]{1,0:T(8,128)(2,1)S(1)}, bf16[64,2048]{1,0:T(8,128)(2,1)S(1)}, u32[]{:S(2)}, u32[]{:S(2)}) collective-permute-start(bf16[64,2048]{1,0:T(8,128)(2,1)S(1)} %add_convert_fusion.1), channel_id=1, source_target_pairs={{0,4},{1,5},{2,6},{3,7},{4,0},{5,1},{6,2},{7,3},{8,12},{9,13},{10,... | collective-permute-start | bytes 786440 | tf_op jit(solution)/shard_map/ppermute | solution.py:17
  365.3 29.2 %collective-permute-start.17 = (bf16[64,2048]{1,0:T(8,128)(2,1)S(1)}, bf16[64,2048]{1,0:T(8,128)(2,1)S(1)}, u32[]{:S(2)}, u32[]{:S(2)}) collective-permute-start(bf16[64,2048]{1,0:T(8,128)(2,1)S(1)} %add_convert_fusion.3), channel_id=1, source_target_pairs={{0,4},{1,5},{2,6},{3,7},{4,0},{5,1},{6,2},{7,3},{8,12},{9,13},{10,... | collective-permute-start | bytes 786440 | tf_op jit(solution)/shard_map/ppermute | solution.py:17
  365.5 30.0 %collective-permute-start.41 = (bf16[512,896]{1,0:T(8,128)(2,1)S(1)}, bf16[512,896]{1,0:T(8,128)(2,1)S(1)}, u32[]{:S(2)}, u32[]{:S(2)}) collective-permute-start(bf16[512,896]{1,0:T(8,128)(2,1)S(1)} %broadcast_select_fusion.2), channel_id=1, source_target_pairs={{0,1},{2,3},{4,5},{6,7},{8,9},{10,11},{12,13},{14,15},{16,17},{18,... | collective-permute-start | bytes 2752520 | tf_op jit(solution)/shard_map/ppermute | solution.py:92
  384.9 18.5 %collective-permute-start.38 = (bf16[512,896]{1,0:T(8,128)(2,1)S(1)}, bf16[512,896]{1,0:T(8,128)(2,1)S(1)}, u32[]{:S(2)}, u32[]{:S(2)}) collective-permute-start(bf16[512,896]{1,0:T(8,128)(2,1)S(1)} %broadcast_select_fusion.3), channel_id=1, source_target_pairs={{0,1},{2,3},{4,5},{6,7},{8,9},{10,11},{12,13},{14,15},{16,17},{18,... | collective-permute-start | bytes 2752520 | tf_op jit(solution)/shard_map/ppermute | solution.py:92

commit v3 on v2

--- a/solution.py
+++ b/solution.py
@@ -39,8 +39,13 @@
     return [2 * k + 1 for k in rest] + [2 * k for k in rest]
 
 
+def after(value, *earlier):
+    return lax.optimization_barrier((value,) + earlier)[0]
+
+
 def halving(total, axis, size):
     m = total.shape[0] // size
+    last = None
     received = []
     bit, left = 1, size
     while left > 1:
@@ -49,12 +54,13 @@
         for x in received:
             sent = sent + x[:half].astype(jnp.float32)
         received = [x[half:] for x in received]
-        received.append(swap(sent.astype(jnp.bfloat16), axis, size, bit))
+        last = sent.astype(jnp.bfloat16)
+        received.append(swap(last, axis, size, bit))
         total = total[half:]
         bit, left = bit * 2, left // 2
     for x in received:
         total = total + x.astype(jnp.float32)
-    return total
+    return total, last
 
 
 def pick(stacked, index, m):
@@ -83,15 +89,20 @@
         from_holder = col ^ ((row * SLAB_DEV) // units_dev)
 
         def broadcast(slab):
-            for bit in bits_down(cols):
+            steps, unseen = [], cols - 1
+            for bit in [1] + [b for b in bits_down(cols) if b > 1]:
+                reached = [k for k in range(cols) if not k & unseen]
                 pairs = [
                     (r * cols + (holders[r] ^ k), r * cols + (holders[r] ^ k ^ bit))
                     for r in range(rows)
-                    for k in range(0, cols, 2 * bit)
+                    for k in reached
                 ]
+                unseen -= bit
                 arrived = lax.ppermute(slab, ("row", "col"), pairs)
-                slab = jnp.where(from_holder % (2 * bit) == bit, arrived, slab)
-            return slab
+                here = ((from_holder & bit) != 0) & ((from_holder & unseen) == 0)
+                slab = jnp.where(here, arrived, slab)
+                steps.append(slab)
+            return steps
 
         def local_tokens(preact, h):
             split = preact.reshape((per_row, CHUNKS, part, preact.shape[1]))
@@ -113,26 +124,33 @@
                 target = col ^ k
                 position = (row ^ (target // per_row)) * per_row + target % per_row
                 blocks.append(pick(total, position, part))
-            return halving(jnp.concatenate(blocks, axis=0), "col", cols)
+            return halving(jnp.concatenate(blocks, axis=0), "col", cols)[0]
 
-        hidden = [
-            halving(contract_last(cotangent(h), down_weight), "row", rows) for h in range(CHUNKS)
+        def gather(block):
+            return jnp.concatenate(gather_relative(block, "row", rows), axis=0)
+
+        grads, earlier = [], ()
+        for h in range(CHUNKS):
+            part_sum = contract_last(after(cotangent(h), *earlier), down_weight)
+            hidden_grad, last = halving(part_sum, "row", rows)
+            earlier = (last,)
+            grads.append(
+                swiglu_grads(hidden_grad, local_tokens(gate_preact, h), local_tokens(up_preact, h))
+            )
+        gates = [gather(grad_gate) for grad_gate, _ in grads]
+        slabs = [
+            broadcast(lax.dynamic_slice_in_dim(gate, offset, SLAB_DEV, 1)) for gate in gates
         ]
-        grads = [
-            swiglu_grads(hidden[h], local_tokens(gate_preact, h), local_tokens(up_preact, h))
-            for h in range(CHUNKS)
-        ]
-        gates, slabs, outs = [], [], []
+        gate_sums, outs = [], []
         for h in range(CHUNKS):
-            gates.append(jnp.concatenate(gather_relative(grads[h][0], "row", rows), axis=0))
-            slabs.append(broadcast(lax.dynamic_slice_in_dim(gates[h], offset, SLAB_DEV, 1)))
+            earlier = tuple(steps[0] for steps in slabs[:h])
+            gate_sums.append(contract_last(after(gates[h], *earlier), gate_weight))
         for h in range(CHUNKS):
-            up_all = jnp.concatenate(gather_relative(grads[h][1], "row", rows), axis=0)
-            outs.append(
-                scatter(contract_last(gates[h], gate_weight) + contract_last(up_all, up_weight))
-            )
+            up_all = gather(after(grads[h][1], gate_sums[h]))
+            earlier = tuple(steps[min(h + 1 - n, len(steps) - 1)] for n, steps in enumerate(slabs[: h + 2]))
+            outs.append(scatter(gate_sums[h] + contract_last(after(up_all, *earlier), up_weight)))
         factor = lax.dot_general(
-            jnp.concatenate(slabs, axis=0),
+            jnp.concatenate([steps[-1] for steps in slabs], axis=0),
             jnp.concatenate(gates, axis=0),
             (((0,), (0,)), ((), ())),
             preferred_element_type=jnp.float32,

time: 415 us -> 331 us (0.80)
  waiting for transfers between devices: 236 us -> 144 us
  starting transfers between devices: 40.9 us -> 53.9 us
  matrix products: 86.9 us -> 82.6 us
    ppermute x36, waiting for transfers between devices: 181 us -> 106 us  [swap(): return lax.ppermute(block, axis, [(i, i ^ bit) for i in range(size)])]
    ppermute x6, waiting for transfers between devices: 54.8 us -> 37.4 us  [broadcast(): arrived = lax.ppermute(slab, ('row', 'col'), pairs)]
    ppermute x6, starting transfers between devices: 10.4 us -> 16.9 us  [broadcast(): arrived = lax.ppermute(slab, ('row', 'col'), pairs)]
    ppermute x36, starting transfers between devices: 30.5 us -> 37 us  [swap(): return lax.ppermute(block, axis, [(i, i ^ bit) for i in range(size)])]
    unnamed x48 -> x64, local copies, waits for them, and re-layouts: 19.9 us -> 18.4 us
  transfers between devices with their start and end apart: 42 -> 42, of which waited for: 23 -> 22; matrix products, arithmetic and copies ran while one was open for 25% -> 32% of each run, Pallas kernels for 0% -> 0%
where the time goes in v3:
time: 331 us; the launch traced here: 330 us
  waiting for transfers between devices  144 us (44%)
  matrix products  82.6 us (25%)
  starting transfers between devices  53.9 us (16%)
  local copies, waits for them, and re-layouts  28.8 us (9%)
  other arithmetic  19.7 us (6%)
    ppermute x36, waiting for transfers between devices, swap(): return lax.ppermute(block, axis, [(i, i ^ bit) for i in range(size)])  106 us
    dot_general x6, matrix products, contract_last(): lax.dot_general(left, right, (((1,), (1,)), ((), ())), preferred_element_...  72.6 us
    ppermute x6, waiting for transfers between devices, broadcast(): arrived = lax.ppermute(slab, ('row', 'col'), pairs)  37.4 us
    ppermute x36, starting transfers between devices, swap(): return lax.ppermute(block, axis, [(i, i ^ bit) for i in range(size)])  37 us
    unnamed x64, local copies, waits for them, and re-layouts  18.4 us
    ppermute x6, starting transfers between devices, broadcast(): arrived = lax.ppermute(slab, ('row', 'col'), pairs)  16.9 us
    dot_general x1, matrix products, shards(): lax.dot_general(jnp.concatenate([steps[-1] for steps in slabs], axis=0),...  9.98 us
  transfers between devices with their start and end apart: 42, of which 22 were waited for; matrix products, arithmetic and copies ran while one was open for 32% of the time, Pallas kernels for 0%

profile of v3, /device:TPU:0, one launch (start us, length us, event | category | flops | bytes accessed | tf_op | source)
XLA Modules:
  0.0 330.2 jit_solution(8305364523864257593)
XLA Ops:
  0.6 2.0 fusion.30
  2.6 2.9 collective-permute-start.17
  5.5 1.6 collective-permute-start.18
  7.1 2.6 collective-permute-start.20
  10.7 1.9 collective-permute-done.17
  12.6 3.5 %collective-permute-start.3 = (bf16[64,2048]{1,0:T(8,128)(2,1)}, bf16[64,2048]{1,0:T(8,128)(2,1)S(1)}, u32[]{:S(2)}, u32[]{:S(2)}) collective-permute-start(bf16[64,2048]{1,0:T(8,128)(2,1)} %get-tuple-element.34), channel_id=1, source_target_pairs={{0,4},{1,5},{2,6},{3,7},{4,0},{5,1},{6,2},{7,3},{8,12},{9,13},{10,... | collective-permute-start | bytes 786440 | tf_op jit(solution)/shard_map/ppermute | solution.py:17
  16.0 5.0 %collective-permute-done.18 = bf16[64,2048]{1,0:T(8,128)(2,1)S(1)} collective-permute-done((bf16[64,2048]{1,0:T(8,128)(2,1)}, bf16[64,2048]{1,0:T(8,128)(2,1)S(1)}, u32[]{:S(2)}, u32[]{:S(2)}) %collective-permute-start.18) | collective-permute-done | bytes 262176 | tf_op jit(solution)/shard_map/ppermute | solution.py:17
  21.1 1.3 collective-permute-done.20
  25.2 6.6 %collective-permute-done.1 = bf16[64,2048]{1,0:T(8,128)(2,1)S(1)} collective-permute-done((bf16[64,2048]{1,0:T(8,128)(2,1)}, bf16[64,2048]{1,0:T(8,128)(2,1)S(1)}, u32[]{:S(2)}, u32[]{:S(2)}) %collective-permute-start.1) | collective-permute-done | bytes 262176 | tf_op jit(solution)/shard_map/ppermute | solution.py:17
  31.9 2.6 collective-permute-start.5
  35.2 2.3 collective-permute-done.22
  37.5 4.1 %collective-permute-done.5 = bf16[64,2048]{1,0:T(8,128)(2,1)S(1)} collective-permute-done((bf16[64,2048]{1,0:T(8,128)(2,1)S(1)}, bf16[64,2048]{1,0:T(8,128)(2,1)S(1)}, u32[]{:S(2)}, u32[]{:S(2)}) %collective-permute-start.5) | collective-permute-done | bytes 262176 | tf_op jit(solution)/shard_map/ppermute | solution.py:17
  44.9 1.8 collective-permute-done.4
  46.7 4.4 %collective-permute-done.23 = bf16[64,2048]{1,0:T(8,128)(2,1)S(1)} collective-permute-done((bf16[64,2048]{1,0:T(8,128)(2,1)S(1)}, bf16[64,2048]{1,0:T(8,128)(2,1)S(1)}, u32[]{:S(2)}, u32[]{:S(2)}) %collective-permute-start.23) | collective-permute-done | bytes 262176 | tf_op jit(solution)/shard_map/ppermute | solution.py:17
  51.9 2.1 collective-permute-done.6
  54.0 1.0 dynamic-slice_dynamic-update-slice_fusion.7
  55.2 11.3 %fusion.31 = f32[512,3584]{1,0:T(8,128)S(1)} fusion(bf16[512,2048]{1,0:T(8,128)(2,1)S(1)} %dynamic-slice_dynamic-update-slice_fusion.8, bf16[3584,2048]{1,0:T(8,128)(2,1)} %param.11), kind=kOutput, calls=%fused_computation.121 | convolution fusion | flops 7516192768 | bytes 24117248 | tf_op jit(solution)/shard_map/dot_general | solution.py:11
  66.8 2.9 copy-done.6
  70.6 1.3 fusion.20
  72.2 1.5 collective-permute-start.8
  73.7 11.3 %fusion.33 = f32[512,3584]{1,0:T(8,128)S(1)} fusion(bf16[512,2048]{1,0:T(8,128)(2,1)S(1)} %dynamic-slice_dynamic-update-slice_fusion, bf16[3584,2048]{1,0:T(8,128)(2,1)} %param.11), kind=kOutput, calls=%fused_computation.123 | convolution fusion | flops 7516192768 | bytes 24117248 | tf_op jit(solution)/shard_map/dot_general | solution.py:11
  85.0 3.0 copy-done
  88.0 1.4 slice.214
  90.7 1.9 fusion.28
  92.7 2.2 collective-permute-done.8
  94.9 3.8 %fusion.8 = (bf16[128,3584]{1,0:T(8,128)(2,1)S(1)}, bf16[128,3584]{1,0:T(8,128)(2,1)S(1)}) fusion(bf16[2,1,64,3584]{3,2,1,0:T(8,128)(2,1)} %get-tuple-element.41, bf16[128,3584]{1,0:T(8,128)(2,1)} %collective-permute-done.8, bf16[256,3584]{1,0:T(8,128)(2,1)} %copy-done.10, f32[512,3584]{1,0:T(8,128)} %copy-done.1, bf16[2,1,64,3584]{3,2,1,0:T(8,128)(2,1)} %get-tuple-element.30), kind=kLoop, calls=%fused_computation.23 | loop fusion | flops 8716288 | bytes 7340032 | tf_op jit(solution)/shard_map/convert_element_type | solution.py:76
  98.7 1.6 collective-permute-start.10
  100.4 1.3 fusion.18
  102.3 19.7 %collective-permute-done.10 = bf16[128,3584]{1,0:T(8,128)(2,1)S(1)} collective-permute-done((bf16[128,3584]{1,0:T(8,128)(2,1)S(1)}, bf16[128,3584]{1,0:T(8,128)(2,1)S(1)}, u32[]{:S(2)}, u32[]{:S(2)}) %collective-permute-start.10) | collective-permute-done | bytes 917536 | tf_op jit(solution)/shard_map/ppermute | solution.py:17
  122.2 17.8 %collective-permute-done.25 = bf16[128,3584]{1,0:T(8,128)(2,1)S(1)} collective-permute-done((bf16[128,3584]{1,0:T(8,128)(2,1)S(1)}, bf16[128,3584]{1,0:T(8,128)(2,1)S(1)}, u32[]{:S(2)}, u32[]{:S(2)}) %collective-permute-start.25) | collective-permute-done | bytes 917536 | tf_op jit(solution)/shard_map/ppermute | solution.py:17
  140.0 2.4 fusion.17
  142.4 1.6 collective-permute-start.27
  145.2 12.7 %fusion.32 = f32[512,2048]{1,0:T(8,128)} fusion(bf16[512,3584]{1,0:T(8,128)(2,1)S(1)} %pad_maximum_fusion, bf16[2048,3584]{1,0:T(8,128)(2,1)} %param.9), kind=kOutput, calls=%fused_computation.122 | convolution fusion | flops 7516192768 | bytes 22544384 | tf_op jit(solution)/shard_map/dot_general | solution.py:11
  159.2 2.7 collective-permute-start.15
  161.9 1.0 constant_dynamic-update-slice_fusion.20
  163.9 18.0 %collective-permute-done.15 = bf16[512,896]{1,0:T(8,128)(2,1)S(1)} collective-permute-done((bf16[512,896]{1,0:T(8,128)(2,1)S(1)}, bf16[512,896]{1,0:T(8,128)(2,1)S(1)}, u32[]{:S(2)}, u32[]{:S(2)}) %collective-permute-start.15) | collective-permute-done | bytes 917536 | tf_op jit(solution)/shard_map/ppermute | solution.py:101
  182.4 1.3 collective-permute-start.16
  187.2 4.4 %collective-permute-start.29 = (bf16[512,896]{1,0:T(8,128)(2,1)S(1)}, bf16[512,896]{1,0:T(8,128)(2,1)S(1)}, u32[]{:S(2)}, u32[]{:S(2)}) collective-permute-start(bf16[512,896]{1,0:T(8,128)(2,1)S(1)} %constant_dynamic-slice_fusion.4), channel_id=1, source_target_pairs={{0,1},{8,9},{16,17},{24,25}} | collective-permute-start | bytes 2752520 | tf_op jit(solution)/shard_map/ppermute | solution.py:101
  191.6 12.5 %fusion.34 = f32[512,2048]{1,0:T(8,128)} fusion(bf16[512,3584]{1,0:T(8,128)(2,1)S(1)} %pad_maximum_fusion.2, bf16[2048,3584]{1,0:T(8,128)(2,1)} %param.9), kind=kOutput, calls=%fused_computation.124 | convolution fusion | flops 7516192768 | bytes 22544384 | tf_op jit(solution)/shard_map/dot_general | solution.py:11
  204.1 1.3 collective-permute-start.34
  205.6 2.3 collective-permute-start.36
  208.1 3.4 %collective-permute-done.29 = bf16[512,896]{1,0:T(8,128)(2,1)S(1)} collective-permute-done((bf16[512,896]{1,0:T(8,128)(2,1)S(1)}, bf16[512,896]{1,0:T(8,128)(2,1)S(1)}, u32[]{:S(2)}, u32[]{:S(2)}) %collective-permute-start.29) | collective-permute-done | bytes 917536 | tf_op jit(solution)/shard_map/ppermute | solution.py:101
  212.0 2.2 collective-permute-start.37
  214.2 11.7 %convolution_add_fusion.1 = f32[512,2048]{1,0:T(8,128)S(1)} fusion(f32[512,2048]{1,0:T(8,128)} %fusion.32, bf16[512,3584]{1,0:T(8,128)(2,1)S(1)} %pad_maximum_fusion.1, bf16[2048,3584]{1,0:T(8,128)(2,1)} %param.10), kind=kOutput, calls=%fused_computation.8 | convolution fusion | flops 7517241344 | bytes 26738688 | tf_op jit(solution)/shard_map/dot_general | solution.py:11
  226.3 1.1 pad_maximum_fusion.4
  227.4 2.4 collective-permute-start.30
  229.9 1.1 broadcast_select_fusion.1
  231.0 16.1 %collective-permute-done.37 = bf16[512,896]{1,0:T(8,128)(2,1)} collective-permute-done((bf16[512,896]{1,0:T(8,128)(2,1)S(1)}, bf16[512,896]{1,0:T(8,128)(2,1)}, u32[]{:S(2)}, u32[]{:S(2)}) %collective-permute-start.37) | collective-permute-done | bytes 917536 | tf_op jit(solution)/shard_map/ppermute | solution.py:101
  247.2 1.6 pad_maximum_fusion.3
  248.8 13.1 %convolution_add_fusion = f32[512,2048]{1,0:T(8,128)} fusion(f32[512,2048]{1,0:T(8,128)} %fusion.34, bf16[512,3584]{1,0:T(8,128)(2,1)S(1)} %pad_maximum_fusion.3, bf16[2048,3584]{1,0:T(8,128)(2,1)} %param.10), kind=kOutput, calls=%fused_computation.7 | convolution fusion | flops 7517241344 | bytes 26738688 | tf_op jit(solution)/shard_map/dot_general | solution.py:11
  262.0 1.7 dynamic-slice_convert_fusion.3
  264.1 1.4 fusion.25
  265.6 1.0 constant_dynamic-update-slice_fusion.16
  266.6 4.0 %collective-permute-start.41 = (bf16[512,896]{1,0:T(8,128)(2,1)S(1)}, bf16[512,896]{1,0:T(8,128)(2,1)S(1)}, u32[]{:S(2)}, u32[]{:S(2)}) collective-permute-start(bf16[512,896]{1,0:T(8,128)(2,1)S(1)} %broadcast_select_fusion.4), channel_id=1, source_target_pairs={{0,2},{1,3},{4,6},{5,7},{8,10},{9,11},{12,14},{13,15},{16,18},{17,... | collective-permute-start | bytes 2752520 | tf_op jit(solution)/shard_map/ppermute | solution.py:101
  270.7 8.3 %collective-permute-done.31 = bf16[128,2048]{1,0:T(8,128)(2,1)S(1)} collective-permute-done((bf16[128,2048]{1,0:T(8,128)(2,1)S(1)}, bf16[128,2048]{1,0:T(8,128)(2,1)S(1)}, u32[]{:S(2)}, u32[]{:S(2)}) %collective-permute-start.31) | collective-permute-done | bytes 524320 | tf_op jit(solution)/shard_map/ppermute | solution.py:17
  279.0 1.2 add_convert_fusion.3
  280.2 4.7 %collective-permute-start.32 = (bf16[64,2048]{1,0:T(8,128)(2,1)S(1)}, bf16[64,2048]{1,0:T(8,128)(2,1)S(1)}, u32[]{:S(2)}, u32[]{:S(2)}) collective-permute-start(bf16[64,2048]{1,0:T(8,128)(2,1)S(1)} %add_convert_fusion.3), channel_id=1, source_target_pairs={{0,4},{1,5},{2,6},{3,7},{4,0},{5,1},{6,2},{7,3},{8,12},{9,13},{10,... | collective-permute-start | bytes 786440 | tf_op jit(solution)/shard_map/ppermute | solution.py:17
  284.9 3.9 %collective-permute-done.38 = bf16[256,2048]{1,0:T(8,128)(2,1)S(1)} collective-permute-done((bf16[256,2048]{1,0:T(8,128)(2,1)S(1)}, bf16[256,2048]{1,0:T(8,128)(2,1)S(1)}, u32[]{:S(2)}, u32[]{:S(2)}) %collective-permute-start.38) | collective-permute-done | bytes 1048608 | tf_op jit(solution)/shard_map/ppermute | solution.py:17
  289.0 14.2 %collective-permute-done.32 = bf16[64,2048]{1,0:T(8,128)(2,1)S(1)} collective-permute-done((bf16[64,2048]{1,0:T(8,128)(2,1)S(1)}, bf16[64,2048]{1,0:T(8,128)(2,1)S(1)}, u32[]{:S(2)}, u32[]{:S(2)}) %collective-permute-start.32) | collective-permute-done | bytes 262176 | tf_op jit(solution)/shard_map/ppermute | solution.py:17
  303.2 1.1 add_convert_fusion.2
  304.4 8.9 %collective-permute-done.39 = bf16[128,2048]{1,0:T(8,128)(2,1)S(1)} collective-permute-done((bf16[128,2048]{1,0:T(8,128)(2,1)S(1)}, bf16[128,2048]{1,0:T(8,128)(2,1)S(1)}, u32[]{:S(2)}, u32[]{:S(2)}) %collective-permute-start.39) | collective-permute-done | bytes 524320 | tf_op jit(solution)/shard_map/ppermute | solution.py:17
  313.4 4.7 %collective-permute-start.40 = (bf16[64,2048]{1,0:T(8,128)(2,1)S(1)}, bf16[64,2048]{1,0:T(8,128)(2,1)S(1)}, u32[]{:S(2)}, u32[]{:S(2)}) collective-permute-start(bf16[64,2048]{1,0:T(8,128)(2,1)S(1)} %add_convert_fusion.1), channel_id=1, source_target_pairs={{0,4},{1,5},{2,6},{3,7},{4,0},{5,1},{6,2},{7,3},{8,12},{9,13},{10,... | collective-permute-start | bytes 786440 | tf_op jit(solution)/shard_map/ppermute | solution.py:17
  318.1 10.0 %convolution_multiply_fusion = f32[896,3584]{1,0:T(8,128)} fusion(bf16[1024,3584]{1,0:T(8,128)(2,1)S(1)} %copy-done.13, bf16[512,896]{1,0:T(8,128)(2,1)S(1)} %broadcast_select_fusion, bf16[512,896]{1,0:T(8,128)(2,1)S(1)} %copy-done.11), kind=kOutput, calls=%fused_computation | convolution fusion | flops 6583549952 | bytes 22020096 | tf_op jit(solution)/shard_map/dot_general | solution.py:152
  328.1 1.1 collective-permute-done.40
  (130 shorter events, 23.2 us)
Async XLA Ops:
  2.6 10.0 %collective-permute-start.17 = (bf16[64,2048]{1,0:T(8,128)(2,1)}, bf16[64,2048]{1,0:T(8,128)(2,1)S(1)}, u32[]{:S(2)}, u32[]{:S(2)}) collective-permute-start(bf16[64,2048]{1,0:T(8,128)(2,1)} %get-tuple-element.37), channel_id=1, source_target_pairs={{0,1},{1,0},{2,3},{3,2},{4,5},{5,4},{6,7},{7,6},{8,9},{9,8},{10,11... | collective-permute-start | bytes 786440 | tf_op jit(solution)/shard_map/ppermute | solution.py:17
  5.5 15.5 %collective-permute-start.18 = (bf16[64,2048]{1,0:T(8,128)(2,1)}, bf16[64,2048]{1,0:T(8,128)(2,1)S(1)}, u32[]{:S(2)}, u32[]{:S(2)}) collective-permute-start(bf16[64,2048]{1,0:T(8,128)(2,1)} %get-tuple-element.37), channel_id=1, source_target_pairs={{0,2},{1,3},{2,0},{3,1},{4,6},{5,7},{6,4},{7,5},{8,10},{9,11},{10,... | collective-permute-start | bytes 786440 | tf_op jit(solution)/shard_map/ppermute | solution.py:17
  7.1 15.3 %collective-permute-start.20 = (bf16[64,2048]{1,0:T(8,128)(2,1)}, bf16[64,2048]{1,0:T(8,128)(2,1)S(1)}, u32[]{:S(2)}, u32[]{:S(2)}) collective-permute-start(bf16[64,2048]{1,0:T(8,128)(2,1)} %get-tuple-element.37), channel_id=1, source_target_pairs={{0,4},{1,5},{2,6},{3,7},{4,0},{5,1},{6,2},{7,3},{8,12},{9,13},{10,... | collective-permute-start | bytes 786440 | tf_op jit(solution)/shard_map/ppermute | solution.py:17
  9.7 14.8 %collective-permute-start = (bf16[64,2048]{1,0:T(8,128)(2,1)}, bf16[64,2048]{1,0:T(8,128)(2,1)S(1)}, u32[]{:S(2)}, u32[]{:S(2)}) collective-permute-start(bf16[64,2048]{1,0:T(8,128)(2,1)} %get-tuple-element.34), channel_id=1, source_target_pairs={{0,1},{1,0},{2,3},{3,2},{4,5},{5,4},{6,7},{7,6},{8,9},{9,8},{10,11... | collective-permute-start | bytes 786440 | tf_op jit(solution)/shard_map/ppermute | solution.py:17
  10.2 21.6 %collective-permute-start.1 = (bf16[64,2048]{1,0:T(8,128)(2,1)}, bf16[64,2048]{1,0:T(8,128)(2,1)S(1)}, u32[]{:S(2)}, u32[]{:S(2)}) collective-permute-start(bf16[64,2048]{1,0:T(8,128)(2,1)} %get-tuple-element.34), channel_id=1, source_target_pairs={{0,2},{1,3},{2,0},{3,1},{4,6},{5,7},{6,4},{7,5},{8,10},{9,11},{10,... | collective-permute-start | bytes 786440 | tf_op jit(solution)/shard_map/ppermute | solution.py:17
  12.6 19.3 %collective-permute-start.3 = (bf16[64,2048]{1,0:T(8,128)(2,1)}, bf16[64,2048]{1,0:T(8,128)(2,1)S(1)}, u32[]{:S(2)}, u32[]{:S(2)}) collective-permute-start(bf16[64,2048]{1,0:T(8,128)(2,1)} %get-tuple-element.34), channel_id=1, source_target_pairs={{0,4},{1,5},{2,6},{3,7},{4,0},{5,1},{6,2},{7,3},{8,12},{9,13},{10,... | collective-permute-start | bytes 786440 | tf_op jit(solution)/shard_map/ppermute | solution.py:17
  21.1 13.5 %collective-permute-start.19 = (bf16[64,2048]{1,0:T(8,128)(2,1)S(1)}, bf16[64,2048]{1,0:T(8,128)(2,1)S(1)}, u32[]{:S(2)}, u32[]{:S(2)}) collective-permute-start(bf16[64,2048]{1,0:T(8,128)(2,1)S(1)} %collective-permute-done.18), channel_id=1, source_target_pairs={{0,1},{1,0},{2,3},{3,2},{4,5},{5,4},{6,7},{7,6},{8,9},{9,8},{10,11... | collective-permute-start | bytes 786440 | tf_op jit(solution)/shard_map/ppermute | solution.py:17
  22.4 21.0 %collective-permute-start.21 = (bf16[64,2048]{1,0:T(8,128)(2,1)S(1)}, bf16[64,2048]{1,0:T(8,128)(2,1)S(1)}, u32[]{:S(2)}, u32[]{:S(2)}) collective-permute-start(bf16[64,2048]{1,0:T(8,128)(2,1)S(1)} %collective-permute-done.20), channel_id=1, source_target_pairs={{0,1},{1,0},{2,3},{3,2},{4,5},{5,4},{6,7},{7,6},{8,9},{9,8},{10,11... | collective-permute-start | bytes 786440 | tf_op jit(solution)/shard_map/ppermute | solution.py:17
  24.5 12.9 %collective-permute-start.22 = (bf16[64,2048]{1,0:T(8,128)(2,1)S(1)}, bf16[64,2048]{1,0:T(8,128)(2,1)S(1)}, u32[]{:S(2)}, u32[]{:S(2)}) collective-permute-start(bf16[64,2048]{1,0:T(8,128)(2,1)S(1)} %collective-permute-done.20), channel_id=1, source_target_pairs={{0,2},{1,3},{2,0},{3,1},{4,6},{5,7},{6,4},{7,5},{8,10},{9,11},{10,... | collective-permute-start | bytes 786440 | tf_op jit(solution)/shard_map/ppermute | solution.py:17
  31.8 13.1 %collective-permute-start.2 = (bf16[64,2048]{1,0:T(8,128)(2,1)S(1)}, bf16[64,2048]{1,0:T(8,128)(2,1)S(1)}, u32[]{:S(2)}, u32[]{:S(2)}) collective-permute-start(bf16[64,2048]{1,0:T(8,128)(2,1)S(1)} %collective-permute-done.1), channel_id=1, source_target_pairs={{0,1},{1,0},{2,3},{3,2},{4,5},{5,4},{6,7},{7,6},{8,9},{9,8},{10,11... | collective-permute-start | bytes 786440 | tf_op jit(solution)/shard_map/ppermute | solution.py:17
  31.9 9.7 %collective-permute-start.5 = (bf16[64,2048]{1,0:T(8,128)(2,1)S(1)}, bf16[64,2048]{1,0:T(8,128)(2,1)S(1)}, u32[]{:S(2)}, u32[]{:S(2)}) collective-permute-start(bf16[64,2048]{1,0:T(8,128)(2,1)S(1)} %collective-permute-done.3), channel_id=1, source_target_pairs={{0,2},{1,3},{2,0},{3,1},{4,6},{5,7},{6,4},{7,5},{8,10},{9,11},{10,... | collective-permute-start | bytes 786440 | tf_op jit(solution)/shard_map/ppermute | solution.py:17
  34.6 12.1 %collective-permute-start.4 = (bf16[64,2048]{1,0:T(8,128)(2,1)S(1)}, bf16[64,2048]{1,0:T(8,128)(2,1)S(1)}, u32[]{:S(2)}, u32[]{:S(2)}) collective-permute-start(bf16[64,2048]{1,0:T(8,128)(2,1)S(1)} %collective-permute-done.3), channel_id=1, source_target_pairs={{0,1},{1,0},{2,3},{3,2},{4,5},{5,4},{6,7},{7,6},{8,9},{9,8},{10,11... | collective-permute-start | bytes 786440 | tf_op jit(solution)/shard_map/ppermute | solution.py:17
  37.4 13.7 %collective-permute-start.23 = (bf16[64,2048]{1,0:T(8,128)(2,1)S(1)}, bf16[64,2048]{1,0:T(8,128)(2,1)S(1)}, u32[]{:S(2)}, u32[]{:S(2)}) collective-permute-start(bf16[64,2048]{1,0:T(8,128)(2,1)S(1)} %collective-permute-done.22), channel_id=1, source_target_pairs={{0,1},{1,0},{2,3},{3,2},{4,5},{5,4},{6,7},{7,6},{8,9},{9,8},{10,11... | collective-permute-start | bytes 786440 | tf_op jit(solution)/shard_map/ppermute | solution.py:17
  41.6 12.3 %collective-permute-start.6 = (bf16[64,2048]{1,0:T(8,128)(2,1)S(1)}, bf16[64,2048]{1,0:T(8,128)(2,1)S(1)}, u32[]{:S(2)}, u32[]{:S(2)}) collective-permute-start(bf16[64,2048]{1,0:T(8,128)(2,1)S(1)} %collective-permute-done.5), channel_id=1, source_target_pairs={{0,1},{1,0},{2,3},{3,2},{4,5},{5,4},{6,7},{7,6},{8,9},{9,8},{10,11... | collective-permute-start | bytes 786440 | tf_op jit(solution)/shard_map/ppermute | solution.py:17
  66.5 5.3 %copy-start.1 = (f32[512,3584]{1,0:T(8,128)}, f32[512,3584]{1,0:T(8,128)S(1)}, u32[]{:S(2)}) copy-start(f32[512,3584]{1,0:T(8,128)S(1)} %fusion.31) | copy-start | bytes 22020100
  66.5 3.2 copy-start.6
  66.7 3.9 %collective-permute-start.7 = (bf16[256,3584]{1,0:T(8,128)(2,1)S(1)}, bf16[256,3584]{1,0:T(8,128)(2,1)S(1)}, u32[]{:S(2)}, u32[]{:S(2)}) collective-permute-start(bf16[256,3584]{1,0:T(8,128)(2,1)S(1)} %slice.215), channel_id=1, source_target_pairs={{0,8},{8,0},{16,24},{24,16},{1,9},{9,1},{17,25},{25,17},{2,10},{10... | collective-permute-start | bytes 5505032 | tf_op jit(solution)/shard_map/ppermute | solution.py:17
  70.6 1.6 copy-start.10
  72.2 22.7 %collective-permute-start.8 = (bf16[128,3584]{1,0:T(8,128)(2,1)}, bf16[128,3584]{1,0:T(8,128)(2,1)}, u32[]{:S(2)}, u32[]{:S(2)}) collective-permute-start(bf16[128,3584]{1,0:T(8,128)(2,1)} %fusion.20), channel_id=1, source_target_pairs={{0,16},{8,24},{16,0},{24,8},{1,17},{9,25},{17,1},{25,9},{2,18},{10... | collective-permute-start | bytes 2752520 | tf_op jit(solution)/shard_map/ppermute | solution.py:17
  85.0 3.1 copy-start
  88.0 2.2 copy-start.8
  88.0 2.7 copy-start.9
  89.4 10.9 %collective-permute-start.24 = (bf16[256,3584]{1,0:T(8,128)(2,1)}, bf16[256,3584]{1,0:T(8,128)(2,1)}, u32[]{:S(2)}, u32[]{:S(2)}) collective-permute-start(bf16[256,3584]{1,0:T(8,128)(2,1)} %slice.214), channel_id=1, source_target_pairs={{0,8},{8,0},{16,24},{24,16},{1,9},{9,1},{17,25},{25,17},{2,10},{10... | collective-permute-start | bytes 5505032 | tf_op jit(solution)/shard_map/ppermute | solution.py:17
  90.7 9.6 %slice-start = ((s8[7340032]{0:T(1024)(128)(4,1)}), s8[3145728]{0:T(1024)(128)(4,1)S(1)}, s32[]{:S(2)}) async-start(s8[7340032]{0:T(1024)(128)(4,1)} %bitcast.37), calls=%async_computation | async-start | bytes 6291456
  94.9 5.5 %slice-start.1 = ((s8[7340032]{0:T(1024)(128)(4,1)}), s8[4194304]{0:T(1024)(128)(4,1)S(1)}, s32[]{:S(2)}) async-start(s8[7340032]{0:T(1024)(128)(4,1)} %bitcast.37), calls=%async_computation.1 | async-start | bytes 8388608
  98.7 23.4 %collective-permute-start.10 = (bf16[128,3584]{1,0:T(8,128)(2,1)S(1)}, bf16[128,3584]{1,0:T(8,128)(2,1)S(1)}, u32[]{:S(2)}, u32[]{:S(2)}) collective-permute-start(bf16[128,3584]{1,0:T(8,128)(2,1)S(1)} %get-tuple-element.15), channel_id=1, source_target_pairs={{0,16},{8,24},{16,0},{24,8},{1,17},{9,25},{17,1},{25,9},{2,18},{10... | collective-permute-start | bytes 2752520 | tf_op jit(solution)/shard_map/ppermute | solution.py:17
  100.3 21.8 %collective-permute-start.9 = (bf16[128,3584]{1,0:T(8,128)(2,1)S(1)}, bf16[128,3584]{1,0:T(8,128)(2,1)S(1)}, u32[]{:S(2)}, u32[]{:S(2)}) collective-permute-start(bf16[128,3584]{1,0:T(8,128)(2,1)S(1)} %get-tuple-element.15), channel_id=1, source_target_pairs={{0,8},{8,0},{16,24},{24,16},{1,9},{9,1},{17,25},{25,17},{2,10},{10... | collective-permute-start | bytes 2752520 | tf_op jit(solution)/shard_map/ppermute | solution.py:17
  101.7 38.3 %copy-start.2 = (bf16[2,1,64,3584]{3,2,1,0:T(8,128)(2,1)S(1)}, bf16[2,1,64,3584]{3,2,1,0:T(8,128)(2,1)}, u32[]{:S(2)}) copy-start(bf16[2,1,64,3584]{3,2,1,0:T(8,128)(2,1)} %get-tuple-element.31) | copy-start | bytes 2752516
  101.7 38.3 %copy-start.3 = (bf16[2,1,64,3584]{3,2,1,0:T(8,128)(2,1)S(1)}, bf16[2,1,64,3584]{3,2,1,0:T(8,128)(2,1)}, u32[]{:S(2)}) copy-start(bf16[2,1,64,3584]{3,2,1,0:T(8,128)(2,1)} %get-tuple-element.40) | copy-start | bytes 2752516
  101.8 38.2 %collective-permute-start.25 = (bf16[128,3584]{1,0:T(8,128)(2,1)S(1)}, bf16[128,3584]{1,0:T(8,128)(2,1)S(1)}, u32[]{:S(2)}, u32[]{:S(2)}) collective-permute-start(bf16[128,3584]{1,0:T(8,128)(2,1)S(1)} %fusion.18), channel_id=1, source_target_pairs={{0,16},{8,24},{16,0},{24,8},{1,17},{9,25},{17,1},{25,9},{2,18},{10... | collective-permute-start | bytes 2752520 | tf_op jit(solution)/shard_map/ppermute | solution.py:17
  122.1 21.9 %collective-permute-start.11 = (bf16[128,3584]{1,0:T(8,128)(2,1)S(1)}, bf16[128,3584]{1,0:T(8,128)(2,1)S(1)}, u32[]{:S(2)}, u32[]{:S(2)}) collective-permute-start(bf16[128,3584]{1,0:T(8,128)(2,1)S(1)} %collective-permute-done.10), channel_id=1, source_target_pairs={{0,8},{8,0},{16,24},{24,16},{1,9},{9,1},{17,25},{25,17},{2,10},{10... | collective-permute-start | bytes 2752520 | tf_op jit(solution)/shard_map/ppermute | solution.py:17
  122.2 17.8 %copy-start.12 = (bf16[1024,3584]{1,0:T(8,128)(2,1)}, bf16[1024,3584]{1,0:T(8,128)(2,1)S(1)}, u32[]{:S(2)}) copy-start(bf16[1024,3584]{1,0:T(8,128)(2,1)S(1)} %constant_dynamic-update-slice_fusion.21) | copy-start | bytes 22020100
  142.4 41.4 %collective-permute-start.27 = (bf16[128,3584]{1,0:T(8,128)(2,1)S(1)}, bf16[128,3584]{1,0:T(8,128)(2,1)S(1)}, u32[]{:S(2)}, u32[]{:S(2)}) collective-permute-start(bf16[128,3584]{1,0:T(8,128)(2,1)S(1)} %get-tuple-element.17), channel_id=1, source_target_pairs={{0,16},{8,24},{16,0},{24,8},{1,17},{9,25},{17,1},{25,9},{2,18},{10... | collective-permute-start | bytes 2752520 | tf_op jit(solution)/shard_map/ppermute | solution.py:17
  144.0 40.4 %collective-permute-start.26 = (bf16[128,3584]{1,0:T(8,128)(2,1)S(1)}, bf16[128,3584]{1,0:T(8,128)(2,1)S(1)}, u32[]{:S(2)}, u32[]{:S(2)}) collective-permute-start(bf16[128,3584]{1,0:T(8,128)(2,1)S(1)} %get-tuple-element.17), channel_id=1, source_target_pairs={{0,8},{8,0},{16,24},{24,16},{1,9},{9,1},{17,25},{25,17},{2,10},{10... | collective-permute-start | bytes 2752520 | tf_op jit(solution)/shard_map/ppermute | solution.py:17
  144.0 1.0 copy-start.4
  157.9 4.0 %copy-start.5 = (bf16[128,3584]{1,0:T(8,128)(2,1)S(1)}, bf16[128,3584]{1,0:T(8,128)(2,1)}, u32[]{:S(2)}) copy-start(bf16[128,3584]{1,0:T(8,128)(2,1)} %copy-done.4) | copy-start | bytes 2752516
  157.9 25.9 %collective-permute-start.13 = (bf16[128,3584]{1,0:T(8,128)(2,1)S(1)}, bf16[128,3584]{1,0:T(8,128)(2,1)S(1)}, u32[]{:S(2)}, u32[]{:S(2)}) collective-permute-start(bf16[128,3584]{1,0:T(8,128)(2,1)S(1)} %get-tuple-element.8), channel_id=1, source_target_pairs={{0,16},{8,24},{16,0},{24,8},{1,17},{9,25},{17,1},{25,9},{2,18},{10... | collective-permute-start | bytes 2752520 | tf_op jit(solution)/shard_map/ppermute | solution.py:17
  158.4 47.1 %collective-permute-start.12 = (bf16[128,3584]{1,0:T(8,128)(2,1)S(1)}, bf16[128,3584]{1,0:T(8,128)(2,1)S(1)}, u32[]{:S(2)}, u32[]{:S(2)}) collective-permute-start(bf16[128,3584]{1,0:T(8,128)(2,1)S(1)} %get-tuple-element.8), channel_id=1, source_target_pairs={{0,8},{8,0},{16,24},{24,16},{1,9},{9,1},{17,25},{25,17},{2,10},{10... | collective-permute-start | bytes 2752520 | tf_op jit(solution)/shard_map/ppermute | solution.py:17
  159.2 22.7 %collective-permute-start.15 = (bf16[512,896]{1,0:T(8,128)(2,1)S(1)}, bf16[512,896]{1,0:T(8,128)(2,1)S(1)}, u32[]{:S(2)}, u32[]{:S(2)}) collective-permute-start(bf16[512,896]{1,0:T(8,128)(2,1)S(1)} %constant_dynamic-slice_fusion.5), channel_id=1, source_target_pairs={{0,1},{8,9},{16,17},{24,25}} | collective-permute-start | bytes 2752520 | tf_op jit(solution)/shard_map/ppermute | solution.py:101
  182.4 23.0 %collective-permute-start.16 = (bf16[512,896]{1,0:T(8,128)(2,1)S(1)}, bf16[512,896]{1,0:T(8,128)(2,1)S(1)}, u32[]{:S(2)}, u32[]{:S(2)}) collective-permute-start(bf16[512,896]{1,0:T(8,128)(2,1)S(1)} %broadcast_select_fusion.3), channel_id=1, source_target_pairs={{0,4},{1,5},{8,12},{9,13},{16,20},{17,21},{24,28},{25,29}} | collective-permute-start | bytes 2752520 | tf_op jit(solution)/shard_map/ppermute | solution.py:101
  183.8 2.6 collective-permute-start.28
  183.9 23.9 %collective-permute-start.14 = (bf16[128,3584]{1,0:T(8,128)(2,1)S(1)}, bf16[128,3584]{1,0:T(8,128)(2,1)S(1)}, u32[]{:S(2)}, u32[]{:S(2)}) collective-permute-start(bf16[128,3584]{1,0:T(8,128)(2,1)S(1)} %collective-permute-done.13), channel_id=1, source_target_pairs={{0,8},{8,0},{16,24},{24,16},{1,9},{9,1},{17,25},{25,17},{2,10},{10... | collective-permute-start | bytes 2752520 | tf_op jit(solution)/shard_map/ppermute | solution.py:17
  187.2 24.3 %collective-permute-start.29 = (bf16[512,896]{1,0:T(8,128)(2,1)S(1)}, bf16[512,896]{1,0:T(8,128)(2,1)S(1)}, u32[]{:S(2)}, u32[]{:S(2)}) collective-permute-start(bf16[512,896]{1,0:T(8,128)(2,1)S(1)} %constant_dynamic-slice_fusion.4), channel_id=1, source_target_pairs={{0,1},{8,9},{16,17},{24,25}} | collective-permute-start | bytes 2752520 | tf_op jit(solution)/shard_map/ppermute | solution.py:101
  204.1 22.2 %collective-permute-start.34 = (bf16[128,3584]{1,0:T(8,128)(2,1)S(1)}, bf16[128,3584]{1,0:T(8,128)(2,1)}, u32[]{:S(2)}, u32[]{:S(2)}) collective-permute-start(bf16[128,3584]{1,0:T(8,128)(2,1)S(1)} %get-tuple-element.12), channel_id=1, source_target_pairs={{0,16},{8,24},{16,0},{24,8},{1,17},{9,25},{17,1},{25,9},{2,18},{10... | collective-permute-start | bytes 2752520 | tf_op jit(solution)/shard_map/ppermute | solution.py:17
  205.4 41.8 %collective-permute-start.33 = (bf16[128,3584]{1,0:T(8,128)(2,1)S(1)}, bf16[128,3584]{1,0:T(8,128)(2,1)}, u32[]{:S(2)}, u32[]{:S(2)}) collective-permute-start(bf16[128,3584]{1,0:T(8,128)(2,1)S(1)} %get-tuple-element.12), channel_id=1, source_target_pairs={{0,8},{8,0},{16,24},{24,16},{1,9},{9,1},{17,25},{25,17},{2,10},{10... | collective-permute-start | bytes 2752520 | tf_op jit(solution)/shard_map/ppermute | solution.py:17
  205.6 24.3 %collective-permute-start.36 = (bf16[512,896]{1,0:T(8,128)(2,1)S(1)}, bf16[512,896]{1,0:T(8,128)(2,1)}, u32[]{:S(2)}, u32[]{:S(2)}) collective-permute-start(bf16[512,896]{1,0:T(8,128)(2,1)S(1)} %broadcast_select_fusion.5), channel_id=1, source_target_pairs={{0,2},{1,3},{4,6},{5,7},{8,10},{9,11},{12,14},{13,15},{16,18},{17,... | collective-permute-start | bytes 2752520 | tf_op jit(solution)/shard_map/ppermute | solution.py:101
  212.0 35.1 %collective-permute-start.37 = (bf16[512,896]{1,0:T(8,128)(2,1)S(1)}, bf16[512,896]{1,0:T(8,128)(2,1)}, u32[]{:S(2)}, u32[]{:S(2)}) collective-permute-start(bf16[512,896]{1,0:T(8,128)(2,1)S(1)} %broadcast_select_fusion.2), channel_id=1, source_target_pairs={{0,4},{1,5},{8,12},{9,13},{16,20},{17,21},{24,28},{25,29}} | collective-permute-start | bytes 2752520 | tf_op jit(solution)/shard_map/ppermute | solution.py:101
  226.3 20.9 %collective-permute-start.35 = (bf16[128,3584]{1,0:T(8,128)(2,1)}, bf16[128,3584]{1,0:T(8,128)(2,1)S(1)}, u32[]{:S(2)}, u32[]{:S(2)}) collective-permute-start(bf16[128,3584]{1,0:T(8,128)(2,1)} %collective-permute-done.34), channel_id=1, source_target_pairs={{0,8},{8,0},{16,24},{24,16},{1,9},{9,1},{17,25},{25,17},{2,10},{10... | collective-permute-start | bytes 2752520 | tf_op jit(solution)/shard_map/ppermute | solution.py:17
  227.4 36.7 %collective-permute-start.30 = (bf16[256,2048]{1,0:T(8,128)(2,1)}, bf16[256,2048]{1,0:T(8,128)(2,1)}, u32[]{:S(2)}, u32[]{:S(2)}) collective-permute-start(bf16[256,2048]{1,0:T(8,128)(2,1)} %pad_maximum_fusion.4), channel_id=1, source_target_pairs={{0,1},{1,0},{2,3},{3,2},{4,5},{5,4},{6,7},{7,6},{8,9},{9,8},{10,11... | collective-permute-start | bytes 3145736 | tf_op jit(solution)/shard_map/ppermute | solution.py:17
  263.6 6.9 %copy-start.7 = (f32[512,2048]{1,0:T(8,128)S(1)}, f32[512,2048]{1,0:T(8,128)}, u32[]{:S(2)}) copy-start(f32[512,2048]{1,0:T(8,128)} %convolution_add_fusion) | copy-start | bytes 12582916
  263.8 25.1 %collective-permute-start.38 = (bf16[256,2048]{1,0:T(8,128)(2,1)S(1)}, bf16[256,2048]{1,0:T(8,128)(2,1)S(1)}, u32[]{:S(2)}, u32[]{:S(2)}) collective-permute-start(bf16[256,2048]{1,0:T(8,128)(2,1)S(1)} %pad_maximum_fusion.5), channel_id=1, source_target_pairs={{0,1},{1,0},{2,3},{3,2},{4,5},{5,4},{6,7},{7,6},{8,9},{9,8},{10,11... | collective-permute-start | bytes 3145736 | tf_op jit(solution)/shard_map/ppermute | solution.py:17
  265.5 13.5 %collective-permute-start.31 = (bf16[128,2048]{1,0:T(8,128)(2,1)S(1)}, bf16[128,2048]{1,0:T(8,128)(2,1)S(1)}, u32[]{:S(2)}, u32[]{:S(2)}) collective-permute-start(bf16[128,2048]{1,0:T(8,128)(2,1)S(1)} %fusion.25), channel_id=1, source_target_pairs={{0,2},{1,3},{2,0},{3,1},{4,6},{5,7},{6,4},{7,5},{8,10},{9,11},{10,... | collective-permute-start | bytes 1572872 | tf_op jit(solution)/shard_map/ppermute | solution.py:17
  266.6 37.7 %collective-permute-start.41 = (bf16[512,896]{1,0:T(8,128)(2,1)S(1)}, bf16[512,896]{1,0:T(8,128)(2,1)S(1)}, u32[]{:S(2)}, u32[]{:S(2)}) collective-permute-start(bf16[512,896]{1,0:T(8,128)(2,1)S(1)} %broadcast_select_fusion.4), channel_id=1, source_target_pairs={{0,2},{1,3},{4,6},{5,7},{8,10},{9,11},{12,14},{13,15},{16,18},{17,... | collective-permute-start | bytes 2752520 | tf_op jit(solution)/shard_map/ppermute | solution.py:101
  279.0 39.1 %copy-start.13 = (bf16[1024,3584]{1,0:T(8,128)(2,1)S(1)}, bf16[1024,3584]{1,0:T(8,128)(2,1)}, u32[]{:S(2)}) copy-start(bf16[1024,3584]{1,0:T(8,128)(2,1)} %constant_dynamic-update-slice_fusion.16) | copy-start | bytes 22020100
  280.2 23.0 %collective-permute-start.32 = (bf16[64,2048]{1,0:T(8,128)(2,1)S(1)}, bf16[64,2048]{1,0:T(8,128)(2,1)S(1)}, u32[]{:S(2)}, u32[]{:S(2)}) collective-permute-start(bf16[64,2048]{1,0:T(8,128)(2,1)S(1)} %add_convert_fusion.3), channel_id=1, source_target_pairs={{0,4},{1,5},{2,6},{3,7},{4,0},{5,1},{6,2},{7,3},{8,12},{9,13},{10,... | collective-permute-start | bytes 786440 | tf_op jit(solution)/shard_map/ppermute | solution.py:17
  288.9 24.4 %collective-permute-start.39 = (bf16[128,2048]{1,0:T(8,128)(2,1)S(1)}, bf16[128,2048]{1,0:T(8,128)(2,1)S(1)}, u32[]{:S(2)}, u32[]{:S(2)}) collective-permute-start(bf16[128,2048]{1,0:T(8,128)(2,1)S(1)} %fusion.26), channel_id=1, source_target_pairs={{0,2},{1,3},{2,0},{3,1},{4,6},{5,7},{6,4},{7,5},{8,10},{9,11},{10,... | collective-permute-start | bytes 1572872 | tf_op jit(solution)/shard_map/ppermute | solution.py:17
  304.3 13.9 %copy-start.11 = (bf16[512,896]{1,0:T(8,128)(2,1)S(1)}, bf16[512,896]{1,0:T(8,128)(2,1)}, u32[]{:S(2)}) copy-start(bf16[512,896]{1,0:T(8,128)(2,1)} %broadcast_select_fusion.1) | copy-start | bytes 2752516
  313.4 15.8 %collective-permute-start.40 = (bf16[64,2048]{1,0:T(8,128)(2,1)S(1)}, bf16[64,2048]{1,0:T(8,128)(2,1)S(1)}, u32[]{:S(2)}, u32[]{:S(2)}) collective-permute-start(bf16[64,2048]{1,0:T(8,128)(2,1)S(1)} %add_convert_fusion.1), channel_id=1, source_target_pairs={{0,4},{1,5},{2,6},{3,7},{4,0},{5,1},{6,2},{7,3},{8,12},{9,13},{10,... | collective-permute-start | bytes 786440 | tf_op jit(solution)/shard_map/ppermute | solution.py:17

commit v4 on v3

--- a/solution.py
+++ b/solution.py
@@ -143,11 +143,10 @@
         ]
         gate_sums, outs = [], []
         for h in range(CHUNKS):
-            earlier = tuple(steps[0] for steps in slabs[:h])
-            gate_sums.append(contract_last(after(gates[h], *earlier), gate_weight))
+            gate_sums.append(contract_last(gates[h], gate_weight))
         for h in range(CHUNKS):
             up_all = gather(after(grads[h][1], gate_sums[h]))
-            earlier = tuple(steps[min(h + 1 - n, len(steps) - 1)] for n, steps in enumerate(slabs[: h + 2]))
+            earlier = [slabs[n][h - n] for n in range(h + 1)]
             outs.append(scatter(gate_sums[h] + contract_last(after(up_all, *earlier), up_weight)))
         factor = lax.dot_general(
             jnp.concatenate([steps[-1] for steps in slabs], axis=0),

time: 331 us -> 354 us (1.069)
  waiting for transfers between devices: 144 us -> 157 us
  starting transfers between devices: 53.9 us -> 58.2 us
    ppermute x6, waiting for transfers between devices: 37.4 us -> 64.7 us  [broadcast(): arrived = lax.ppermute(slab, ('row', 'col'), pairs)]
    ppermute x36, waiting for transfers between devices: 106 us -> 92.5 us  [swap(): return lax.ppermute(block, axis, [(i, i ^ bit) for i in range(size)])]
    ppermute x36, starting transfers between devices: 37 us -> 41.2 us  [swap(): return lax.ppermute(block, axis, [(i, i ^ bit) for i in range(size)])]
    unnamed x64 -> x68, local copies, waits for them, and re-layouts: 18.4 us -> 20.3 us
  transfers between devices with their start and end apart: 42 -> 42, of which waited for: 22 -> 20; matrix products, arithmetic and copies ran while one was open for 32% -> 32% of each run, Pallas kernels for 0% -> 0%
where the time goes in v4:
time: 354 us; the launch traced here: 353 us
  waiting for transfers between devices  157 us (44%)
  matrix products  84.5 us (24%)
  starting transfers between devices  58.2 us (16%)
  local copies, waits for them, and re-layouts  30.7 us (9%)
  other arithmetic  21.7 us (6%)
    ppermute x36, waiting for transfers between devices, swap(): return lax.ppermute(block, axis, [(i, i ^ bit) for i in range(size)])  92.5 us
    dot_general x6, matrix products, contract_last(): lax.dot_general(left, right, (((1,), (1,)), ((), ())), preferred_element_...  72.7 us
    ppermute x6, waiting for transfers between devices, broadcast(): arrived = lax.ppermute(slab, ('row', 'col'), pairs)  64.7 us
    ppermute x36, starting transfers between devices, swap(): return lax.ppermute(block, axis, [(i, i ^ bit) for i in range(size)])  41.2 us
    unnamed x68, local copies, waits for them, and re-layouts  20.3 us
    ppermute x6, starting transfers between devices, broadcast(): arrived = lax.ppermute(slab, ('row', 'col'), pairs)  17 us
    dot_general x1, matrix products, shards(): lax.dot_general(jnp.concatenate([steps[-1] for steps in slabs], axis=0),...  11.9 us
    convert_element_type x2, other arithmetic, swiglu_grads(): grad_up = (hidden_grad * gate_float * logistic).astype(jnp.bfloat16)  8.96 us
  transfers between devices with their start and end apart: 42, of which 20 were waited for; matrix products, arithmetic and copies ran while one was open for 32% of the time, Pallas kernels for 0%

profile of v4, /device:TPU:0, one launch (start us, length us, event | category | flops | bytes accessed | tf_op | source)
XLA Modules:
  0.0 353.4 jit_solution(13282922670156762610)
XLA Ops:
  0.6 2.0 fusion.32
  2.6 4.0 %collective-permute-start.3 = (bf16[64,2048]{1,0:T(8,128)(2,1)}, bf16[64,2048]{1,0:T(8,128)(2,1)S(1)}, u32[]{:S(2)}, u32[]{:S(2)}) collective-permute-start(bf16[64,2048]{1,0:T(8,128)(2,1)} %get-tuple-element.32), channel_id=1, source_target_pairs={{0,4},{1,5},{2,6},{3,7},{4,0},{5,1},{6,2},{7,3},{8,12},{9,13},{10,... | collective-permute-start | bytes 786440 | tf_op jit(solution)/shard_map/ppermute | solution.py:17
  6.6 1.5 collective-permute-start
  8.1 1.6 collective-permute-start.1
  10.5 10.0 %collective-permute-done.3 = bf16[64,2048]{1,0:T(8,128)(2,1)S(1)} collective-permute-done((bf16[64,2048]{1,0:T(8,128)(2,1)}, bf16[64,2048]{1,0:T(8,128)(2,1)S(1)}, u32[]{:S(2)}, u32[]{:S(2)}) %collective-permute-start.3) | collective-permute-done | bytes 262176 | tf_op jit(solution)/shard_map/ppermute | solution.py:17
  20.5 5.6 %collective-permute-start.19 = (bf16[64,2048]{1,0:T(8,128)(2,1)}, bf16[64,2048]{1,0:T(8,128)(2,1)S(1)}, u32[]{:S(2)}, u32[]{:S(2)}) collective-permute-start(bf16[64,2048]{1,0:T(8,128)(2,1)} %get-tuple-element.35), channel_id=1, source_target_pairs={{0,1},{1,0},{2,3},{3,2},{4,5},{5,4},{6,7},{7,6},{8,9},{9,8},{10,11... | collective-permute-start | bytes 786440 | tf_op jit(solution)/shard_map/ppermute | solution.py:17
  27.5 2.6 collective-permute-done.22
  30.2 1.5 collective-permute-start.2
  33.9 5.0 %collective-permute-done.5 = bf16[64,2048]{1,0:T(8,128)(2,1)S(1)} collective-permute-done((bf16[64,2048]{1,0:T(8,128)(2,1)S(1)}, bf16[64,2048]{1,0:T(8,128)(2,1)S(1)}, u32[]{:S(2)}, u32[]{:S(2)}) %collective-permute-start.5) | collective-permute-done | bytes 262176 | tf_op jit(solution)/shard_map/ppermute | solution.py:17
  39.5 1.3 collective-permute-done.2
  40.8 2.5 collective-permute-start.6
  46.2 5.8 %collective-permute-done.21 = bf16[64,2048]{1,0:T(8,128)(2,1)S(1)} collective-permute-done((bf16[64,2048]{1,0:T(8,128)(2,1)S(1)}, bf16[64,2048]{1,0:T(8,128)(2,1)S(1)}, u32[]{:S(2)}, u32[]{:S(2)}) %collective-permute-start.21) | collective-permute-done | bytes 262176 | tf_op jit(solution)/shard_map/ppermute | solution.py:17
  52.1 5.5 %collective-permute-done.6 = bf16[64,2048]{1,0:T(8,128)(2,1)S(1)} collective-permute-done((bf16[64,2048]{1,0:T(8,128)(2,1)S(1)}, bf16[64,2048]{1,0:T(8,128)(2,1)S(1)}, u32[]{:S(2)}, u32[]{:S(2)}) %collective-permute-start.6) | collective-permute-done | bytes 262176 | tf_op jit(solution)/shard_map/ppermute | solution.py:17
  58.3 3.2 collective-permute-done.25
  63.7 11.3 %fusion.33 = f32[512,3584]{1,0:T(8,128)S(1)} fusion(bf16[512,2048]{1,0:T(8,128)(2,1)S(1)} %dynamic-slice_dynamic-update-slice_fusion.8, bf16[3584,2048]{1,0:T(8,128)(2,1)} %param.11), kind=kOutput, calls=%fused_computation.123 | convolution fusion | flops 7516192768 | bytes 24117248 | tf_op jit(solution)/shard_map/dot_general | solution.py:11
  75.6 3.5 collective-permute-done.7
  79.1 1.2 fusion.20
  80.3 2.1 collective-permute-start.8
  82.3 11.3 %fusion.34 = f32[512,3584]{1,0:T(8,128)S(1)} fusion(bf16[512,2048]{1,0:T(8,128)(2,1)S(1)} %dynamic-slice_dynamic-update-slice_fusion, bf16[3584,2048]{1,0:T(8,128)(2,1)} %param.11), kind=kOutput, calls=%fused_computation.124 | convolution fusion | flops 7516192768 | bytes 24117248 | tf_op jit(solution)/shard_map/dot_general | solution.py:11
  93.6 3.0 copy-done
  96.7 1.5 slice.214
  99.4 1.9 fusion.30
  101.3 2.0 collective-permute-done.8
  103.3 4.7 %fusion.8 = (bf16[128,3584]{1,0:T(8,128)(2,1)}, bf16[128,3584]{1,0:T(8,128)(2,1)S(1)}) fusion(bf16[2,1,64,3584]{3,2,1,0:T(8,128)(2,1)} %get-tuple-element.39, bf16[128,3584]{1,0:T(8,128)(2,1)} %collective-permute-done.8, bf16[256,3584]{1,0:T(8,128)(2,1)} %copy-done.11, f32[512,3584]{1,0:T(8,128)} %copy-done.1, bf16[2,1,64,3584]{3,2,1,0:T(8,128)(2,1)} %get-tuple-element.28), kind=kLoop, calls=%fused_computation.23 | loop fusion | flops 8716288 | bytes 7340032 | tf_op jit(solution)/shard_map/convert_element_type | solution.py:76
  108.0 1.7 collective-permute-start.10
  109.8 1.1 constant_dynamic-update-slice_fusion.23
  110.9 2.3 fusion.18
  113.4 17.9 %collective-permute-done.10 = bf16[128,3584]{1,0:T(8,128)(2,1)S(1)} collective-permute-done((bf16[128,3584]{1,0:T(8,128)(2,1)S(1)}, bf16[128,3584]{1,0:T(8,128)(2,1)S(1)}, u32[]{:S(2)}, u32[]{:S(2)}) %collective-permute-start.10) | collective-permute-done | bytes 917536 | tf_op jit(solution)/shard_map/ppermute | solution.py:17
  134.3 13.0 %fusion.29 = f32[512,2048]{1,0:T(8,128)} fusion(bf16[2048,3584]{1,0:T(8,128)(2,1)} %param.9, bf16[128,3584]{1,0:T(8,128)(2,1)} %collective-permute-done.11, bf16[128,3584]{1,0:T(8,128)(2,1)S(1)} %collective-permute-done.10, bf16[128,3584]{1,0:T(8,128)(2,1)} %copy-done.5, bf16[128,3584]{1,0:T(8,128)(2,1)S(1)} %get-tuple-element.13), kind=kOutput, calls=%fused_computation.119 | convolution fusion | flops 7530872832 | bytes 22544384 | tf_op jit(solution)/shard_map/dot_general | solution.py:11
  147.2 1.8 collective-permute-start.13
  149.7 4.2 %fusion.17 = (bf16[128,3584]{1,0:T(8,128)(2,1)}, bf16[128,3584]{1,0:T(8,128)(2,1)S(1)}) fusion(bf16[2,1,64,3584]{3,2,1,0:T(8,128)(2,1)} %get-tuple-element.38, bf16[128,3584]{1,0:T(8,128)(2,1)} %collective-permute-done.27, bf16[256,3584]{1,0:T(8,128)(2,1)} %collective-permute-done.26, f32[512,3584]{1,0:T(8,128)S(1)} %bitcast.36, ...), kind=kLoop, calls=%fused_computation.32 | loop fusion | flops 8716288 | bytes 7340032 | tf_op jit(solution)/shard_map/convert_element_type | solution.py:76
  153.9 1.4 collective-permute-start.29
  155.3 1.3 pad_maximum_fusion
  157.2 3.5 collective-permute-start.15
  160.7 2.2 constant_dynamic-update-slice_fusion.20
  162.9 1.0 constant_dynamic-update-slice_fusion.19
  163.9 17.0 %collective-permute-done.15 = bf16[512,896]{1,0:T(8,128)(2,1)S(1)} collective-permute-done((bf16[512,896]{1,0:T(8,128)(2,1)S(1)}, bf16[512,896]{1,0:T(8,128)(2,1)S(1)}, u32[]{:S(2)}, u32[]{:S(2)}) %collective-permute-start.15) | collective-permute-done | bytes 917536 | tf_op jit(solution)/shard_map/ppermute | solution.py:101
  181.4 2.2 collective-permute-start.34
  183.7 6.2 %collective-permute-done.29 = bf16[128,3584]{1,0:T(8,128)(2,1)S(1)} collective-permute-done((bf16[128,3584]{1,0:T(8,128)(2,1)S(1)}, bf16[128,3584]{1,0:T(8,128)(2,1)S(1)}, u32[]{:S(2)}, u32[]{:S(2)}) %collective-permute-start.29) | collective-permute-done | bytes 917536 | tf_op jit(solution)/shard_map/ppermute | solution.py:17
  189.9 1.0 constant_dynamic-update-slice_fusion.18
  190.9 1.0 constant_dynamic-update-slice_fusion.17
  192.3 12.4 %fusion.28 = f32[512,2048]{1,0:T(8,128)} fusion(bf16[2048,3584]{1,0:T(8,128)(2,1)} %param.9, bf16[128,3584]{1,0:T(8,128)(2,1)S(1)} %collective-permute-done.30, bf16[128,3584]{1,0:T(8,128)(2,1)S(1)} %collective-permute-done.29, bf16[128,3584]{1,0:T(8,128)(2,1)S(1)} %collective-permute-done.28, bf16[128,3584]{1,0:T(8,128)(2,1)S(1)} %get-tuple-element.15), kind=kOutput, calls=%fused_computation.118 | convolution fusion | flops 7530872832 | bytes 22544384 | tf_op jit(solution)/shard_map/dot_general | solution.py:11
  204.7 1.7 collective-permute-start.32
  206.5 1.9 pad_maximum_fusion.1
  208.4 11.7 %convolution_add_fusion.1 = f32[512,2048]{1,0:T(8,128)S(1)} fusion(f32[512,2048]{1,0:T(8,128)} %fusion.29, bf16[512,3584]{1,0:T(8,128)(2,1)S(1)} %pad_maximum_fusion.1, bf16[2048,3584]{1,0:T(8,128)(2,1)} %param.10), kind=kOutput, calls=%fused_computation.8 | convolution fusion | flops 7517241344 | bytes 26738688 | tf_op jit(solution)/shard_map/dot_general | solution.py:11
  220.3 1.6 collective-permute-start.16
  222.7 2.5 collective-permute-start.35
  225.3 2.2 collective-permute-start.39
  227.6 1.0 constant_dynamic-update-slice_fusion.16
  228.7 35.9 %collective-permute-done.35 = bf16[512,896]{1,0:T(8,128)(2,1)S(1)} collective-permute-done((bf16[512,896]{1,0:T(8,128)(2,1)S(1)}, bf16[512,896]{1,0:T(8,128)(2,1)S(1)}, u32[]{:S(2)}, u32[]{:S(2)}) %collective-permute-start.35) | collective-permute-done | bytes 917536 | tf_op jit(solution)/shard_map/ppermute | solution.py:101
  265.2 2.2 collective-permute-start.40
  267.4 1.1 fusion.25
  268.6 1.6 pad_maximum_fusion.3
  270.2 13.1 %convolution_add_fusion = f32[512,2048]{1,0:T(8,128)} fusion(f32[512,2048]{1,0:T(8,128)} %fusion.28, bf16[512,3584]{1,0:T(8,128)(2,1)S(1)} %pad_maximum_fusion.3, bf16[2048,3584]{1,0:T(8,128)(2,1)} %param.10), kind=kOutput, calls=%fused_computation.7 | convolution fusion | flops 7517241344 | bytes 26738688 | tf_op jit(solution)/shard_map/dot_general | solution.py:11
  283.3 1.6 dynamic-slice_convert_fusion.3
  285.0 2.6 collective-permute-start.36
  287.7 10.0 %collective-permute-done.17 = bf16[128,2048]{1,0:T(8,128)(2,1)S(1)} collective-permute-done((bf16[128,2048]{1,0:T(8,128)(2,1)}, bf16[128,2048]{1,0:T(8,128)(2,1)S(1)}, u32[]{:S(2)}, u32[]{:S(2)}) %collective-permute-start.17) | collective-permute-done | bytes 524320 | tf_op jit(solution)/shard_map/ppermute | solution.py:17
  298.0 4.3 %collective-permute-start.41 = (bf16[512,896]{1,0:T(8,128)(2,1)S(1)}, bf16[512,896]{1,0:T(8,128)(2,1)S(1)}, u32[]{:S(2)}, u32[]{:S(2)}) collective-permute-start(bf16[512,896]{1,0:T(8,128)(2,1)S(1)} %broadcast_select_fusion.2), channel_id=1, source_target_pairs={{0,2},{1,3},{4,6},{5,7},{8,10},{9,11},{12,14},{13,15},{16,18},{17,... | collective-permute-start | bytes 2752520 | tf_op jit(solution)/shard_map/ppermute | solution.py:101
  302.4 8.2 %collective-permute-done.36 = bf16[256,2048]{1,0:T(8,128)(2,1)S(1)} collective-permute-done((bf16[256,2048]{1,0:T(8,128)(2,1)S(1)}, bf16[256,2048]{1,0:T(8,128)(2,1)S(1)}, u32[]{:S(2)}, u32[]{:S(2)}) %collective-permute-start.36) | collective-permute-done | bytes 1048608 | tf_op jit(solution)/shard_map/ppermute | solution.py:17
  310.7 1.7 collective-permute-start.37
  312.6 11.7 %collective-permute-done.41 = bf16[512,896]{1,0:T(8,128)(2,1)S(1)} collective-permute-done((bf16[512,896]{1,0:T(8,128)(2,1)S(1)}, bf16[512,896]{1,0:T(8,128)(2,1)S(1)}, u32[]{:S(2)}, u32[]{:S(2)}) %collective-permute-start.41) | collective-permute-done | bytes 917536 | tf_op jit(solution)/shard_map/ppermute | solution.py:101
  324.4 9.6 %collective-permute-done.37 = bf16[128,2048]{1,0:T(8,128)(2,1)S(1)} collective-permute-done((bf16[128,2048]{1,0:T(8,128)(2,1)S(1)}, bf16[128,2048]{1,0:T(8,128)(2,1)S(1)}, u32[]{:S(2)}, u32[]{:S(2)}) %collective-permute-start.37) | collective-permute-done | bytes 524320 | tf_op jit(solution)/shard_map/ppermute | solution.py:17
  334.1 6.5 %collective-permute-start.38 = (bf16[64,2048]{1,0:T(8,128)(2,1)S(1)}, bf16[64,2048]{1,0:T(8,128)(2,1)S(1)}, u32[]{:S(2)}, u32[]{:S(2)}) collective-permute-start(bf16[64,2048]{1,0:T(8,128)(2,1)S(1)} %add_convert_fusion.1), channel_id=1, source_target_pairs={{0,4},{1,5},{2,6},{3,7},{4,0},{5,1},{6,2},{7,3},{8,12},{9,13},{10,... | collective-permute-start | bytes 786440 | tf_op jit(solution)/shard_map/ppermute | solution.py:17
  340.6 11.9 %convolution_multiply_fusion = f32[896,3584]{1,0:T(8,128)} fusion(bf16[1024,3584]{1,0:T(8,128)(2,1)} %constant_dynamic-update-slice_fusion.16, bf16[512,896]{1,0:T(8,128)(2,1)S(1)} %broadcast_select_fusion, bf16[512,896]{1,0:T(8,128)(2,1)S(1)} %broadcast_select_fusion.1), kind=kOutput, calls=%fused_computation | convolution fusion | flops 6583549952 | bytes 22020096 | tf_op jit(solution)/shard_map/dot_general | solution.py:151
  (134 shorter events, 22.0 us)
Async XLA Ops:
  2.6 17.9 %collective-permute-start.3 = (bf16[64,2048]{1,0:T(8,128)(2,1)}, bf16[64,2048]{1,0:T(8,128)(2,1)S(1)}, u32[]{:S(2)}, u32[]{:S(2)}) collective-permute-start(bf16[64,2048]{1,0:T(8,128)(2,1)} %get-tuple-element.32), channel_id=1, source_target_pairs={{0,4},{1,5},{2,6},{3,7},{4,0},{5,1},{6,2},{7,3},{8,12},{9,13},{10,... | collective-permute-start | bytes 786440 | tf_op jit(solution)/shard_map/ppermute | solution.py:17
  6.6 19.4 %collective-permute-start = (bf16[64,2048]{1,0:T(8,128)(2,1)}, bf16[64,2048]{1,0:T(8,128)(2,1)S(1)}, u32[]{:S(2)}, u32[]{:S(2)}) collective-permute-start(bf16[64,2048]{1,0:T(8,128)(2,1)} %get-tuple-element.32), channel_id=1, source_target_pairs={{0,1},{1,0},{2,3},{3,2},{4,5},{5,4},{6,7},{7,6},{8,9},{9,8},{10,11... | collective-permute-start | bytes 786440 | tf_op jit(solution)/shard_map/ppermute | solution.py:17
  8.1 18.7 %collective-permute-start.1 = (bf16[64,2048]{1,0:T(8,128)(2,1)}, bf16[64,2048]{1,0:T(8,128)(2,1)S(1)}, u32[]{:S(2)}, u32[]{:S(2)}) collective-permute-start(bf16[64,2048]{1,0:T(8,128)(2,1)} %get-tuple-element.32), channel_id=1, source_target_pairs={{0,2},{1,3},{2,0},{3,1},{4,6},{5,7},{6,4},{7,5},{8,10},{9,11},{10,... | collective-permute-start | bytes 786440 | tf_op jit(solution)/shard_map/ppermute | solution.py:17
  9.7 20.4 %collective-permute-start.22 = (bf16[64,2048]{1,0:T(8,128)(2,1)}, bf16[64,2048]{1,0:T(8,128)(2,1)S(1)}, u32[]{:S(2)}, u32[]{:S(2)}) collective-permute-start(bf16[64,2048]{1,0:T(8,128)(2,1)} %get-tuple-element.35), channel_id=1, source_target_pairs={{0,4},{1,5},{2,6},{3,7},{4,0},{5,1},{6,2},{7,3},{8,12},{9,13},{10,... | collective-permute-start | bytes 786440 | tf_op jit(solution)/shard_map/ppermute | solution.py:17
  10.0 23.2 %collective-permute-start.20 = (bf16[64,2048]{1,0:T(8,128)(2,1)}, bf16[64,2048]{1,0:T(8,128)(2,1)S(1)}, u32[]{:S(2)}, u32[]{:S(2)}) collective-permute-start(bf16[64,2048]{1,0:T(8,128)(2,1)} %get-tuple-element.35), channel_id=1, source_target_pairs={{0,2},{1,3},{2,0},{3,1},{4,6},{5,7},{6,4},{7,5},{8,10},{9,11},{10,... | collective-permute-start | bytes 786440 | tf_op jit(solution)/shard_map/ppermute | solution.py:17
  20.5 11.2 %collective-permute-start.19 = (bf16[64,2048]{1,0:T(8,128)(2,1)}, bf16[64,2048]{1,0:T(8,128)(2,1)S(1)}, u32[]{:S(2)}, u32[]{:S(2)}) collective-permute-start(bf16[64,2048]{1,0:T(8,128)(2,1)} %get-tuple-element.35), channel_id=1, source_target_pairs={{0,1},{1,0},{2,3},{3,2},{4,5},{5,4},{6,7},{7,6},{8,9},{9,8},{10,11... | collective-permute-start | bytes 786440 | tf_op jit(solution)/shard_map/ppermute | solution.py:17
  26.1 12.8 %collective-permute-start.5 = (bf16[64,2048]{1,0:T(8,128)(2,1)S(1)}, bf16[64,2048]{1,0:T(8,128)(2,1)S(1)}, u32[]{:S(2)}, u32[]{:S(2)}) collective-permute-start(bf16[64,2048]{1,0:T(8,128)(2,1)S(1)} %collective-permute-done.3), channel_id=1, source_target_pairs={{0,2},{1,3},{2,0},{3,1},{4,6},{5,7},{6,4},{7,5},{8,10},{9,11},{10,... | collective-permute-start | bytes 786440 | tf_op jit(solution)/shard_map/ppermute | solution.py:17
  26.8 18.0 %collective-permute-start.4 = (bf16[64,2048]{1,0:T(8,128)(2,1)S(1)}, bf16[64,2048]{1,0:T(8,128)(2,1)S(1)}, u32[]{:S(2)}, u32[]{:S(2)}) collective-permute-start(bf16[64,2048]{1,0:T(8,128)(2,1)S(1)} %collective-permute-done.3), channel_id=1, source_target_pairs={{0,1},{1,0},{2,3},{3,2},{4,5},{5,4},{6,7},{7,6},{8,9},{9,8},{10,11... | collective-permute-start | bytes 786440 | tf_op jit(solution)/shard_map/ppermute | solution.py:17
  30.2 10.6 %collective-permute-start.2 = (bf16[64,2048]{1,0:T(8,128)(2,1)S(1)}, bf16[64,2048]{1,0:T(8,128)(2,1)S(1)}, u32[]{:S(2)}, u32[]{:S(2)}) collective-permute-start(bf16[64,2048]{1,0:T(8,128)(2,1)S(1)} %collective-permute-done.1), channel_id=1, source_target_pairs={{0,1},{1,0},{2,3},{3,2},{4,5},{5,4},{6,7},{7,6},{8,9},{9,8},{10,11... | collective-permute-start | bytes 786440 | tf_op jit(solution)/shard_map/ppermute | solution.py:17
  31.7 11.5 %collective-permute-start.24 = (bf16[64,2048]{1,0:T(8,128)(2,1)S(1)}, bf16[64,2048]{1,0:T(8,128)(2,1)S(1)}, u32[]{:S(2)}, u32[]{:S(2)}) collective-permute-start(bf16[64,2048]{1,0:T(8,128)(2,1)S(1)} %collective-permute-done.22), channel_id=1, source_target_pairs={{0,2},{1,3},{2,0},{3,1},{4,6},{5,7},{6,4},{7,5},{8,10},{9,11},{10,... | collective-permute-start | bytes 786440 | tf_op jit(solution)/shard_map/ppermute | solution.py:17
  33.3 18.8 %collective-permute-start.23 = (bf16[64,2048]{1,0:T(8,128)(2,1)S(1)}, bf16[64,2048]{1,0:T(8,128)(2,1)S(1)}, u32[]{:S(2)}, u32[]{:S(2)}) collective-permute-start(bf16[64,2048]{1,0:T(8,128)(2,1)S(1)} %collective-permute-done.22), channel_id=1, source_target_pairs={{0,1},{1,0},{2,3},{3,2},{4,5},{5,4},{6,7},{7,6},{8,9},{9,8},{10,11... | collective-permute-start | bytes 786440 | tf_op jit(solution)/shard_map/ppermute | solution.py:17
  38.9 13.1 %collective-permute-start.21 = (bf16[64,2048]{1,0:T(8,128)(2,1)S(1)}, bf16[64,2048]{1,0:T(8,128)(2,1)S(1)}, u32[]{:S(2)}, u32[]{:S(2)}) collective-permute-start(bf16[64,2048]{1,0:T(8,128)(2,1)S(1)} %collective-permute-done.20), channel_id=1, source_target_pairs={{0,1},{1,0},{2,3},{3,2},{4,5},{5,4},{6,7},{7,6},{8,9},{9,8},{10,11... | collective-permute-start | bytes 786440 | tf_op jit(solution)/shard_map/ppermute | solution.py:17
  40.8 16.9 %collective-permute-start.6 = (bf16[64,2048]{1,0:T(8,128)(2,1)S(1)}, bf16[64,2048]{1,0:T(8,128)(2,1)S(1)}, u32[]{:S(2)}, u32[]{:S(2)}) collective-permute-start(bf16[64,2048]{1,0:T(8,128)(2,1)S(1)} %collective-permute-done.5), channel_id=1, source_target_pairs={{0,1},{1,0},{2,3},{3,2},{4,5},{5,4},{6,7},{7,6},{8,9},{9,8},{10,11... | collective-permute-start | bytes 786440 | tf_op jit(solution)/shard_map/ppermute | solution.py:17
  43.2 18.3 %collective-permute-start.25 = (bf16[64,2048]{1,0:T(8,128)(2,1)S(1)}, bf16[64,2048]{1,0:T(8,128)(2,1)S(1)}, u32[]{:S(2)}, u32[]{:S(2)}) collective-permute-start(bf16[64,2048]{1,0:T(8,128)(2,1)S(1)} %collective-permute-done.24), channel_id=1, source_target_pairs={{0,1},{1,0},{2,3},{3,2},{4,5},{5,4},{6,7},{7,6},{8,9},{9,8},{10,11... | collective-permute-start | bytes 786440 | tf_op jit(solution)/shard_map/ppermute | solution.py:17
  58.3 5.2 %copy-start.7 = (bf16[512,2048]{1,0:T(8,128)(2,1)S(1)}, bf16[512,2048]{1,0:T(8,128)(2,1)}, u32[]{:S(2)}) copy-start(bf16[512,2048]{1,0:T(8,128)(2,1)} %constant_dynamic-update-slice_fusion) | copy-start | bytes 6291460
  75.0 5.2 %copy-start.1 = (f32[512,3584]{1,0:T(8,128)}, f32[512,3584]{1,0:T(8,128)S(1)}, u32[]{:S(2)}) copy-start(f32[512,3584]{1,0:T(8,128)S(1)} %fusion.33) | copy-start | bytes 22020100
  75.2 3.9 %collective-permute-start.7 = (bf16[256,3584]{1,0:T(8,128)(2,1)S(1)}, bf16[256,3584]{1,0:T(8,128)(2,1)S(1)}, u32[]{:S(2)}, u32[]{:S(2)}) collective-permute-start(bf16[256,3584]{1,0:T(8,128)(2,1)S(1)} %slice.215), channel_id=1, source_target_pairs={{0,8},{8,0},{16,24},{24,16},{1,9},{9,1},{17,25},{25,17},{2,10},{10... | collective-permute-start | bytes 5505032 | tf_op jit(solution)/shard_map/ppermute | solution.py:17
  79.1 3.2 copy-start.11
  80.3 23.0 %collective-permute-start.8 = (bf16[128,3584]{1,0:T(8,128)(2,1)}, bf16[128,3584]{1,0:T(8,128)(2,1)}, u32[]{:S(2)}, u32[]{:S(2)}) collective-permute-start(bf16[128,3584]{1,0:T(8,128)(2,1)} %fusion.20), channel_id=1, source_target_pairs={{0,16},{8,24},{16,0},{24,8},{1,17},{9,25},{17,1},{25,9},{2,18},{10... | collective-permute-start | bytes 2752520 | tf_op jit(solution)/shard_map/ppermute | solution.py:17
  93.6 3.1 copy-start
  96.7 2.2 copy-start.9
  96.7 2.7 copy-start.10
  98.1 12.7 %collective-permute-start.26 = (bf16[256,3584]{1,0:T(8,128)(2,1)}, bf16[256,3584]{1,0:T(8,128)(2,1)}, u32[]{:S(2)}, u32[]{:S(2)}) collective-permute-start(bf16[256,3584]{1,0:T(8,128)(2,1)} %slice.214), channel_id=1, source_target_pairs={{0,8},{8,0},{16,24},{24,16},{1,9},{9,1},{17,25},{25,17},{2,10},{10... | collective-permute-start | bytes 5505032 | tf_op jit(solution)/shard_map/ppermute | solution.py:17
  99.4 11.5 %slice-start = ((s8[7340032]{0:T(1024)(128)(4,1)}), s8[3145728]{0:T(1024)(128)(4,1)S(1)}, s32[]{:S(2)}) async-start(s8[7340032]{0:T(1024)(128)(4,1)} %bitcast.35), calls=%async_computation | async-start | bytes 6291456
  103.3 7.6 %slice-start.1 = ((s8[7340032]{0:T(1024)(128)(4,1)}), s8[4194304]{0:T(1024)(128)(4,1)S(1)}, s32[]{:S(2)}) async-start(s8[7340032]{0:T(1024)(128)(4,1)} %bitcast.35), calls=%async_computation.1 | async-start | bytes 8388608
  108.0 23.3 %collective-permute-start.10 = (bf16[128,3584]{1,0:T(8,128)(2,1)S(1)}, bf16[128,3584]{1,0:T(8,128)(2,1)S(1)}, u32[]{:S(2)}, u32[]{:S(2)}) collective-permute-start(bf16[128,3584]{1,0:T(8,128)(2,1)S(1)} %get-tuple-element.13), channel_id=1, source_target_pairs={{0,16},{8,24},{16,0},{24,8},{1,17},{9,25},{17,1},{25,9},{2,18},{10... | collective-permute-start | bytes 2752520 | tf_op jit(solution)/shard_map/ppermute | solution.py:17
  109.8 21.5 %collective-permute-start.9 = (bf16[128,3584]{1,0:T(8,128)(2,1)S(1)}, bf16[128,3584]{1,0:T(8,128)(2,1)S(1)}, u32[]{:S(2)}, u32[]{:S(2)}) collective-permute-start(bf16[128,3584]{1,0:T(8,128)(2,1)S(1)} %get-tuple-element.13), channel_id=1, source_target_pairs={{0,8},{8,0},{16,24},{24,16},{1,9},{9,1},{17,25},{25,17},{2,10},{10... | collective-permute-start | bytes 2752520 | tf_op jit(solution)/shard_map/ppermute | solution.py:17
  113.1 36.6 %collective-permute-start.27 = (bf16[128,3584]{1,0:T(8,128)(2,1)}, bf16[128,3584]{1,0:T(8,128)(2,1)}, u32[]{:S(2)}, u32[]{:S(2)}) collective-permute-start(bf16[128,3584]{1,0:T(8,128)(2,1)} %fusion.18), channel_id=1, source_target_pairs={{0,16},{8,24},{16,0},{24,8},{1,17},{9,25},{17,1},{25,9},{2,18},{10... | collective-permute-start | bytes 2752520 | tf_op jit(solution)/shard_map/ppermute | solution.py:17
  131.3 15.9 %copy-start.3 = (bf16[128,3584]{1,0:T(8,128)(2,1)}, bf16[128,3584]{1,0:T(8,128)(2,1)S(1)}, u32[]{:S(2)}) copy-start(bf16[128,3584]{1,0:T(8,128)(2,1)S(1)} %collective-permute-done.10) | copy-start | bytes 2752516
  131.3 3.0 collective-permute-start.11
  131.3 1.0 copy-start.5
  147.2 36.4 %collective-permute-start.13 = (bf16[128,3584]{1,0:T(8,128)(2,1)}, bf16[128,3584]{1,0:T(8,128)(2,1)}, u32[]{:S(2)}, u32[]{:S(2)}) collective-permute-start(bf16[128,3584]{1,0:T(8,128)(2,1)} %get-tuple-element.7), channel_id=1, source_target_pairs={{0,16},{8,24},{16,0},{24,8},{1,17},{9,25},{17,1},{25,9},{2,18},{10... | collective-permute-start | bytes 2752520 | tf_op jit(solution)/shard_map/ppermute | solution.py:17
  149.0 57.5 %collective-permute-start.12 = (bf16[128,3584]{1,0:T(8,128)(2,1)}, bf16[128,3584]{1,0:T(8,128)(2,1)}, u32[]{:S(2)}, u32[]{:S(2)}) collective-permute-start(bf16[128,3584]{1,0:T(8,128)(2,1)} %get-tuple-element.7), channel_id=1, source_target_pairs={{0,8},{8,0},{16,24},{24,16},{1,9},{9,1},{17,25},{25,17},{2,10},{10... | collective-permute-start | bytes 2752520 | tf_op jit(solution)/shard_map/ppermute | solution.py:17
  149.7 5.7 %copy-start.4 = (bf16[128,3584]{1,0:T(8,128)(2,1)S(1)}, bf16[128,3584]{1,0:T(8,128)(2,1)}, u32[]{:S(2)}) copy-start(bf16[128,3584]{1,0:T(8,128)(2,1)} %copy-done.3) | copy-start | bytes 2752516
  149.7 5.7 %copy-start.6 = (bf16[128,3584]{1,0:T(8,128)(2,1)S(1)}, bf16[128,3584]{1,0:T(8,128)(2,1)}, u32[]{:S(2)}) copy-start(bf16[128,3584]{1,0:T(8,128)(2,1)} %copy-done.5) | copy-start | bytes 2752516
  153.9 36.0 %collective-permute-start.29 = (bf16[128,3584]{1,0:T(8,128)(2,1)S(1)}, bf16[128,3584]{1,0:T(8,128)(2,1)S(1)}, u32[]{:S(2)}, u32[]{:S(2)}) collective-permute-start(bf16[128,3584]{1,0:T(8,128)(2,1)S(1)} %get-tuple-element.15), channel_id=1, source_target_pairs={{0,16},{8,24},{16,0},{24,8},{1,17},{9,25},{17,1},{25,9},{2,18},{10... | collective-permute-start | bytes 2752520 | tf_op jit(solution)/shard_map/ppermute | solution.py:17
  155.3 34.5 %collective-permute-start.28 = (bf16[128,3584]{1,0:T(8,128)(2,1)S(1)}, bf16[128,3584]{1,0:T(8,128)(2,1)S(1)}, u32[]{:S(2)}, u32[]{:S(2)}) collective-permute-start(bf16[128,3584]{1,0:T(8,128)(2,1)S(1)} %get-tuple-element.15), channel_id=1, source_target_pairs={{0,8},{8,0},{16,24},{24,16},{1,9},{9,1},{17,25},{25,17},{2,10},{10... | collective-permute-start | bytes 2752520 | tf_op jit(solution)/shard_map/ppermute | solution.py:17
  157.2 23.7 %collective-permute-start.15 = (bf16[512,896]{1,0:T(8,128)(2,1)S(1)}, bf16[512,896]{1,0:T(8,128)(2,1)S(1)}, u32[]{:S(2)}, u32[]{:S(2)}) collective-permute-start(bf16[512,896]{1,0:T(8,128)(2,1)S(1)} %constant_dynamic-slice_fusion.5), channel_id=1, source_target_pairs={{0,1},{8,9},{16,17},{24,25}} | collective-permute-start | bytes 2752520 | tf_op jit(solution)/shard_map/ppermute | solution.py:101
  181.4 43.8 %collective-permute-start.34 = (bf16[512,896]{1,0:T(8,128)(2,1)S(1)}, bf16[512,896]{1,0:T(8,128)(2,1)}, u32[]{:S(2)}, u32[]{:S(2)}) collective-permute-start(bf16[512,896]{1,0:T(8,128)(2,1)S(1)} %broadcast_select_fusion.5), channel_id=1, source_target_pairs={{0,4},{1,5},{8,12},{9,13},{16,20},{17,21},{24,28},{25,29}} | collective-permute-start | bytes 2752520 | tf_op jit(solution)/shard_map/ppermute | solution.py:101
  183.7 22.8 %collective-permute-start.14 = (bf16[128,3584]{1,0:T(8,128)(2,1)}, bf16[128,3584]{1,0:T(8,128)(2,1)S(1)}, u32[]{:S(2)}, u32[]{:S(2)}) collective-permute-start(bf16[128,3584]{1,0:T(8,128)(2,1)} %collective-permute-done.13), channel_id=1, source_target_pairs={{0,8},{8,0},{16,24},{24,16},{1,9},{9,1},{17,25},{25,17},{2,10},{10... | collective-permute-start | bytes 2752520 | tf_op jit(solution)/shard_map/ppermute | solution.py:17
  189.9 2.5 collective-permute-start.30
  191.9 12.8 %copy-start.2 = (bf16[128,3584]{1,0:T(8,128)(2,1)S(1)}, bf16[128,3584]{1,0:T(8,128)(2,1)}, u32[]{:S(2)}) copy-start(bf16[128,3584]{1,0:T(8,128)(2,1)} %get-tuple-element.10) | copy-start | bytes 2752516
  204.7 23.9 %collective-permute-start.32 = (bf16[128,3584]{1,0:T(8,128)(2,1)S(1)}, bf16[128,3584]{1,0:T(8,128)(2,1)}, u32[]{:S(2)}, u32[]{:S(2)}) collective-permute-start(bf16[128,3584]{1,0:T(8,128)(2,1)S(1)} %copy-done.2), channel_id=1, source_target_pairs={{0,16},{8,24},{16,0},{24,8},{1,17},{9,25},{17,1},{25,9},{2,18},{10... | collective-permute-start | bytes 2752520 | tf_op jit(solution)/shard_map/ppermute | solution.py:17
  206.5 62.0 %collective-permute-start.31 = (bf16[128,3584]{1,0:T(8,128)(2,1)S(1)}, bf16[128,3584]{1,0:T(8,128)(2,1)}, u32[]{:S(2)}, u32[]{:S(2)}) collective-permute-start(bf16[128,3584]{1,0:T(8,128)(2,1)S(1)} %copy-done.2), channel_id=1, source_target_pairs={{0,8},{8,0},{16,24},{24,16},{1,9},{9,1},{17,25},{25,17},{2,10},{10... | collective-permute-start | bytes 2752520 | tf_op jit(solution)/shard_map/ppermute | solution.py:17
  220.3 47.1 %collective-permute-start.16 = (bf16[256,2048]{1,0:T(8,128)(2,1)S(1)}, bf16[256,2048]{1,0:T(8,128)(2,1)S(1)}, u32[]{:S(2)}, u32[]{:S(2)}) collective-permute-start(bf16[256,2048]{1,0:T(8,128)(2,1)S(1)} %pad_maximum_fusion.4), channel_id=1, source_target_pairs={{0,1},{1,0},{2,3},{3,2},{4,5},{5,4},{6,7},{7,6},{8,9},{9,8},{10,11... | collective-permute-start | bytes 3145736 | tf_op jit(solution)/shard_map/ppermute | solution.py:17
  222.7 41.9 %collective-permute-start.35 = (bf16[512,896]{1,0:T(8,128)(2,1)S(1)}, bf16[512,896]{1,0:T(8,128)(2,1)S(1)}, u32[]{:S(2)}, u32[]{:S(2)}) collective-permute-start(bf16[512,896]{1,0:T(8,128)(2,1)S(1)} %constant_dynamic-slice_fusion.2), channel_id=1, source_target_pairs={{0,1},{8,9},{16,17},{24,25}} | collective-permute-start | bytes 2752520 | tf_op jit(solution)/shard_map/ppermute | solution.py:101
  225.3 62.2 %collective-permute-start.39 = (bf16[512,896]{1,0:T(8,128)(2,1)S(1)}, bf16[512,896]{1,0:T(8,128)(2,1)}, u32[]{:S(2)}, u32[]{:S(2)}) collective-permute-start(bf16[512,896]{1,0:T(8,128)(2,1)S(1)} %broadcast_select_fusion.3), channel_id=1, source_target_pairs={{0,2},{1,3},{4,6},{5,7},{8,10},{9,11},{12,14},{13,15},{16,18},{17,... | collective-permute-start | bytes 2752520 | tf_op jit(solution)/shard_map/ppermute | solution.py:101
  228.6 40.0 %collective-permute-start.33 = (bf16[128,3584]{1,0:T(8,128)(2,1)}, bf16[128,3584]{1,0:T(8,128)(2,1)S(1)}, u32[]{:S(2)}, u32[]{:S(2)}) collective-permute-start(bf16[128,3584]{1,0:T(8,128)(2,1)} %collective-permute-done.32), channel_id=1, source_target_pairs={{0,8},{8,0},{16,24},{24,16},{1,9},{9,1},{17,25},{25,17},{2,10},{10... | collective-permute-start | bytes 2752520 | tf_op jit(solution)/shard_map/ppermute | solution.py:17
  265.2 32.7 %collective-permute-start.40 = (bf16[512,896]{1,0:T(8,128)(2,1)S(1)}, bf16[512,896]{1,0:T(8,128)(2,1)}, u32[]{:S(2)}, u32[]{:S(2)}) collective-permute-start(bf16[512,896]{1,0:T(8,128)(2,1)S(1)} %broadcast_select_fusion.4), channel_id=1, source_target_pairs={{0,4},{1,5},{8,12},{9,13},{16,20},{17,21},{24,28},{25,29}} | collective-permute-start | bytes 2752520 | tf_op jit(solution)/shard_map/ppermute | solution.py:101
  267.4 1.2 copy-start.12
  268.5 29.2 %collective-permute-start.17 = (bf16[128,2048]{1,0:T(8,128)(2,1)}, bf16[128,2048]{1,0:T(8,128)(2,1)S(1)}, u32[]{:S(2)}, u32[]{:S(2)}) collective-permute-start(bf16[128,2048]{1,0:T(8,128)(2,1)} %fusion.25), channel_id=1, source_target_pairs={{0,2},{1,3},{2,0},{3,1},{4,6},{5,7},{6,4},{7,5},{8,10},{9,11},{10,... | collective-permute-start | bytes 1572872 | tf_op jit(solution)/shard_map/ppermute | solution.py:17
  284.9 12.8 %copy-start.13 = (bf16[256,2048]{1,0:T(8,128)(2,1)S(1)}, bf16[256,2048]{1,0:T(8,128)(2,1)}, u32[]{:S(2)}) copy-start(bf16[256,2048]{1,0:T(8,128)(2,1)} %copy-done.12) | copy-start | bytes 3145732
  285.0 25.6 %collective-permute-start.36 = (bf16[256,2048]{1,0:T(8,128)(2,1)S(1)}, bf16[256,2048]{1,0:T(8,128)(2,1)S(1)}, u32[]{:S(2)}, u32[]{:S(2)}) collective-permute-start(bf16[256,2048]{1,0:T(8,128)(2,1)S(1)} %pad_maximum_fusion.5), channel_id=1, source_target_pairs={{0,1},{1,0},{2,3},{3,2},{4,5},{5,4},{6,7},{7,6},{8,9},{9,8},{10,11... | collective-permute-start | bytes 3145736 | tf_op jit(solution)/shard_map/ppermute | solution.py:17
  287.6 14.8 %copy-start.8 = (f32[512,2048]{1,0:T(8,128)S(1)}, f32[512,2048]{1,0:T(8,128)}, u32[]{:S(2)}) copy-start(f32[512,2048]{1,0:T(8,128)} %convolution_add_fusion) | copy-start | bytes 12582916
  297.7 4.7 %copy-start.14 = (bf16[128,2048]{1,0:T(8,128)(2,1)}, bf16[128,2048]{1,0:T(8,128)(2,1)S(1)}, u32[]{:S(2)}) copy-start(bf16[128,2048]{1,0:T(8,128)(2,1)S(1)} %collective-permute-done.17) | copy-start | bytes 1572868
  297.8 14.7 %collective-permute-start.18 = (bf16[64,2048]{1,0:T(8,128)(2,1)S(1)}, bf16[64,2048]{1,0:T(8,128)(2,1)S(1)}, u32[]{:S(2)}, u32[]{:S(2)}) collective-permute-start(bf16[64,2048]{1,0:T(8,128)(2,1)S(1)} %add_convert_fusion.3), channel_id=1, source_target_pairs={{0,4},{1,5},{2,6},{3,7},{4,0},{5,1},{6,2},{7,3},{8,12},{9,13},{10,... | collective-permute-start | bytes 786440 | tf_op jit(solution)/shard_map/ppermute | solution.py:17
  298.0 26.3 %collective-permute-start.41 = (bf16[512,896]{1,0:T(8,128)(2,1)S(1)}, bf16[512,896]{1,0:T(8,128)(2,1)S(1)}, u32[]{:S(2)}, u32[]{:S(2)}) collective-permute-start(bf16[512,896]{1,0:T(8,128)(2,1)S(1)} %broadcast_select_fusion.2), channel_id=1, source_target_pairs={{0,2},{1,3},{4,6},{5,7},{8,10},{9,11},{12,14},{13,15},{16,18},{17,... | collective-permute-start | bytes 2752520 | tf_op jit(solution)/shard_map/ppermute | solution.py:101
  310.6 1.9 copy-start.15
  310.7 23.3 %collective-permute-start.37 = (bf16[128,2048]{1,0:T(8,128)(2,1)S(1)}, bf16[128,2048]{1,0:T(8,128)(2,1)S(1)}, u32[]{:S(2)}, u32[]{:S(2)}) collective-permute-start(bf16[128,2048]{1,0:T(8,128)(2,1)S(1)} %fusion.26), channel_id=1, source_target_pairs={{0,2},{1,3},{2,0},{3,1},{4,6},{5,7},{6,4},{7,5},{8,10},{9,11},{10,... | collective-permute-start | bytes 1572872 | tf_op jit(solution)/shard_map/ppermute | solution.py:17
  334.1 18.4 %collective-permute-start.38 = (bf16[64,2048]{1,0:T(8,128)(2,1)S(1)}, bf16[64,2048]{1,0:T(8,128)(2,1)S(1)}, u32[]{:S(2)}, u32[]{:S(2)}) collective-permute-start(bf16[64,2048]{1,0:T(8,128)(2,1)S(1)} %add_convert_fusion.1), channel_id=1, source_target_pairs={{0,4},{1,5},{2,6},{3,7},{4,0},{5,1},{6,2},{7,3},{8,12},{9,13},{10,... | collective-permute-start | bytes 786440 | tf_op jit(solution)/shard_map/ppermute | solution.py:17
